TPU v7x, 128 devices: a whole 4x4x4 slice. The times are simulated.
128 devices in a mesh: row: 4 (over z_hi, core), col: 8 (over x, z_lo), depth: 4 (over y).
Axes of the slice: x: 4, y: 4, z: 4 (z_hi: 2, z_lo: 2; z = z_hi * 2 + z_lo), core: 2. Of those that a mesh axis runs over, the one named last changes fastest.
Arguments:
- activations: bfloat16 [3072, 8192], P(('row', 'depth'), 'col'), may hold values from -6 to 6
- grad_output: bfloat16 [3072, 28672], P('col', ('row', 'depth')), may hold values from -0.75 to 0.75
- weight: bfloat16 [28672, 8192], P(('row', 'depth'), 'col'), may hold values from -0.0625 to 0.0625
Outputs:
- grad_input: bfloat16 [3072, 8192], P(('row', 'depth'), 'col')
- grad_weight: bfloat16 [28672, 8192], P(('row', 'depth'), 'col')
All inputs are finite; a program needn't handle non-finite values.
Results may differ from a plain program's by a relative error of at most 0.019.
Values may be sent and summed in bfloat16 or wider, within the bound.
No kernel may reach another device: no remote copies, remote signals or barrier semaphores. Data moves between devices by JAX's collectives and lax.ppermute only.
A program may use at most 128 MiB of HBM per device.

v0:
```python
import jax
import jax.numpy as jnp
from jax import lax
from jax.sharding import PartitionSpec as P


def reduce_rows(term, total_rows):
    return lax.psum_scatter(
        term(
            jnp.int32(0),
            lax.axis_size(("row", "depth")) * (total_rows // lax.axis_size(("row", "depth"))),
        ).astype(jnp.bfloat16),
        ("row", "depth"),
        scatter_dimension=0,
        tiled=True,
    ).astype(jnp.float32)


def shards(activations, grad_output, weight):
    total_rows = activations.shape[0] * lax.axis_size(("row", "depth"))
    contract = (((0,), (0,)), ((), ()))
    all_grads = lax.all_gather(grad_output, "col", axis=0, tiled=True)
    weight_grad = lax.dot_general(
        all_grads,
        lax.all_gather(activations, ("row", "depth"), axis=0, tiled=True),
        contract,
        preferred_element_type=jnp.float32,
    )

    def term(start, count):
        return jnp.dot(all_grads, weight, preferred_element_type=jnp.float32)

    grad_input = reduce_rows(term, total_rows)
    return (grad_input.astype(jnp.bfloat16), weight_grad.astype(jnp.bfloat16))


def solution(mesh):
    in_specs = (P(("row", "depth"), "col"), P("col", ("row", "depth")), P(("row", "depth"), "col"))
    out_specs = (P(("row", "depth"), "col"), P(("row", "depth"), "col"))
    return jax.shard_map(shards, mesh=mesh, in_specs=in_specs, out_specs=out_specs, check_vma=False)
```

profile of v0, /device:TPU:0, one launch (start us, length us, event | category | flops | bytes accessed | tf_op | source)
XLA Modules:
  0.0 397.1 jit_solution(14476592189447447861)
XLA Ops:
  7.2 0.0 all-gather.3.cloned.1.call-start
  7.2 0.7 all-gather.3.cloned.1.call-update
  7.9 0.0 all-gather.5.cloned.1.call-start
  7.9 0.7 all-gather.5.cloned.1.call-update
  8.6 0.0 reduce-scatter.2.cloned.1.call-start
  8.7 221.0 %all-gather.3.cloned.1.call-done = bf16[3072,1792]{1,0:T(8,128)(2,1)} async-done(((bf16[384,1792]{1,0:T(8,128)(2,1)}), bf16[3072,1792]{1,0:T(8,128)(2,1)}) %all-gather.3.cloned.1.call-update) | async-done | bytes 11010064 | tf_op jit(solution)/shard_map/all_gather | solution.py:22
  229.7 17.2 %convolution_convert_fusion = bf16[3072,1024]{1,0:T(8,128)(2,1)} fusion(bf16[3072,1792]{1,0:T(8,128)(2,1)} %all-gather.3.cloned.1.call-done, bf16[1792,1024]{1,0:T(8,128)(2,1)} %param.5), kind=kOutput, calls=%fused_computation | convolution fusion | flops 11277434880 | bytes 20971520 | tf_op jit(solution)/shard_map/dot_general | solution.py:31
  246.8 0.0 reduce-scatter.2.cloned.1.call-update
  246.9 51.1 %all-gather.5.cloned.1.call-done = bf16[3072,1024]{1,0:T(8,128)(2,1)} async-done(((bf16[192,1024]{1,0:T(8,128)(2,1)}), bf16[3072,1024]{1,0:T(8,128)(2,1)}) %all-gather.5.cloned.1.call-update) | async-done | bytes 6291472 | tf_op jit(solution)/shard_map/all_gather | solution.py:25
  297.9 17.5 %convolution_convert_fusion.1 = bf16[1792,1024]{1,0:T(8,128)(2,1)} fusion(bf16[3072,1792]{1,0:T(8,128)(2,1)} %all-gather.3.cloned.1.call-done, bf16[3072,1024]{1,0:T(8,128)(2,1)} %all-gather.5.cloned.1.call-done), kind=kOutput, calls=%fused_computation.1 | convolution fusion | flops 11276124160 | bytes 20971520 | tf_op jit(solution)/shard_map/dot_general | solution.py:23
  315.4 75.2 %reduce-scatter.2.cloned.1.call-done = bf16[192,1024]{1,0:T(8,128)(2,1)} async-done(((bf16[3072,1024]{1,0:T(8,128)(2,1)}), bf16[192,1024]{1,0:T(8,128)(2,1)}) %reduce-scatter.2.cloned.1.call-update) | async-done | bytes 393232 | tf_op jit(solution)/shard_map/reduce_scatter | solution.py:8
Async XLA Ops:
  7.2 222.5 %all-gather.3.cloned.1.call-start = ((), (), s32[]{:S(2)}) async-start(), calls=%async_computation.1 | async-start | bytes 12386304 | tf_op jit(solution)/shard_map/all_gather | solution.py:22
  7.9 290.1 %all-gather.5.cloned.1.call-start = ((), (), s32[]{:S(2)}) async-start(), calls=%async_computation.3 | async-start | bytes 6684672 | tf_op jit(solution)/shard_map/all_gather | solution.py:25
  8.6 382.0 %reduce-scatter.2.cloned.1.call-start = ((), (), s32[]{:S(2)}) async-start(), calls=%async_computation.2 | async-start | bytes 6684672 | tf_op jit(solution)/shard_map/reduce_scatter | solution.py:8
Sparse Core Ops, SparseCore 0:
  9.6 220.0 all-gather.2
  232.1 65.7 all-gather.4
  302.7 87.8 reduce-scatter.1
where the time goes:
time: 397 us
  waiting for transfers between devices  349 us (88%)
  matrix products  34.6 us (9%)
  between operations  13.7 us (3%)
    all_gather x1, waiting for transfers between devices, shards(): all_grads = lax.all_gather(grad_output, 'col', axis=0, tiled=True)  221 us
    reduce_scatter x1, waiting for transfers between devices, reduce_rows(): lax.psum_scatter(term(jnp.int32(0), lax.axis_size(('row', 'depth')) * (to...  75.2 us
    all_gather x1, waiting for transfers between devices, shards(): lax.all_gather(activations, ('row', 'depth'), axis=0, tiled=True)  51.1 us
    dot_general x1, matrix products, shards(): lax.dot_general(all_grads, lax.all_gather(activations, ('row', 'depth'),...  17.5 us
    dot_general x1, matrix products, term(): return jnp.dot(all_grads, weight, preferred_element_type=jnp.float32)  17.2 us
  transfers between devices with their start and end apart: 3, of which 3 were waited for; matrix products, arithmetic and copies ran while one was open for 9% of the time, Pallas kernels for 0%

commit v1 on v0

v1 whole, which is shorter than its diff:
```python
import functools

import jax
import jax.numpy as jnp
from jax import lax
from jax.experimental import pallas as pl
from jax.experimental.pallas import tpu as pltpu
from jax.sharding import PartitionSpec as P

BLOCK = 192
PARTS = ((0, 96), (96, 96))
VMEM_LIMIT = 48 * 1024 * 1024

PIECES = (
    ((0, 0, 0), (0, 0, 1)),
    ((3, 0, 0), (3, 0, 1)),
    ((1, 0, 0), (1, 0, 1)),
    ((0, 1, 0), (0, 1, 1)),
    ((2, 0, 0), (3, 1, 0)),
    ((2, 0, 1), (1, 1, 0)),
    ((1, 1, 1), (3, 1, 1)),
    ((2, 1, 0),),
    ((2, 1, 1),),
)


def source_of(shift, flip):
    col = lax.axis_index("col")
    x = lax.rem(col // 2 + shift, 4)
    z = lax.rem(col + flip, 2)
    return x, z


def grad_input_kernel(n, *refs):
    count = len(PIECES)
    chunks, w_hbm = refs[:count], refs[count]
    keep, send = refs[count + 1], refs[count + 2]
    w, g, w_sem, g_sem = refs[count + 3:]
    row, y = lax.axis_index("row"), lax.axis_index("depth")
    w_copy = pltpu.make_async_copy(w_hbm, w, w_sem)
    w_copy.start()
    copies, at, places = [], 0, []
    for ref, pieces in zip(chunks, PIECES):
        rows = n * len(pieces)
        copy = pltpu.make_async_copy(ref, g.at[pl.ds(at, rows)], g_sem.at[len(copies)])
        copy.start()
        copies.append((copy, at + rows))
        places += [(at + n * i, p) for i, p in enumerate(pieces)]
        at += rows
    w_copy.wait()
    waited = 0
    group = 4
    for first in range(0, len(places), group):
        inside = places[first:first + group]
        low, high = inside[0][0], inside[-1][0] + n
        while waited < len(copies) and (waited == 0 or copies[waited - 1][1] < high):
            copies[waited][0].wait()
            waited += 1
        product = jnp.dot(g[low:high, :], w[...], preferred_element_type=jnp.float32).astype(jnp.bfloat16)
        for start, (shift, flip, q) in inside:
            x, z = source_of(shift, flip)
            apart = lax.rem(x + row, 2)
            far = lax.rem(x // 2 + row // 2, 2)
            ahead = lax.rem(2 * z + q + 4 - y, 4)
            value = product[start - low:start - low + n]

            @pl.when(apart == 0)
            def _():
                keep[ahead, far] = value

            @pl.when(apart == 1)
            def _():
                send[ahead, far] = value


def grad_input_part(n, chunks, weight):
    ff, d = weight.shape
    rows = 16 * n
    out = jax.ShapeDtypeStruct((4, 2, n, d), jnp.bfloat16)
    return pl.pallas_call(
        functools.partial(grad_input_kernel, n),
        out_shape=(out, out),
        in_specs=[pl.BlockSpec(memory_space=pl.ANY)] * (len(PIECES) + 1),
        out_specs=(pl.BlockSpec(memory_space=pltpu.VMEM),) * 2,
        scratch_shapes=[
            pltpu.VMEM((ff, d), jnp.bfloat16),
            pltpu.VMEM((rows, ff), jnp.bfloat16),
            pltpu.SemaphoreType.DMA,
            pltpu.SemaphoreType.DMA((len(PIECES),)),
        ],
        compiler_params=pltpu.CompilerParams(vmem_limit_bytes=VMEM_LIMIT),
        cost_estimate=pl.CostEstimate(
            flops=2 * rows * ff * d, bytes_accessed=2 * (rows * ff + ff * d + rows * d), transcendentals=0
        ),
    )(*[c.reshape(-1, ff) for c in chunks], weight)


TILE = 256


def grad_weight_kernel(first, last, *refs):
    count = len(PIECES) * len(PARTS)
    chunks, acts_hbm, out = refs[:count], refs[count], refs[-6]
    acts, g, o, in_sem, out_sem = refs[-5:]
    acts_copy = pltpu.make_async_copy(acts_hbm, acts, in_sem.at[0])
    acts_copy.start()
    copies = []
    for tile in range(first, last):
        of_tile, index = [], 0
        for part, (low, n) in enumerate(PARTS):
            for ref, pieces in zip(chunks[part * len(PIECES):], PIECES):
                for i, (shift, flip, q) in enumerate(pieces):
                    x, z = source_of(shift, flip)
                    token = pl.multiple_of((4 * x + 2 * z + q) * BLOCK + low, 32)
                    of_tile.append(
                        pltpu.make_async_copy(
                            ref.at[pl.ds(n * i, n), pl.ds(TILE * tile, TILE)],
                            g.at[tile - first, pl.ds(token, n), :],
                            in_sem.at[1 + index + (tile - first) * 16 * len(PARTS)],
                        )
                    )
                    of_tile[-1].start()
                    index += 1
        copies.append(of_tile)
    acts_copy.wait()
    outs = []
    for tile in range(first, last):
        at = tile - first
        for copy in copies[at]:
            copy.wait()
        o[at] = lax.dot_general(
            g[at], acts[...], (((0,), (0,)), ((), ())), preferred_element_type=jnp.float32
        ).astype(jnp.bfloat16)
        outs.append(pltpu.make_async_copy(o.at[at], out.at[pl.ds(TILE * tile, TILE), :], out_sem.at[at]))
        outs[-1].start()
    for copy in outs:
        copy.wait()


def grad_weight_tiles(first, last, chunks, acts, into):
    ff, d, tokens = chunks[0].shape[-1], acts.shape[1], acts.shape[0]
    tiles = last - first
    args = [c.reshape(-1, ff) for c in chunks] + [acts] + ([] if into is None else [into])
    return pl.pallas_call(
        functools.partial(grad_weight_kernel, first, last),
        out_shape=jax.ShapeDtypeStruct((ff, d), jnp.bfloat16),
        in_specs=[pl.BlockSpec(memory_space=pl.ANY)] * len(args),
        out_specs=pl.BlockSpec(memory_space=pl.ANY),
        scratch_shapes=[
            pltpu.VMEM((tokens, d), jnp.bfloat16),
            pltpu.VMEM((tiles, tokens, TILE), jnp.bfloat16),
            pltpu.VMEM((tiles, TILE, d), jnp.bfloat16),
            pltpu.SemaphoreType.DMA((1 + tiles * 16 * len(PARTS),)),
            pltpu.SemaphoreType.DMA((tiles,)),
        ],
        input_output_aliases={} if into is None else {len(args) - 1: 0},
        compiler_params=pltpu.CompilerParams(vmem_limit_bytes=VMEM_LIMIT),
        cost_estimate=pl.CostEstimate(
            flops=2 * tokens * TILE * tiles * d,
            bytes_accessed=2 * (tokens * TILE * tiles + tokens * d + TILE * tiles * d),
            transcendentals=0,
        ),
    )(*args)


def along_x(value, shift):
    return lax.ppermute(value, "col", [(i, (i + 2 * shift) % 8) for i in range(8)])


def along_z(value):
    return lax.ppermute(value, "col", [(i, i ^ 1) for i in range(8)])


def along_y(value, shift):
    return lax.ppermute(value, "depth", [(i, (i + shift) % 4) for i in range(4)])


def other_core(value):
    return lax.ppermute(value, "row", [(i, i ^ 1) for i in range(4)])


def other_z_hi(value):
    return lax.ppermute(value, "row", [(i, i ^ 2) for i in range(4)])


def gather_part(own):
    left, right, z = along_x(own, 1), along_x(own, -1), along_z(own)
    left2 = along_x(jnp.stack([left[0], z[0]]), 1)
    right2 = along_x(jnp.stack([right[1], z[0]]), -1)
    z2 = along_z(jnp.stack([right[1], left[1]]))
    left3 = along_x(left2[1], 1)
    right3 = along_x(z2[0], -1)
    return [own, left, right, z, left2, right2, z2, left3, right3]


def add(*terms):
    return sum(t.astype(jnp.float32) for t in terms).astype(jnp.bfloat16)


def reduce_part(keep, send):
    got = other_core(send)
    q = [add(keep[i], got[i]) for i in range(4)]
    near = add(q[0], along_y(q[1], 1), along_y(q[2], 2), along_y(q[3], 3))
    return add(near[0], other_z_hi(near[1]))


def shards(activations, grad_output, weight):
    ff = grad_output.shape[1]
    blocks = grad_output.reshape(2, BLOCK, ff)
    acts = lax.all_gather(activations, ("row", "depth"), axis=0, tiled=True)
    gathered, results = [], []
    for low, n in PARTS:
        gathered.append(gather_part(blocks[:, low:low + n]))
    for (low, n), chunks in zip(PARTS, gathered):
        results.append(reduce_part(*grad_input_part(n, chunks, weight)))
    every = gathered[0] + gathered[1]
    tiles = ff // TILE
    weight_grad = grad_weight_tiles(0, 2, every, acts, None)
    weight_grad = grad_weight_tiles(2, tiles, every, acts, weight_grad)
    return jnp.concatenate(results, axis=0), weight_grad


def solution(mesh):
    in_specs = (P(("row", "depth"), "col"), P("col", ("row", "depth")), P(("row", "depth"), "col"))
    out_specs = (P(("row", "depth"), "col"), P(("row", "depth"), "col"))
    return jax.shard_map(shards, mesh=mesh, in_specs=in_specs, out_specs=out_specs, check_vma=False)
```

time: 397 us -> 203 us (0.51)
  waiting for transfers between devices: 349 us -> 93.3 us
  Pallas kernels: 0 us -> 44.1 us
  starting transfers between devices: 0.11 us -> 39.4 us
  matrix products: 34.6 us -> 0 us
  local copies, waits for them, and re-layouts: 0 us -> 7.89 us
    all_gather x2 -> x1, waiting for transfers between devices: 272 us -> 0.01 us  [shards(): acts = lax.all_gather(activations, ('row', 'depth'), axis=0, tiled=True)]
    ppermute x0 -> x26, waiting for transfers between devices: none -> 92.6 us  [the longest x4 50.1 us: along_z(): return lax.ppermute(value, 'col', [(i, i ^ 1) for i in range(8)])]
    reduce_scatter x1 -> x0, waiting for transfers between devices: 75.2 us -> none  [reduce_rows(): lax.psum_scatter(term(jnp.int32(0), lax.axis_size(('row', 'depth')) * (to...]
    pallas_call x0 -> x4, Pallas kernels: none -> 44.1 us  [the longest x2 22.3 us: grad_weight_tiles(): pl.pallas_call(functools.partial(grad_weight_kernel, first, last), out_sh...]
    ppermute x0 -> x26, starting transfers between devices: none -> 39.4 us  [the longest x12 12.6 us: along_x(): lax.ppermute(value, 'col', [(i, (i + 2 * shift) % 8) for i in range(8)])]
    dot_general x2 -> x0, matrix products: 34.6 us -> none  [the longest x1 17.5 us: shards(): lax.dot_general(all_grads, lax.all_gather(activations, ('row', 'depth'),...]
    unnamed x0 -> x50, local copies, waits for them, and re-layouts: none -> 6.18 us
  transfers between devices with their start and end apart: 3 -> 27, of which waited for: 3 -> 14; matrix products, arithmetic and copies ran while one was open for 9% -> 2% of each run, Pallas kernels for 0% -> 11%
where the time goes in v1:
time: 203 us; the launch traced here: 202 us
  waiting for transfers between devices  93.3 us (46%)
  Pallas kernels  44.1 us (22%)
  starting transfers between devices  39.4 us (19%)
  between operations  14.5 us (7%)
  local copies, waits for them, and re-layouts  7.89 us (4%)
  other arithmetic  2.8 us (1%)
    ppermute x4, waiting for transfers between devices, along_z(): return lax.ppermute(value, 'col', [(i, i ^ 1) for i in range(8)])  50.1 us
    pallas_call x2, Pallas kernels, grad_weight_tiles(): pl.pallas_call(functools.partial(grad_weight_kernel, first, last), out_sh...  22.3 us
    pallas_call x2, Pallas kernels, grad_input_part(): pl.pallas_call(functools.partial(grad_input_kernel, n), out_shape=(out, o...  21.8 us
    ppermute x6, waiting for transfers between devices, along_y(): lax.ppermute(value, 'depth', [(i, (i + shift) % 4) for i in range(4)])  21.6 us
    ppermute x12, waiting for transfers between devices, along_x(): lax.ppermute(value, 'col', [(i, (i + 2 * shift) % 8) for i in range(8)])  16.6 us
    ppermute x12, starting transfers between devices, along_x(): lax.ppermute(value, 'col', [(i, (i + 2 * shift) % 8) for i in range(8)])  12.6 us
    ppermute x6, starting transfers between devices, along_y(): lax.ppermute(value, 'depth', [(i, (i + shift) % 4) for i in range(4)])  12 us
    ppermute x2, starting transfers between devices, other_z_hi(): return lax.ppermute(value, 'row', [(i, i ^ 2) for i in range(4)])  7.78 us
  transfers between devices with their start and end apart: 27, of which 14 were waited for; matrix products, arithmetic and copies ran while one was open for 2% of the time, Pallas kernels for 11%

profile of v1, /device:TPU:0, one launch (start us, length us, event | category | flops | bytes accessed | tf_op | source)
XLA Modules:
  0.0 202.0 jit_solution(2922724825470836688)
XLA Ops:
  7.2 0.7 all-gather.2.cloned.1.call-update
  7.9 1.4 fusion.16
  9.3 2.1 %collective-permute-start.2 = (bf16[2,96,1792]{2,1,0:T(8,128)(2,1)S(1)}, bf16[2,96,1792]{2,1,0:T(8,128)(2,1)S(1)}, u32[]{:S(2)}, u32[]{:S(2)}) collective-permute-start(bf16[2,96,1792]{2,1,0:T(8,128)(2,1)S(1)} %get-tuple-element.16), channel_id=1, source_target_pairs={{0,4},{4,0},{8,12},{12,8},{16,20},{20,16},{24,28},{28,24},{1,5},{5... | collective-permute-start | bytes 2064392 | tf_op jit(solution)/shard_map/ppermute | solution.py:171
  11.4 2.8 %collective-permute-start.1 = (bf16[2,96,1792]{2,1,0:T(8,128)(2,1)S(1)}, bf16[2,96,1792]{2,1,0:T(8,128)(2,1)S(1)}, u32[]{:S(2)}, u32[]{:S(2)}) collective-permute-start(bf16[2,96,1792]{2,1,0:T(8,128)(2,1)S(1)} %get-tuple-element.16), channel_id=1, source_target_pairs={{0,24},{4,28},{8,0},{12,4},{16,8},{20,12},{24,16},{28,20},{1,25},{... | collective-permute-start | bytes 2064392 | tf_op jit(solution)/shard_map/ppermute | solution.py:167
  14.2 0.8 collective-permute-start.13
  15.0 15.7 %collective-permute-done.2 = bf16[2,96,1792]{2,1,0:T(8,128)(2,1)S(1)} collective-permute-done((bf16[2,96,1792]{2,1,0:T(8,128)(2,1)S(1)}, bf16[2,96,1792]{2,1,0:T(8,128)(2,1)S(1)}, u32[]{:S(2)}, u32[]{:S(2)}) %collective-permute-start.2) | collective-permute-done | bytes 688160 | tf_op jit(solution)/shard_map/ppermute | solution.py:171
  30.7 2.6 %collective-permute-start.14 = (bf16[2,96,1792]{2,1,0:T(8,128)(2,1)S(1)}, bf16[2,96,1792]{2,1,0:T(8,128)(2,1)S(1)}, u32[]{:S(2)}, u32[]{:S(2)}) collective-permute-start(bf16[2,96,1792]{2,1,0:T(8,128)(2,1)S(1)} %get-tuple-element.17), channel_id=1, source_target_pairs={{0,24},{4,28},{8,0},{12,4},{16,8},{20,12},{24,16},{28,20},{1,25},{... | collective-permute-start | bytes 2064392 | tf_op jit(solution)/shard_map/ppermute | solution.py:167
  33.4 0.4 collective-permute-done
  34.0 2.2 %collective-permute-start.5 = (bf16[2,96,1792]{2,1,0:T(8,128)(2,1)S(1)}, bf16[2,96,1792]{2,1,0:T(8,128)(2,1)S(1)}, u32[]{:S(2)}, u32[]{:S(2)}) collective-permute-start(bf16[2,96,1792]{2,1,0:T(8,128)(2,1)S(1)} %get-tuple-element.22), channel_id=1, source_target_pairs={{0,4},{4,0},{8,12},{12,8},{16,20},{20,16},{24,28},{28,24},{1,5},{5... | collective-permute-start | bytes 2064392 | tf_op jit(solution)/shard_map/ppermute | solution.py:171
  36.2 10.4 %collective-permute-done.15 = bf16[2,96,1792]{2,1,0:T(8,128)(2,1)S(1)} collective-permute-done((bf16[2,96,1792]{2,1,0:T(8,128)(2,1)S(1)}, bf16[2,96,1792]{2,1,0:T(8,128)(2,1)S(1)}, u32[]{:S(2)}, u32[]{:S(2)}) %collective-permute-start.15) | collective-permute-done | bytes 688160 | tf_op jit(solution)/shard_map/ppermute | solution.py:171
  46.7 1.8 collective-permute-done.13
  48.8 1.8 collective-permute-start.18
  50.5 1.7 collective-permute-start.4
  52.3 10.9 %collective-permute-done.3 = bf16[2,96,1792]{2,1,0:T(8,128)(2,1)S(1)} collective-permute-done((bf16[2,96,1792]{2,1,0:T(8,128)(2,1)S(1)}, bf16[2,96,1792]{2,1,0:T(8,128)(2,1)S(1)}, u32[]{:S(2)}, u32[]{:S(2)}) %collective-permute-start.3) | collective-permute-done | bytes 688160 | tf_op jit(solution)/shard_map/ppermute | solution.py:167
  63.3 9.9 %collective-permute-done.5 = bf16[2,96,1792]{2,1,0:T(8,128)(2,1)S(1)} collective-permute-done((bf16[2,96,1792]{2,1,0:T(8,128)(2,1)S(1)}, bf16[2,96,1792]{2,1,0:T(8,128)(2,1)S(1)}, u32[]{:S(2)}, u32[]{:S(2)}) %collective-permute-start.5) | collective-permute-done | bytes 688160 | tf_op jit(solution)/shard_map/ppermute | solution.py:171
  73.1 1.3 collective-permute-start.6
  74.5 3.5 %collective-permute-done.16 = bf16[2,96,1792]{2,1,0:T(8,128)(2,1)S(1)} collective-permute-done((bf16[2,96,1792]{2,1,0:T(8,128)(2,1)S(1)}, bf16[2,96,1792]{2,1,0:T(8,128)(2,1)S(1)}, u32[]{:S(2)}, u32[]{:S(2)}) %collective-permute-start.16) | collective-permute-done | bytes 688160 | tf_op jit(solution)/shard_map/ppermute | solution.py:167
  78.0 14.1 %collective-permute-done.18 = bf16[2,96,1792]{2,1,0:T(8,128)(2,1)S(1)} collective-permute-done((bf16[2,96,1792]{2,1,0:T(8,128)(2,1)S(1)}, bf16[2,96,1792]{2,1,0:T(8,128)(2,1)S(1)}, u32[]{:S(2)}, u32[]{:S(2)}) %collective-permute-start.18) | collective-permute-done | bytes 688160 | tf_op jit(solution)/shard_map/ppermute | solution.py:171
  92.1 1.5 collective-permute-start.19
  93.7 1.8 collective-permute-start.20
  95.5 10.8 %shard_map.50 = (bf16[4,2,96,1024]{3,2,1,0:T(8,128)(2,1)}, bf16[4,2,96,1024]{3,2,1,0:T(8,128)(2,1)}) custom-call(bf16[192,1792]{1,0:T(8,128)(2,1)S(1)} %bitcast.59, bf16[192,1792]{1,0:T(8,128)(2,1)S(1)} %bitcast.65, bf16[192,1792]{1,0:T(8,128)(2,1)S(1)} %bitcast.74, bf16[192,1792]{1,0:T(8,128)(2,1)S(1)} %bitcast.71, bf16[192,1792]{1,0:T(8,128)(2,1)S(1)} %bitcast.83, ...), custom_call_target="tpu_custom_call" | custom-call | flops 5637144576 | bytes 12320768 | tf_op jit(solution)/shard_map/pallas_call | solution.py:80
  106.8 10.9 %shard_map.51 = (bf16[4,2,96,1024]{3,2,1,0:T(8,128)(2,1)}, bf16[4,2,96,1024]{3,2,1,0:T(8,128)(2,1)}) custom-call(bf16[192,1792]{1,0:T(8,128)(2,1)S(1)} %bitcast.62, bf16[192,1792]{1,0:T(8,128)(2,1)S(1)} %bitcast.68, bf16[192,1792]{1,0:T(8,128)(2,1)S(1)} %bitcast.80, bf16[192,1792]{1,0:T(8,128)(2,1)S(1)} %bitcast.77, bf16[192,1792]{1,0:T(8,128)(2,1)S(1)} %bitcast.89, ...), custom_call_target="tpu_custom_call" | custom-call | flops 5637144576 | bytes 12320768 | tf_op jit(solution)/shard_map/pallas_call | solution.py:80
  117.8 0.6 collective-permute-start.21
  118.4 0.5 fusion.7
  118.9 3.2 %collective-permute-start.10 = (bf16[2,96,1024]{2,1,0:T(8,128)(2,1)S(1)}, bf16[2,96,1024]{2,1,0:T(8,128)(2,1)S(1)}, u32[]{:S(2)}, u32[]{:S(2)}) collective-permute-start(bf16[2,96,1024]{2,1,0:T(8,128)(2,1)S(1)} %get-tuple-element.12), channel_id=1, source_target_pairs={{0,2},{1,3},{2,0},{3,1},{4,6},{5,7},{6,4},{7,5},{8,10},{9,11},{10,... | collective-permute-start | bytes 1179656 | tf_op jit(solution)/shard_map/ppermute | solution.py:175
  122.1 1.1 collective-permute-start.11
  123.2 1.0 collective-permute-start.9
  124.2 0.5 fusion.11
  124.7 0.7 collective-permute-start.22
  125.4 3.0 %collective-permute-start.23 = (bf16[2,96,1024]{2,1,0:T(8,128)(2,1)S(1)}, bf16[2,96,1024]{2,1,0:T(8,128)(2,1)S(1)}, u32[]{:S(2)}, u32[]{:S(2)}) collective-permute-start(bf16[2,96,1024]{2,1,0:T(8,128)(2,1)S(1)} %get-tuple-element.15), channel_id=1, source_target_pairs={{0,2},{1,3},{2,0},{3,1},{4,6},{5,7},{6,4},{7,5},{8,10},{9,11},{10,... | collective-permute-start | bytes 1179656 | tf_op jit(solution)/shard_map/ppermute | solution.py:175
  128.5 4.0 %collective-permute-done.10 = bf16[2,96,1024]{2,1,0:T(8,128)(2,1)S(1)} collective-permute-done((bf16[2,96,1024]{2,1,0:T(8,128)(2,1)S(1)}, bf16[2,96,1024]{2,1,0:T(8,128)(2,1)S(1)}, u32[]{:S(2)}, u32[]{:S(2)}) %collective-permute-start.10) | collective-permute-done | bytes 393248 | tf_op jit(solution)/shard_map/ppermute | solution.py:175
  132.5 3.0 %collective-permute-start.24 = (bf16[2,96,1024]{2,1,0:T(8,128)(2,1)S(1)}, bf16[2,96,1024]{2,1,0:T(8,128)(2,1)S(1)}, u32[]{:S(2)}, u32[]{:S(2)}) collective-permute-start(bf16[2,96,1024]{2,1,0:T(8,128)(2,1)S(1)} %get-tuple-element.14), channel_id=1, source_target_pairs={{0,3},{1,0},{2,1},{3,2},{4,7},{5,4},{6,5},{7,6},{8,11},{9,8},{10,9... | collective-permute-start | bytes 1179656 | tf_op jit(solution)/shard_map/ppermute | solution.py:175
  135.5 5.8 %collective-permute-done.11 = bf16[2,96,1024]{2,1,0:T(8,128)(2,1)S(1)} collective-permute-done((bf16[2,96,1024]{2,1,0:T(8,128)(2,1)S(1)}, bf16[2,96,1024]{2,1,0:T(8,128)(2,1)S(1)}, u32[]{:S(2)}, u32[]{:S(2)}) %collective-permute-start.11) | collective-permute-done | bytes 393248 | tf_op jit(solution)/shard_map/ppermute | solution.py:175
  141.6 3.8 %collective-permute-start.12 = (bf16[96,1024]{1,0:T(8,128)(2,1)S(1)}, bf16[96,1024]{1,0:T(8,128)(2,1)S(1)}, u32[]{:S(2)}, u32[]{:S(2)}) collective-permute-start(bf16[96,1024]{1,0:T(8,128)(2,1)S(1)} %slice_bitcast_fusion.6), channel_id=1, source_target_pairs={{0,64},{32,96},{64,0},{96,32},{1,65},{33,97},{65,1},{97,33},{2,66}... | collective-permute-start | bytes 589832 | tf_op jit(solution)/shard_map/ppermute | solution.py:183
  145.4 3.9 %collective-permute-done.22 = bf16[2,96,1024]{2,1,0:T(8,128)(2,1)S(1)} collective-permute-done((bf16[2,96,1024]{2,1,0:T(8,128)(2,1)S(1)}, bf16[2,96,1024]{2,1,0:T(8,128)(2,1)S(1)}, u32[]{:S(2)}, u32[]{:S(2)}) %collective-permute-start.22) | collective-permute-done | bytes 393248 | tf_op jit(solution)/shard_map/ppermute | solution.py:175
  149.3 7.6 %collective-permute-done.23 = bf16[2,96,1024]{2,1,0:T(8,128)(2,1)S(1)} collective-permute-done((bf16[2,96,1024]{2,1,0:T(8,128)(2,1)S(1)}, bf16[2,96,1024]{2,1,0:T(8,128)(2,1)S(1)}, u32[]{:S(2)}, u32[]{:S(2)}) %collective-permute-start.23) | collective-permute-done | bytes 393248 | tf_op jit(solution)/shard_map/ppermute | solution.py:175
  156.9 0.3 collective-permute-done.24
  157.6 4.0 %collective-permute-start.25 = (bf16[96,1024]{1,0:T(8,128)(2,1)S(1)}, bf16[96,1024]{1,0:T(8,128)(2,1)S(1)}, u32[]{:S(2)}, u32[]{:S(2)}) collective-permute-start(bf16[96,1024]{1,0:T(8,128)(2,1)S(1)} %slice_bitcast_fusion.4), channel_id=1, source_target_pairs={{0,64},{32,96},{64,0},{96,32},{1,65},{33,97},{65,1},{97,33},{2,66}... | collective-permute-start | bytes 589832 | tf_op jit(solution)/shard_map/ppermute | solution.py:183
  161.6 4.2 %collective-permute-done.25 = bf16[96,1024]{1,0:T(8,128)(2,1)S(1)} collective-permute-done((bf16[96,1024]{1,0:T(8,128)(2,1)S(1)}, bf16[96,1024]{1,0:T(8,128)(2,1)S(1)}, u32[]{:S(2)}, u32[]{:S(2)}) %collective-permute-start.25) | collective-permute-done | bytes 196640 | tf_op jit(solution)/shard_map/ppermute | solution.py:183
  165.9 0.8 pad_maximum_fusion.6
  166.7 1.1 copy-done.9
  167.8 1.1 copy-done.13
  168.9 1.0 copy-done.16
  169.9 1.0 copy-done.18
  170.8 1.0 copy-done.20
  171.8 1.0 copy-done.22
  172.8 7.9 %shard_map.52.refs_19_ = bf16[1792,1024]{1,0:T(8,128)(2,1)} custom-call(bf16[192,1792]{1,0:T(8,128)(2,1)S(1)} %bitcast.60, bf16[192,1792]{1,0:T(8,128)(2,1)S(1)} %bitcast.66, bf16[192,1792]{1,0:T(8,128)(2,1)S(1)} %bitcast.75, bf16[192,1792]{1,0:T(8,128)(2,1)S(1)} %bitcast.72, bf16[192,1792]{1,0:T(8,128)(2,1)S(1)} %bitcast.84, ...), custom_call_target="tpu_custom_call" | custom-call | flops 3221225472 | bytes 10485760 | tf_op jit(solution)/shard_map/pallas_call | solution.py:144
  180.7 14.4 %shard_map.53 = bf16[1792,1024]{1,0:T(8,128)(2,1)} custom-call(bf16[192,1792]{1,0:T(8,128)(2,1)S(1)} %bitcast.61, bf16[192,1792]{1,0:T(8,128)(2,1)S(1)} %bitcast.67, bf16[192,1792]{1,0:T(8,128)(2,1)S(1)} %bitcast.76, bf16[192,1792]{1,0:T(8,128)(2,1)S(1)} %bitcast.73, bf16[192,1792]{1,0:T(8,128)(2,1)S(1)} %bitcast.85, ...), custom_call_target="tpu_custom_call", output_to_operand_aliasing={{}: (19, {})} | custom-call | flops 8053063680 | bytes 16777216 | tf_op jit(solution)/shard_map/pallas_call | solution.py:144
  (83 shorter events, 2.0 us)
Async XLA Ops:
  7.2 159.5 %all-gather.2.cloned.1.call-start = ((), (), s32[]{:S(2)}) async-start(), calls=%async_computation | async-start | bytes 6684672 | tf_op jit(solution)/shard_map/all_gather | solution.py:210
  9.3 97.5 %copy-start = (bf16[2,96,1792]{2,1,0:T(8,128)(2,1)}, bf16[2,96,1792]{2,1,0:T(8,128)(2,1)S(1)}, u32[]{:S(2)}) copy-start(bf16[2,96,1792]{2,1,0:T(8,128)(2,1)S(1)} %get-tuple-element.17) | copy-start | bytes 2064388
  9.3 21.4 %collective-permute-start.2 = (bf16[2,96,1792]{2,1,0:T(8,128)(2,1)S(1)}, bf16[2,96,1792]{2,1,0:T(8,128)(2,1)S(1)}, u32[]{:S(2)}, u32[]{:S(2)}) collective-permute-start(bf16[2,96,1792]{2,1,0:T(8,128)(2,1)S(1)} %get-tuple-element.16), channel_id=1, source_target_pairs={{0,4},{4,0},{8,12},{12,8},{16,20},{20,16},{24,28},{28,24},{1,5},{5... | collective-permute-start | bytes 2064392 | tf_op jit(solution)/shard_map/ppermute | solution.py:171
  11.4 21.9 %collective-permute-start.1 = (bf16[2,96,1792]{2,1,0:T(8,128)(2,1)S(1)}, bf16[2,96,1792]{2,1,0:T(8,128)(2,1)S(1)}, u32[]{:S(2)}, u32[]{:S(2)}) collective-permute-start(bf16[2,96,1792]{2,1,0:T(8,128)(2,1)S(1)} %get-tuple-element.16), channel_id=1, source_target_pairs={{0,24},{4,28},{8,0},{12,4},{16,8},{20,12},{24,16},{28,20},{1,25},{... | collective-permute-start | bytes 2064392 | tf_op jit(solution)/shard_map/ppermute | solution.py:167
  14.2 19.6 %collective-permute-start = (bf16[2,96,1792]{2,1,0:T(8,128)(2,1)S(1)}, bf16[2,96,1792]{2,1,0:T(8,128)(2,1)S(1)}, u32[]{:S(2)}, u32[]{:S(2)}) collective-permute-start(bf16[2,96,1792]{2,1,0:T(8,128)(2,1)S(1)} %get-tuple-element.16), channel_id=1, source_target_pairs={{0,8},{4,12},{8,16},{12,20},{16,24},{20,28},{24,0},{28,4},{1,9},{5... | collective-permute-start | bytes 2064392 | tf_op jit(solution)/shard_map/ppermute | solution.py:167
  14.2 34.3 %collective-permute-start.13 = (bf16[2,96,1792]{2,1,0:T(8,128)(2,1)S(1)}, bf16[2,96,1792]{2,1,0:T(8,128)(2,1)S(1)}, u32[]{:S(2)}, u32[]{:S(2)}) collective-permute-start(bf16[2,96,1792]{2,1,0:T(8,128)(2,1)S(1)} %get-tuple-element.17), channel_id=1, source_target_pairs={{0,8},{4,12},{8,16},{12,20},{16,24},{20,28},{24,0},{28,4},{1,9},{5... | collective-permute-start | bytes 2064392 | tf_op jit(solution)/shard_map/ppermute | solution.py:167
  14.9 31.7 %collective-permute-start.15 = (bf16[2,96,1792]{2,1,0:T(8,128)(2,1)S(1)}, bf16[2,96,1792]{2,1,0:T(8,128)(2,1)S(1)}, u32[]{:S(2)}, u32[]{:S(2)}) collective-permute-start(bf16[2,96,1792]{2,1,0:T(8,128)(2,1)S(1)} %get-tuple-element.17), channel_id=1, source_target_pairs={{0,4},{4,0},{8,12},{12,8},{16,20},{20,16},{24,28},{28,24},{1,5},{5... | collective-permute-start | bytes 2064392 | tf_op jit(solution)/shard_map/ppermute | solution.py:171
  30.7 16.0 %collective-permute-start.14 = (bf16[2,96,1792]{2,1,0:T(8,128)(2,1)S(1)}, bf16[2,96,1792]{2,1,0:T(8,128)(2,1)S(1)}, u32[]{:S(2)}, u32[]{:S(2)}) collective-permute-start(bf16[2,96,1792]{2,1,0:T(8,128)(2,1)S(1)} %get-tuple-element.17), channel_id=1, source_target_pairs={{0,24},{4,28},{8,0},{12,4},{16,8},{20,12},{24,16},{28,20},{1,25},{... | collective-permute-start | bytes 2064392 | tf_op jit(solution)/shard_map/ppermute | solution.py:167
  33.3 62.2 %copy-start.2 = (bf16[2,96,1792]{2,1,0:T(8,128)(2,1)}, bf16[2,96,1792]{2,1,0:T(8,128)(2,1)S(1)}, u32[]{:S(2)}) copy-start(bf16[2,96,1792]{2,1,0:T(8,128)(2,1)S(1)} %collective-permute-done.1) | copy-start | bytes 2064388
  33.9 29.3 %collective-permute-start.3 = (bf16[2,96,1792]{2,1,0:T(8,128)(2,1)S(1)}, bf16[2,96,1792]{2,1,0:T(8,128)(2,1)S(1)}, u32[]{:S(2)}, u32[]{:S(2)}) collective-permute-start(bf16[2,96,1792]{2,1,0:T(8,128)(2,1)S(1)} %get-tuple-element.24), channel_id=1, source_target_pairs={{0,8},{4,12},{8,16},{12,20},{16,24},{20,28},{24,0},{28,4},{1,9},{5... | collective-permute-start | bytes 2064392 | tf_op jit(solution)/shard_map/ppermute | solution.py:167
  34.0 39.1 %collective-permute-start.5 = (bf16[2,96,1792]{2,1,0:T(8,128)(2,1)S(1)}, bf16[2,96,1792]{2,1,0:T(8,128)(2,1)S(1)}, u32[]{:S(2)}, u32[]{:S(2)}) collective-permute-start(bf16[2,96,1792]{2,1,0:T(8,128)(2,1)S(1)} %get-tuple-element.22), channel_id=1, source_target_pairs={{0,4},{4,0},{8,12},{12,8},{16,20},{20,16},{24,28},{28,24},{1,5},{5... | collective-permute-start | bytes 2064392 | tf_op jit(solution)/shard_map/ppermute | solution.py:171
  46.6 60.1 %copy-start.4 = (bf16[2,96,1792]{2,1,0:T(8,128)(2,1)}, bf16[2,96,1792]{2,1,0:T(8,128)(2,1)S(1)}, u32[]{:S(2)}) copy-start(bf16[2,96,1792]{2,1,0:T(8,128)(2,1)S(1)} %collective-permute-done.15) | copy-start | bytes 2064388
  46.7 60.1 %copy-start.5 = (bf16[2,96,1792]{2,1,0:T(8,128)(2,1)}, bf16[2,96,1792]{2,1,0:T(8,128)(2,1)S(1)}, u32[]{:S(2)}) copy-start(bf16[2,96,1792]{2,1,0:T(8,128)(2,1)S(1)} %collective-permute-done.14) | copy-start | bytes 2064388
  48.5 58.3 %copy-start.1 = (bf16[2,96,1792]{2,1,0:T(8,128)(2,1)}, bf16[2,96,1792]{2,1,0:T(8,128)(2,1)S(1)}, u32[]{:S(2)}) copy-start(bf16[2,96,1792]{2,1,0:T(8,128)(2,1)S(1)} %collective-permute-done.13) | copy-start | bytes 2064388
  48.7 29.3 %collective-permute-start.16 = (bf16[2,96,1792]{2,1,0:T(8,128)(2,1)S(1)}, bf16[2,96,1792]{2,1,0:T(8,128)(2,1)S(1)}, u32[]{:S(2)}, u32[]{:S(2)}) collective-permute-start(bf16[2,96,1792]{2,1,0:T(8,128)(2,1)S(1)} %get-tuple-element.27), channel_id=1, source_target_pairs={{0,8},{4,12},{8,16},{12,20},{16,24},{20,28},{24,0},{28,4},{1,9},{5... | collective-permute-start | bytes 2064392 | tf_op jit(solution)/shard_map/ppermute | solution.py:167
  48.8 43.4 %collective-permute-start.18 = (bf16[2,96,1792]{2,1,0:T(8,128)(2,1)S(1)}, bf16[2,96,1792]{2,1,0:T(8,128)(2,1)S(1)}, u32[]{:S(2)}, u32[]{:S(2)}) collective-permute-start(bf16[2,96,1792]{2,1,0:T(8,128)(2,1)S(1)} %get-tuple-element.25), channel_id=1, source_target_pairs={{0,4},{4,0},{8,12},{12,8},{16,20},{20,16},{24,28},{28,24},{1,5},{5... | collective-permute-start | bytes 2064392 | tf_op jit(solution)/shard_map/ppermute | solution.py:171
  50.5 43.1 %collective-permute-start.4 = (bf16[2,96,1792]{2,1,0:T(8,128)(2,1)S(1)}, bf16[2,96,1792]{2,1,0:T(8,128)(2,1)S(1)}, u32[]{:S(2)}, u32[]{:S(2)}) collective-permute-start(bf16[2,96,1792]{2,1,0:T(8,128)(2,1)S(1)} %get-tuple-element.23), channel_id=1, source_target_pairs={{0,24},{4,28},{8,0},{12,4},{16,8},{20,12},{24,16},{28,20},{1,25},{... | collective-permute-start | bytes 2064392 | tf_op jit(solution)/shard_map/ppermute | solution.py:167
  63.2 43.1 %copy-start.6 = (bf16[2,96,1792]{2,1,0:T(8,128)(2,1)}, bf16[2,96,1792]{2,1,0:T(8,128)(2,1)S(1)}, u32[]{:S(2)}) copy-start(bf16[2,96,1792]{2,1,0:T(8,128)(2,1)S(1)} %collective-permute-done.3) | copy-start | bytes 2064388
  63.2 43.5 %collective-permute-start.17 = (bf16[2,96,1792]{2,1,0:T(8,128)(2,1)S(1)}, bf16[2,96,1792]{2,1,0:T(8,128)(2,1)S(1)}, u32[]{:S(2)}, u32[]{:S(2)}) collective-permute-start(bf16[2,96,1792]{2,1,0:T(8,128)(2,1)S(1)} %get-tuple-element.26), channel_id=1, source_target_pairs={{0,24},{4,28},{8,0},{12,4},{16,8},{20,12},{24,16},{28,20},{1,25},{... | collective-permute-start | bytes 2064392 | tf_op jit(solution)/shard_map/ppermute | solution.py:167
  73.1 33.2 %copy-start.8 = (bf16[2,96,1792]{2,1,0:T(8,128)(2,1)}, bf16[2,96,1792]{2,1,0:T(8,128)(2,1)S(1)}, u32[]{:S(2)}) copy-start(bf16[2,96,1792]{2,1,0:T(8,128)(2,1)S(1)} %collective-permute-done.5) | copy-start | bytes 2064388
  73.1 22.3 %collective-permute-start.6 = (bf16[96,1792]{1,0:T(8,128)(2,1)S(1)}, bf16[96,1792]{1,0:T(8,128)(2,1)S(1)}, u32[]{:S(2)}, u32[]{:S(2)}) collective-permute-start(bf16[96,1792]{1,0:T(8,128)(2,1)S(1)} %slice_bitcast_fusion.3), channel_id=1, source_target_pairs={{0,8},{4,12},{8,16},{12,20},{16,24},{20,28},{24,0},{28,4},{1,9},{5... | collective-permute-start | bytes 1032200 | tf_op jit(solution)/shard_map/ppermute | solution.py:167
  78.0 28.8 %copy-start.10 = (bf16[2,96,1792]{2,1,0:T(8,128)(2,1)}, bf16[2,96,1792]{2,1,0:T(8,128)(2,1)S(1)}, u32[]{:S(2)}) copy-start(bf16[2,96,1792]{2,1,0:T(8,128)(2,1)S(1)} %collective-permute-done.16) | copy-start | bytes 2064388
  78.0 17.5 %collective-permute-start.7 = (bf16[96,1792]{1,0:T(8,128)(2,1)S(1)}, bf16[96,1792]{1,0:T(8,128)(2,1)S(1)}, u32[]{:S(2)}, u32[]{:S(2)}) collective-permute-start(bf16[96,1792]{1,0:T(8,128)(2,1)S(1)} %slice_bitcast_fusion.2), channel_id=1, source_target_pairs={{0,24},{4,28},{8,0},{12,4},{16,8},{20,12},{24,16},{28,20},{1,25},{... | collective-permute-start | bytes 1032200 | tf_op jit(solution)/shard_map/ppermute | solution.py:167
  92.1 14.7 %copy-start.11 = (bf16[2,96,1792]{2,1,0:T(8,128)(2,1)}, bf16[2,96,1792]{2,1,0:T(8,128)(2,1)S(1)}, u32[]{:S(2)}) copy-start(bf16[2,96,1792]{2,1,0:T(8,128)(2,1)S(1)} %collective-permute-done.18) | copy-start | bytes 2064388
  92.1 14.6 %collective-permute-start.19 = (bf16[96,1792]{1,0:T(8,128)(2,1)S(1)}, bf16[96,1792]{1,0:T(8,128)(2,1)S(1)}, u32[]{:S(2)}, u32[]{:S(2)}) collective-permute-start(bf16[96,1792]{1,0:T(8,128)(2,1)S(1)} %slice_bitcast_fusion.1), channel_id=1, source_target_pairs={{0,8},{4,12},{8,16},{12,20},{16,24},{20,28},{24,0},{28,4},{1,9},{5... | collective-permute-start | bytes 1032200 | tf_op jit(solution)/shard_map/ppermute | solution.py:167
  93.7 12.7 %copy-start.12 = (bf16[2,96,1792]{2,1,0:T(8,128)(2,1)}, bf16[2,96,1792]{2,1,0:T(8,128)(2,1)S(1)}, u32[]{:S(2)}) copy-start(bf16[2,96,1792]{2,1,0:T(8,128)(2,1)S(1)} %collective-permute-done.4) | copy-start | bytes 2064388
  93.7 13.1 %collective-permute-start.20 = (bf16[96,1792]{1,0:T(8,128)(2,1)S(1)}, bf16[96,1792]{1,0:T(8,128)(2,1)S(1)}, u32[]{:S(2)}, u32[]{:S(2)}) collective-permute-start(bf16[96,1792]{1,0:T(8,128)(2,1)S(1)} %slice_bitcast_fusion), channel_id=1, source_target_pairs={{0,24},{4,28},{8,0},{12,4},{16,8},{20,12},{24,16},{28,20},{1,25},{... | collective-permute-start | bytes 1032200 | tf_op jit(solution)/shard_map/ppermute | solution.py:167
  95.5 10.9 %copy-start.15 = (bf16[96,1792]{1,0:T(8,128)(2,1)}, bf16[96,1792]{1,0:T(8,128)(2,1)S(1)}, u32[]{:S(2)}) copy-start(bf16[96,1792]{1,0:T(8,128)(2,1)S(1)} %collective-permute-done.6.refs_7_) | copy-start | bytes 1032196
  95.5 10.9 %copy-start.17 = (bf16[96,1792]{1,0:T(8,128)(2,1)}, bf16[96,1792]{1,0:T(8,128)(2,1)S(1)}, u32[]{:S(2)}) copy-start(bf16[96,1792]{1,0:T(8,128)(2,1)S(1)} %collective-permute-done.7.refs_8_) | copy-start | bytes 1032196
  106.4 12.0 %collective-permute-start.8 = (bf16[4,2,96,1024]{3,2,1,0:T(8,128)(2,1)}, bf16[4,2,96,1024]{3,2,1,0:T(8,128)(2,1)S(1)}, u32[]{:S(2)}, u32[]{:S(2)}) collective-permute-start(bf16[4,2,96,1024]{3,2,1,0:T(8,128)(2,1)} %get-tuple-element.7), channel_id=1, source_target_pairs={{0,32},{32,0},{64,96},{96,64},{1,33},{33,1},{65,97},{97,65},{2,34}... | collective-permute-start | bytes 4718600 | tf_op jit(solution)/shard_map/ppermute | solution.py:179
  106.7 11.1 %copy-start.14 = (bf16[2,96,1792]{2,1,0:T(8,128)(2,1)}, bf16[2,96,1792]{2,1,0:T(8,128)(2,1)S(1)}, u32[]{:S(2)}) copy-start(bf16[2,96,1792]{2,1,0:T(8,128)(2,1)S(1)} %collective-permute-done.17) | copy-start | bytes 2064388
  106.7 11.1 %copy-start.19 = (bf16[96,1792]{1,0:T(8,128)(2,1)}, bf16[96,1792]{1,0:T(8,128)(2,1)S(1)}, u32[]{:S(2)}) copy-start(bf16[96,1792]{1,0:T(8,128)(2,1)S(1)} %collective-permute-done.19.refs_7_.refs_16_) | copy-start | bytes 1032196
  106.8 11.0 %copy-start.21 = (bf16[96,1792]{1,0:T(8,128)(2,1)}, bf16[96,1792]{1,0:T(8,128)(2,1)S(1)}, u32[]{:S(2)}) copy-start(bf16[96,1792]{1,0:T(8,128)(2,1)S(1)} %collective-permute-done.20.refs_8_.refs_17_) | copy-start | bytes 1032196
  106.8 11.6 %copy-start.24 = (bf16[4,2,96,1024]{3,2,1,0:T(8,128)(2,1)S(1)}, bf16[4,2,96,1024]{3,2,1,0:T(8,128)(2,1)}, u32[]{:S(2)}) copy-start(bf16[4,2,96,1024]{3,2,1,0:T(8,128)(2,1)} %get-tuple-element.6) | copy-start | bytes 4718596
  117.8 6.4 %collective-permute-start.21 = (bf16[4,2,96,1024]{3,2,1,0:T(8,128)(2,1)}, bf16[4,2,96,1024]{3,2,1,0:T(8,128)(2,1)S(1)}, u32[]{:S(2)}, u32[]{:S(2)}) collective-permute-start(bf16[4,2,96,1024]{3,2,1,0:T(8,128)(2,1)} %get-tuple-element.9), channel_id=1, source_target_pairs={{0,32},{32,0},{64,96},{96,64},{1,33},{33,1},{65,97},{97,65},{2,34}... | collective-permute-start | bytes 4718600 | tf_op jit(solution)/shard_map/ppermute | solution.py:179
  118.4 5.8 %copy-start.23 = (bf16[4,2,96,1024]{3,2,1,0:T(8,128)(2,1)S(1)}, bf16[4,2,96,1024]{3,2,1,0:T(8,128)(2,1)}, u32[]{:S(2)}) copy-start(bf16[4,2,96,1024]{3,2,1,0:T(8,128)(2,1)} %get-tuple-element.8) | copy-start | bytes 4718596
  118.9 13.6 %collective-permute-start.10 = (bf16[2,96,1024]{2,1,0:T(8,128)(2,1)S(1)}, bf16[2,96,1024]{2,1,0:T(8,128)(2,1)S(1)}, u32[]{:S(2)}, u32[]{:S(2)}) collective-permute-start(bf16[2,96,1024]{2,1,0:T(8,128)(2,1)S(1)} %get-tuple-element.12), channel_id=1, source_target_pairs={{0,2},{1,3},{2,0},{3,1},{4,6},{5,7},{6,4},{7,5},{8,10},{9,11},{10,... | collective-permute-start | bytes 1179656 | tf_op jit(solution)/shard_map/ppermute | solution.py:175
  122.1 19.1 %collective-permute-start.11 = (bf16[2,96,1024]{2,1,0:T(8,128)(2,1)S(1)}, bf16[2,96,1024]{2,1,0:T(8,128)(2,1)S(1)}, u32[]{:S(2)}, u32[]{:S(2)}) collective-permute-start(bf16[2,96,1024]{2,1,0:T(8,128)(2,1)S(1)} %get-tuple-element.11), channel_id=1, source_target_pairs={{0,3},{1,0},{2,1},{3,2},{4,7},{5,4},{6,5},{7,6},{8,11},{9,8},{10,9... | collective-permute-start | bytes 1179656 | tf_op jit(solution)/shard_map/ppermute | solution.py:175
  123.2 18.0 %collective-permute-start.9 = (bf16[2,96,1024]{2,1,0:T(8,128)(2,1)S(1)}, bf16[2,96,1024]{2,1,0:T(8,128)(2,1)S(1)}, u32[]{:S(2)}, u32[]{:S(2)}) collective-permute-start(bf16[2,96,1024]{2,1,0:T(8,128)(2,1)S(1)} %get-tuple-element.10), channel_id=1, source_target_pairs={{0,1},{1,2},{2,3},{3,0},{4,5},{5,6},{6,7},{7,4},{8,9},{9,10},{10,1... | collective-permute-start | bytes 1179656 | tf_op jit(solution)/shard_map/ppermute | solution.py:175
  124.7 24.6 %collective-permute-start.22 = (bf16[2,96,1024]{2,1,0:T(8,128)(2,1)S(1)}, bf16[2,96,1024]{2,1,0:T(8,128)(2,1)S(1)}, u32[]{:S(2)}, u32[]{:S(2)}) collective-permute-start(bf16[2,96,1024]{2,1,0:T(8,128)(2,1)S(1)} %get-tuple-element.13), channel_id=1, source_target_pairs={{0,1},{1,2},{2,3},{3,0},{4,5},{5,6},{6,7},{7,4},{8,9},{9,10},{10,1... | collective-permute-start | bytes 1179656 | tf_op jit(solution)/shard_map/ppermute | solution.py:175
  125.4 31.4 %collective-permute-start.23 = (bf16[2,96,1024]{2,1,0:T(8,128)(2,1)S(1)}, bf16[2,96,1024]{2,1,0:T(8,128)(2,1)S(1)}, u32[]{:S(2)}, u32[]{:S(2)}) collective-permute-start(bf16[2,96,1024]{2,1,0:T(8,128)(2,1)S(1)} %get-tuple-element.15), channel_id=1, source_target_pairs={{0,2},{1,3},{2,0},{3,1},{4,6},{5,7},{6,4},{7,5},{8,10},{9,11},{10,... | collective-permute-start | bytes 1179656 | tf_op jit(solution)/shard_map/ppermute | solution.py:175
  132.5 24.7 %collective-permute-start.24 = (bf16[2,96,1024]{2,1,0:T(8,128)(2,1)S(1)}, bf16[2,96,1024]{2,1,0:T(8,128)(2,1)S(1)}, u32[]{:S(2)}, u32[]{:S(2)}) collective-permute-start(bf16[2,96,1024]{2,1,0:T(8,128)(2,1)S(1)} %get-tuple-element.14), channel_id=1, source_target_pairs={{0,3},{1,0},{2,1},{3,2},{4,7},{5,4},{6,5},{7,6},{8,11},{9,8},{10,9... | collective-permute-start | bytes 1179656 | tf_op jit(solution)/shard_map/ppermute | solution.py:175
  141.6 20.0 %collective-permute-start.12 = (bf16[96,1024]{1,0:T(8,128)(2,1)S(1)}, bf16[96,1024]{1,0:T(8,128)(2,1)S(1)}, u32[]{:S(2)}, u32[]{:S(2)}) collective-permute-start(bf16[96,1024]{1,0:T(8,128)(2,1)S(1)} %slice_bitcast_fusion.6), channel_id=1, source_target_pairs={{0,64},{32,96},{64,0},{96,32},{1,65},{33,97},{65,1},{97,33},{2,66}... | collective-permute-start | bytes 589832 | tf_op jit(solution)/shard_map/ppermute | solution.py:183
  157.5 9.1 %copy-start.3 = (bf16[2,96,1792]{2,1,0:T(8,128)(2,1)S(1)}, bf16[2,96,1792]{2,1,0:T(8,128)(2,1)}, u32[]{:S(2)}) copy-start(bf16[2,96,1792]{2,1,0:T(8,128)(2,1)} %copy-done.2) | copy-start | bytes 2064388
  157.5 9.1 %copy-start.7 = (bf16[2,96,1792]{2,1,0:T(8,128)(2,1)S(1)}, bf16[2,96,1792]{2,1,0:T(8,128)(2,1)}, u32[]{:S(2)}) copy-start(bf16[2,96,1792]{2,1,0:T(8,128)(2,1)} %copy-done.6) | copy-start | bytes 2064388
  157.6 8.3 %collective-permute-start.25 = (bf16[96,1024]{1,0:T(8,128)(2,1)S(1)}, bf16[96,1024]{1,0:T(8,128)(2,1)S(1)}, u32[]{:S(2)}, u32[]{:S(2)}) collective-permute-start(bf16[96,1024]{1,0:T(8,128)(2,1)S(1)} %slice_bitcast_fusion.4), channel_id=1, source_target_pairs={{0,64},{32,96},{64,0},{96,32},{1,65},{33,97},{65,1},{97,33},{2,66}... | collective-permute-start | bytes 589832 | tf_op jit(solution)/shard_map/ppermute | solution.py:183
  166.7 1.1 copy-start.9
  167.8 1.1 copy-start.13
  (4 other events, 3.9 us)
Sparse Core Ops, SparseCore 0:
  10.4 86.7 all-gather.1

commit v2 on v1

v2 whole, which is shorter than its diff:
```python
import functools

import jax
import jax.numpy as jnp
from jax import lax
from jax.experimental import pallas as pl
from jax.experimental.pallas import tpu as pltpu
from jax.sharding import PartitionSpec as P

BLOCK = 192
HINT = 16
PARTS = ((0, 128), (128, 64))
VMEM_LIMIT = 48 * 1024 * 1024
ANY = pl.BlockSpec(memory_space=pl.ANY)

PIECES = (
    ((0, 0, 0), (0, 0, 1)),
    ((3, 0, 0), (3, 0, 1)),
    ((1, 0, 0), (1, 0, 1)),
    ((0, 1, 0), (0, 1, 1)),
    ((2, 0, 0), (3, 1, 0)),
    ((2, 0, 1), (1, 1, 0)),
    ((1, 1, 1), (3, 1, 1)),
    ((2, 1, 0),),
    ((2, 1, 1),),
)


def source_of(shift, flip):
    col = lax.axis_index("col")
    x = lax.rem(col // 2 + shift, 4)
    z = lax.rem(col + flip, 2)
    return x, z


def grad_input_kernel(n, wanted, *refs):
    count = len(wanted)
    chunks, w_hbm = refs[:count], refs[count]
    keep, send = refs[-8:-6]
    w, g, o, w_sem, g_sem, o_sem = refs[-6:]
    row, y = lax.axis_index("row"), lax.axis_index("depth")
    w_copy = pltpu.make_async_copy(w_hbm, w, w_sem)
    w_copy.start()
    copies, at, places = [], 0, []
    for ref, index in zip(chunks, wanted):
        rows = n * len(PIECES[index])
        copy = pltpu.make_async_copy(ref, g.at[pl.ds(at, rows)], g_sem.at[len(copies)])
        copy.start()
        copies.append((copy, at + rows))
        places += [(at + n * i, p) for i, p in enumerate(PIECES[index])]
        at += rows
    w_copy.wait()
    waited, outs = 0, []
    group = 4
    for first in range(0, len(places), group):
        inside = places[first:first + group]
        low, high = inside[0][0], inside[-1][0] + n
        while waited < len(copies) and (waited == 0 or copies[waited - 1][1] < high):
            copies[waited][0].wait()
            waited += 1
        o[low:high, :] = jnp.dot(g[low:high, :], w[...], preferred_element_type=jnp.float32).astype(jnp.bfloat16)
        for start, (shift, flip, q) in inside:
            x, z = source_of(shift, flip)
            apart = lax.rem(x + row, 2)
            far = lax.rem(x // 2 + row // 2, 2)
            ahead = lax.rem(2 * z + q + 4 - y, 4)
            for which, ref in enumerate((keep, send)):
                copy = pltpu.make_async_copy(o.at[pl.ds(start, n)], ref.at[ahead, far], o_sem.at[len(outs) // 2])
                outs.append((apart == which, copy))
                pl.when(apart == which)(copy.start)
    for here, copy in outs:
        pl.when(here)(copy.wait)


def grad_input_part(n, wanted, chunks, weight, into=(), after=()):
    ff, d = weight.shape
    rows = n * sum(len(PIECES[index]) for index in wanted)
    out = jax.ShapeDtypeStruct((4, 2, n, d), jnp.bfloat16)
    args = [chunks[index] for index in wanted] + [weight, *after, *into]
    return pl.pallas_call(
        functools.partial(grad_input_kernel, n, wanted),
        out_shape=(out, out),
        in_specs=[ANY] * len(args),
        out_specs=(ANY,) * 2,
        scratch_shapes=[
            pltpu.VMEM((ff, d), jnp.bfloat16),
            pltpu.VMEM((rows, ff), jnp.bfloat16),
            pltpu.VMEM((rows, d), jnp.bfloat16),
            pltpu.SemaphoreType.DMA,
            pltpu.SemaphoreType.DMA((len(wanted),)),
            pltpu.SemaphoreType.DMA((rows // n,)),
        ],
        input_output_aliases={len(args) - 2 + i: i for i in range(len(into))},
        compiler_params=pltpu.CompilerParams(vmem_limit_bytes=VMEM_LIMIT),
        cost_estimate=pl.CostEstimate(
            flops=2 * rows * ff * d // HINT, bytes_accessed=rows * ff // HINT, transcendentals=0
        ),
    )(*args)


TILE = 256


def grad_weight_kernel(n, first, last, has_sum, final, *refs):
    count = len(PIECES)
    chunks, mine_hbm, other_hbm = refs[:count], refs[count], refs[count + 1]
    sum_hbm = refs[count + 2] if has_sum else None
    out = refs[-9]
    acts, g, total, o, g_sem, a_sem, t_sem, o_sem = refs[-8:]
    row, y = lax.axis_index("row"), lax.axis_index("depth")
    low = sum(m for _, m in PARTS[: [m for _, m in PARTS].index(n)])
    a_copies = []
    for core, ref in enumerate((mine_hbm, other_hbm)):
        for block in range(8):
            copy = pltpu.make_async_copy(
                ref.at[block // 2, block % 2, pl.ds(low, n), :],
                acts.at[pl.ds((core * 8 + block) * n, n), :],
                a_sem.at[core * 8 + block],
            )
            copy.start()
            a_copies.append(copy)
    copies = []
    for tile in range(first, last):
        at = tile - first
        of_tile = []
        for ref, pieces in zip(chunks, PIECES):
            for i, (shift, flip, q) in enumerate(pieces):
                x, z = source_of(shift, flip)
                block = lax.rem(x + row, 2) * 8 + (2 * z + q) * 2 + lax.rem(x // 2 + row // 2, 2)
                of_tile.append(
                    pltpu.make_async_copy(
                        ref.at[pl.ds(n * i, n), pl.ds(TILE * tile, TILE)],
                        g.at[at, pl.ds(pl.multiple_of(block * n, n), n), :],
                        g_sem.at[at * 16 + len(of_tile)],
                    )
                )
                of_tile[-1].start()
        if has_sum:
            of_tile.append(
                pltpu.make_async_copy(sum_hbm.at[pl.ds(TILE * tile, TILE), :], total.at[at], t_sem.at[at])
            )
            of_tile[-1].start()
        copies.append(of_tile)
    for copy in a_copies:
        copy.wait()
    outs = []
    for tile in range(first, last):
        at = tile - first
        for copy in copies[at]:
            copy.wait()
        value = lax.dot_general(g[at], acts[...], (((0,), (0,)), ((), ())), preferred_element_type=jnp.float32)
        if has_sum:
            value = value + total[at]
        if final:
            o[at] = value.astype(jnp.bfloat16)
        else:
            total[at] = value
        outs.append(
            pltpu.make_async_copy(
                (o if final else total).at[at], out.at[pl.ds(TILE * tile, TILE), :], o_sem.at[at]
            )
        )
        outs[-1].start()
    for copy in outs:
        copy.wait()


def grad_weight_tiles(n, first, last, chunks, mine, other, into=None, so_far=None, final=False, after=()):
    ff, d = chunks[0].shape[-1], mine.shape[-1]
    tiles, tokens = last - first, 16 * n
    args = [c.reshape(-1, ff) for c in chunks] + [mine, other] + ([] if so_far is None else [so_far])
    args += list(after) + ([] if into is None else [into])
    return pl.pallas_call(
        functools.partial(grad_weight_kernel, n, first, last, so_far is not None, final),
        out_shape=jax.ShapeDtypeStruct((ff, d), jnp.bfloat16 if final else jnp.float32),
        in_specs=[ANY] * len(args),
        out_specs=ANY,
        scratch_shapes=[
            pltpu.VMEM((tokens, d), jnp.bfloat16),
            pltpu.VMEM((tiles, tokens, TILE), jnp.bfloat16),
            pltpu.VMEM((tiles, TILE, d), jnp.float32),
            pltpu.VMEM((tiles, TILE, d), jnp.bfloat16),
            pltpu.SemaphoreType.DMA((tiles * 16,)),
            pltpu.SemaphoreType.DMA((16,)),
            pltpu.SemaphoreType.DMA((tiles,)),
            pltpu.SemaphoreType.DMA((tiles,)),
        ],
        input_output_aliases={} if into is None else {len(args) - 1: 0},
        compiler_params=pltpu.CompilerParams(vmem_limit_bytes=VMEM_LIMIT),
        cost_estimate=pl.CostEstimate(
            flops=2 * tokens * TILE * tiles * d // HINT,
            bytes_accessed=tokens * TILE * tiles // HINT,
            transcendentals=0,
        ),
    )(*args)


def pack_kernel(places, count, *refs):
    out, sems = refs[-2:]
    copies = []
    for k, (index, start, rows, to) in enumerate(places):
        copies.append(pltpu.make_async_copy(refs[index].at[pl.ds(start, rows)], out.at[pl.ds(to, rows)], sems.at[k]))
        copies[-1].start()
    for copy in copies:
        copy.wait()


def pack(sources, after=()):
    args, places, to = [], [], 0
    for array, start, rows in sources:
        places.append((len(args), start, rows, to))
        args.append(array)
        to += rows
    shape = jax.ShapeDtypeStruct((to, args[0].shape[1]), args[0].dtype)
    return pl.pallas_call(
        functools.partial(pack_kernel, tuple(places), len(args)),
        out_shape=shape,
        in_specs=[ANY] * (len(args) + len(after)),
        out_specs=ANY,
        scratch_shapes=[pltpu.SemaphoreType.DMA((len(places),))],
        cost_estimate=pl.CostEstimate(flops=0, bytes_accessed=4 * shape.size, transcendentals=0),
    )(*args, *after)


def along_x(value, shift):
    return lax.ppermute(value, "col", [(i, (i + 2 * shift) % 8) for i in range(8)])


def along_z(value):
    return lax.ppermute(value, "col", [(i, i ^ 1) for i in range(8)])


def along_y(value, shift):
    return lax.ppermute(value, "depth", [(i, (i + shift) % 4) for i in range(4)])


def other_core(value):
    return lax.ppermute(value, "row", [(i, i ^ 1) for i in range(4)])


def other_z_hi(value):
    return lax.ppermute(value, "row", [(i, i ^ 2) for i in range(4)])


def tie_kernel(*refs):
    pass


def tie(value, after):
    return pl.pallas_call(
        tie_kernel,
        out_shape=jax.ShapeDtypeStruct(value.shape, value.dtype),
        in_specs=[ANY] * (1 + len(after)),
        out_specs=ANY,
        input_output_aliases={0: 0},
        compiler_params=pltpu.CompilerParams(has_side_effects=True),
    )(value, *after)


def first_step(own):
    return along_x(own, 1), along_x(own, -1), along_z(own)


def second_sends(left, right, z):
    n = left.shape[0] // 2
    return (
        jnp.concatenate([left[:n], z[:n]]),
        jnp.concatenate([right[n:], z[:n]]),
        jnp.concatenate([right[n:], left[n:]]),
    )


def second_step(left, right, z):
    return along_x(left, 1), along_x(right, -1), along_z(z)


def third_sends(second, after=()):
    left2, right2, z2 = second
    n = left2.shape[0] // 2
    return pack([(left2, n, n)], after=(right2, *after)), pack([(z2, 0, n)], after=(right2, *after))


def third_step(left, right):
    return along_x(left, 1), along_x(right, -1)


def sum_kernel(groups, *refs):
    outs = refs[len(refs) - len(groups):]
    for out, terms in zip(outs, groups):
        total = None
        for index, at in terms:
            value = (refs[index][...] if at is None else refs[index][at]).astype(jnp.float32)
            total = value if total is None else total + value
        out[...] = total.astype(out.dtype)


def sums(inputs, groups, after=()):
    def shape_of(term):
        return inputs[term[0]].shape if term[1] is None else inputs[term[0]].shape[1:]

    shapes = [jax.ShapeDtypeStruct(shape_of(g[0]), jnp.bfloat16) for g in groups]
    vmem = pl.BlockSpec(memory_space=pltpu.VMEM)
    return pl.pallas_call(
        functools.partial(sum_kernel, groups),
        out_shape=shapes,
        in_specs=[vmem] * len(inputs) + [ANY] * len(after),
        out_specs=[vmem] * len(groups),
        compiler_params=pltpu.CompilerParams(vmem_limit_bytes=VMEM_LIMIT // 2),
    )(*inputs, *after)


def add_cores(keep, got, after=()):
    return sums((keep, got), [((0, i), (1, i)) for i in range(4)], after)


def send_y(q):
    return [along_y(q[i], i) for i in (1, 2, 3)]


def add_y(q, got, after=()):
    return sums((q[0], *got), [tuple((i, k) for i in range(4)) for k in range(2)], after)


def final_kernel(low, n, has_into, near, got, *refs):
    out, value, sem = refs[-3:]
    value[...] = (near[...].astype(jnp.float32) + got[...].astype(jnp.float32)).astype(value.dtype)
    copy = pltpu.make_async_copy(value, out.at[pl.ds(low, n), :], sem)
    copy.start()
    copy.wait()


def final(low, near, got, into=None, after=()):
    n, d = near.shape
    vmem = pl.BlockSpec(memory_space=pltpu.VMEM)
    args = [near, got, *after] + ([] if into is None else [into])
    return pl.pallas_call(
        functools.partial(final_kernel, low, n, into is not None),
        out_shape=jax.ShapeDtypeStruct((BLOCK, d), jnp.bfloat16),
        in_specs=[vmem] * 2 + [ANY] * (len(args) - 2),
        out_specs=ANY,
        scratch_shapes=[pltpu.VMEM((n, d), jnp.bfloat16), pltpu.SemaphoreType.DMA],
        input_output_aliases={} if into is None else {len(args) - 1: 0},
    )(*args)


ALL = tuple(range(len(PIECES)))
EARLY, LATE = ALL[:4], ALL[4:]


def shards(activations, grad_output, weight):
    ff = grad_output.shape[1]
    tiles = ff // TILE
    (low0, n0), (low1, n1) = PARTS

    own0 = pack([(grad_output, low0, n0), (grad_output, BLOCK + low0, n0)])
    first0 = first_step(own0)
    far = other_z_hi(pack([(activations, 0, BLOCK)], after=(own0,)))
    pair = pack([(activations, 0, BLOCK), (far, 0, BLOCK)], after=(own0,))
    mine = lax.all_gather(pair.reshape(2, BLOCK, -1), "depth", axis=0)
    sends = second_sends(*first0)
    second0 = second_step(*sends)
    own1 = pack([(grad_output, low1, n1), (grad_output, BLOCK + low1, n1)], after=sends)
    first1 = first_step(own1)
    third0 = third_step(*third_sends(second0))
    chunks0 = [own0, *first0, *second0, *third0]
    sends = second_sends(*first1)
    second1 = second_step(*sends)
    mine = tie(mine, (*sends, *third0))
    other = other_core(mine)

    keep0, send0 = grad_input_part(n0, ALL, chunks0, weight, after=sends)
    cores0 = other_core(send0)
    so_far = grad_weight_tiles(n0, 0, 4, chunks0, mine, other, after=(keep0,))
    q0 = add_cores(keep0, cores0, after=(so_far,))
    y0 = send_y(q0)
    sends = third_sends(second1, after=(so_far,))
    third1 = third_step(*sends)
    chunks1 = [own1, *first1, *second1, *third1]
    so_far = grad_weight_tiles(n0, 4, tiles, chunks0, mine, other, into=so_far, after=(q0[0], *sends))
    part1 = grad_input_part(n1, EARLY, chunks1, weight, after=(so_far,))
    keep1, send1 = grad_input_part(n1, LATE, chunks1, weight, into=part1)
    cores1 = other_core(send1)
    near0 = add_y(q0, y0, after=(keep1,))
    far0 = other_z_hi(near0[1])
    q1 = add_cores(keep1, cores1, after=(near0[0],))
    y1 = send_y(q1)
    weight_grad = grad_weight_tiles(
        n1, 0, tiles, chunks1, mine, other, so_far=so_far, final=True, after=(q1[0],)
    )
    result = final(low0, near0[0], far0, after=(weight_grad,))
    near1 = add_y(q1, y1, after=(result,))
    far1 = other_z_hi(near1[1])
    result = final(low1, near1[0], far1, into=result)
    return result, weight_grad


def solution(mesh):
    in_specs = (P(("row", "depth"), "col"), P("col", ("row", "depth")), P(("row", "depth"), "col"))
    out_specs = (P(("row", "depth"), "col"), P(("row", "depth"), "col"))
    return jax.shard_map(shards, mesh=mesh, in_specs=in_specs, out_specs=out_specs, check_vma=False)
```

time: 203 us -> 333 us (1.64)
  Pallas kernels: 44.1 us -> 184 us
  waiting for transfers between devices: 93.3 us -> 65 us
  local copies, waits for them, and re-layouts: 7.89 us -> 25.8 us
    pallas_call x4 -> x21, Pallas kernels: 44.1 us -> 184 us  [the longest x8 128 us: pack(): pl.pallas_call(functools.partial(pack_kernel, tuple(places), len(args)),...]
    ppermute x4, waiting for transfers between devices: 50.1 us -> 2.17 us  [along_z(): return lax.ppermute(value, 'col', [(i, i ^ 1) for i in range(8)])]
    unnamed x50 -> x72, local copies, waits for them, and re-layouts: 6.18 us -> 22.7 us
    ppermute x2 -> x3, waiting for transfers between devices: 4.2 us -> 14.6 us  [other_z_hi(): return lax.ppermute(value, 'row', [(i, i ^ 2) for i in range(4)])]
    ppermute x12, waiting for transfers between devices: 16.6 us -> 25.9 us  [along_x(): lax.ppermute(value, 'col', [(i, (i + 2 * shift) % 8) for i in range(8)])]
    ppermute x2 -> x3, starting transfers between devices: 7.78 us -> 7.65 us  [other_z_hi(): return lax.ppermute(value, 'row', [(i, i ^ 2) for i in range(4)])]
  transfers between devices with their start and end apart: 27 -> 29, of which waited for: 14 -> 9; matrix products, arithmetic and copies ran while one was open for 2% -> 2% of each run, Pallas kernels for 11% -> 33%
where the time goes in v2:
time: 333 us; the launch traced here: 332 us
  Pallas kernels  184 us (55%)
  waiting for transfers between devices  65 us (20%)
  starting transfers between devices  39.6 us (12%)
  local copies, waits for them, and re-layouts  25.8 us (8%)
  between operations  14.5 us (4%)
    pallas_call x8, Pallas kernels, pack(): pl.pallas_call(functools.partial(pack_kernel, tuple(places), len(args)),...  128 us
    pallas_call x3, Pallas kernels, grad_weight_tiles(): pl.pallas_call(functools.partial(grad_weight_kernel, n, first, last, so_f...  26.4 us
    ppermute x12, waiting for transfers between devices, along_x(): lax.ppermute(value, 'col', [(i, (i + 2 * shift) % 8) for i in range(8)])  25.9 us
    pallas_call x3, Pallas kernels, grad_input_part(): pl.pallas_call(functools.partial(grad_input_kernel, n, wanted), out_shape...  23.6 us
    unnamed x72, local copies, waits for them, and re-layouts  22.7 us
    ppermute x6, waiting for transfers between devices, along_y(): lax.ppermute(value, 'depth', [(i, (i + shift) % 4) for i in range(4)])  22.3 us
    ppermute x12, starting transfers between devices, along_x(): lax.ppermute(value, 'col', [(i, (i + 2 * shift) % 8) for i in range(8)])  15.7 us
    ppermute x3, waiting for transfers between devices, other_z_hi(): return lax.ppermute(value, 'row', [(i, i ^ 2) for i in range(4)])  14.6 us
  transfers between devices with their start and end apart: 29, of which 9 were waited for; matrix products, arithmetic and copies ran while one was open for 2% of the time, Pallas kernels for 33%

profile of v2, /device:TPU:0, one launch (start us, length us, event | category | flops | bytes accessed | tf_op | source)
XLA Modules:
  0.0 332.0 jit_solution(5913265048304699779)
XLA Ops:
  7.2 28.9 %shard_map.50.refs_1_.refs_2_.refs_0_ = bf16[256,1792]{1,0:T(8,128)(2,1)} custom-call(bf16[384,1792]{1,0:T(8,128)(2,1)} %refs_1_.3, bf16[384,1792]{1,0:T(8,128)(2,1)} %refs_1_.3), custom_call_target="tpu_custom_call" | custom-call | bytes 1835008 | tf_op jit(solution)/shard_map/pallas_call | solution.py:215
  36.1 13.0 %shard_map.54 = bf16[192,1024]{1,0:T(8,128)(2,1)} custom-call(bf16[192,1024]{1,0:T(8,128)(2,1)} %refs_0_.7, bf16[256,1792]{1,0:T(8,128)(2,1)} %shard_map.50.refs_1_.refs_2_.refs_0_), custom_call_target="tpu_custom_call" | custom-call | bytes 786432 | tf_op jit(solution)/shard_map/pallas_call | solution.py:215
  49.2 4.0 %collective-permute-start.14 = (bf16[192,1024]{1,0:T(8,128)(2,1)}, bf16[192,1024]{1,0:T(8,128)(2,1)S(1)}, u32[]{:S(2)}, u32[]{:S(2)}) collective-permute-start(bf16[192,1024]{1,0:T(8,128)(2,1)} %shard_map.54), channel_id=1, source_target_pairs={{0,64},{32,96},{64,0},{96,32},{1,65},{33,97},{65,1},{97,33},{2,66}... | collective-permute-start | bytes 1179656 | tf_op jit(solution)/shard_map/ppermute | solution.py:242
  53.2 9.3 %collective-permute-done.14.refs_1_ = bf16[192,1024]{1,0:T(8,128)(2,1)S(1)} collective-permute-done((bf16[192,1024]{1,0:T(8,128)(2,1)}, bf16[192,1024]{1,0:T(8,128)(2,1)S(1)}, u32[]{:S(2)}, u32[]{:S(2)}) %collective-permute-start.14) | collective-permute-done | bytes 393248 | tf_op jit(solution)/shard_map/ppermute | solution.py:242
  63.3 24.9 %shard_map.55 = bf16[384,1024]{1,0:T(8,128)(2,1)} custom-call(bf16[192,1024]{1,0:T(8,128)(2,1)} %refs_0_.7, bf16[192,1024]{1,0:T(8,128)(2,1)} %copy-done.33, bf16[256,1792]{1,0:T(8,128)(2,1)} %shard_map.50.refs_1_.refs_2_.refs_0_), custom_call_target="tpu_custom_call" | custom-call | bytes 1572864 | tf_op jit(solution)/shard_map/pallas_call | solution.py:215
  88.3 2.8 collective-permute-start.2
  91.1 1.3 collective-permute-start.1
  92.4 17.8 %collective-permute-done.2.refs_2_ = bf16[256,1792]{1,0:T(8,128)(2,1)S(1)} collective-permute-done((bf16[256,1792]{1,0:T(8,128)(2,1)S(1)}, bf16[256,1792]{1,0:T(8,128)(2,1)S(1)}, u32[]{:S(2)}, u32[]{:S(2)}) %collective-permute-start.2) | collective-permute-done | bytes 917536 | tf_op jit(solution)/shard_map/ppermute | solution.py:226
  110.2 2.2 collective-permute-done.1.refs_3_
  114.3 1.6 pad_maximum_fusion.2
  117.0 1.4 collective-permute-start.10
  119.0 15.0 %shard_map.51.refs_0_ = bf16[128,1792]{1,0:T(8,128)(2,1)} custom-call(bf16[384,1792]{1,0:T(8,128)(2,1)} %refs_1_.3, bf16[384,1792]{1,0:T(8,128)(2,1)} %refs_1_.3, bf16[256,1792]{1,0:T(8,128)(2,1)} %get-tuple-element.44.refs_2_, bf16[256,1792]{1,0:T(8,128)(2,1)} %get-tuple-element.43.refs_3_, bf16[256,1792]{1,0:T(8,128)(2,1)} %get-tuple-element.42.refs_4_), custom_call_target="tpu_custom_call" | custom-call | bytes 917504 | tf_op jit(solution)/shard_map/pallas_call | solution.py:215
  134.2 3.2 collective-permute-start.6
  138.3 1.8 collective-permute-done.10.refs_1_.refs_5_
  140.2 15.0 %shard_map.53 = bf16[128,1792]{1,0:T(8,128)(2,1)} custom-call(bf16[256,1792]{1,0:T(8,128)(2,1)} %collective-permute-done.11.refs_0_.refs_6_, bf16[256,1792]{1,0:T(8,128)(2,1)} %collective-permute-done.10.refs_1_.refs_5_), custom_call_target="tpu_custom_call" | custom-call | bytes 917504 | tf_op jit(solution)/shard_map/pallas_call | solution.py:215
  155.2 1.7 collective-permute-start.13
  157.8 15.0 %shard_map.52 = bf16[128,1792]{1,0:T(8,128)(2,1)} custom-call(bf16[256,1792]{1,0:T(8,128)(2,1)} %copy-done.2, bf16[256,1792]{1,0:T(8,128)(2,1)} %collective-permute-done.10.refs_1_.refs_5_), custom_call_target="tpu_custom_call" | custom-call | bytes 917504 | tf_op jit(solution)/shard_map/pallas_call | solution.py:215
  177.5 5.3 %collective-permute-done.12.refs_4_.refs_7_ = bf16[128,1792]{1,0:T(8,128)(2,1)S(1)} collective-permute-done((bf16[128,1792]{1,0:T(8,128)(2,1)}, bf16[128,1792]{1,0:T(8,128)(2,1)S(1)}, u32[]{:S(2)}, u32[]{:S(2)}) %collective-permute-start.12) | collective-permute-done | bytes 458784 | tf_op jit(solution)/shard_map/ppermute | solution.py:226
  183.6 1.3 copy-done.5
  184.9 1.2 copy-done.8
  190.1 11.5 %shard_map.57 = (bf16[4,2,128,1024]{3,2,1,0:T(8,128)(2,1)}, bf16[4,2,128,1024]{3,2,1,0:T(8,128)(2,1)}) custom-call(bf16[256,1792]{1,0:T(8,128)(2,1)S(1)} %copy-done.1, bf16[256,1792]{1,0:T(8,128)(2,1)S(1)} %collective-permute-done.refs_1_, bf16[256,1792]{1,0:T(8,128)(2,1)S(1)} %copy-done.5, bf16[256,1792]{1,0:T(8,128)(2,1)S(1)} %copy-done.8, ...), custom_call_target="tpu_custom_call" | custom-call | flops 469762048 | bytes 229376 | tf_op jit(solution)/shard_map/pallas_call | solution.py:80
  202.1 2.0 collective-permute-start.5
  204.1 1.4 collective-permute-start.8
  205.6 1.7 copy-done.32
  207.3 9.1 %shard_map.58.refs_2_.refs_14_ = f32[1792,1024]{1,0:T(8,128)} custom-call(bf16[256,1792]{1,0:T(8,128)(2,1)S(1)} %copy-done.1, bf16[256,1792]{1,0:T(8,128)(2,1)S(1)} %collective-permute-done.refs_1_, bf16[256,1792]{1,0:T(8,128)(2,1)S(1)} %copy-done.5, bf16[256,1792]{1,0:T(8,128)(2,1)S(1)} %copy-done.8, bf16[256,1792]{1,0:T(8,128)(2,1)S(1)} %copy-done.3, ...), custom_call_target="tpu_custom_call" | custom-call | flops 268435456 | bytes 131072 | tf_op jit(solution)/shard_map/pallas_call | solution.py:173
  218.0 8.1 %shard_map.59.refs_12_ = bf16[64,1792]{1,0:T(8,128)(2,1)} custom-call(bf16[128,1792]{1,0:T(8,128)(2,1)} %copy-done.22, bf16[128,1792]{1,0:T(8,128)(2,1)} %copy-done.17, f32[1792,1024]{1,0:T(8,128)} %shard_map.58.refs_2_.refs_14_), custom_call_target="tpu_custom_call" | custom-call | bytes 458752 | tf_op jit(solution)/shard_map/pallas_call | solution.py:215
  226.2 8.1 %shard_map.60.refs_13_ = bf16[64,1792]{1,0:T(8,128)(2,1)} custom-call(bf16[128,1792]{1,0:T(8,128)(2,1)} %collective-permute-done.8.refs_0_.refs_2_.refs_6_, bf16[128,1792]{1,0:T(8,128)(2,1)} %copy-done.17, f32[1792,1024]{1,0:T(8,128)} %shard_map.58.refs_2_.refs_14_), custom_call_target="tpu_custom_call" | custom-call | bytes 458752 | tf_op jit(solution)/shard_map/pallas_call | solution.py:215
  234.2 3.3 collective-permute-start.17
  237.5 3.1 copy-done
  240.6 1.6 copy-done.10
  242.2 2.2 shard_map.61
  246.2 7.8 %shard_map.62.refs_5_.refs_11_ = f32[1792,1024]{1,0:T(8,128)} custom-call(bf16[256,1792]{1,0:T(8,128)(2,1)S(1)} %copy-done.1, bf16[256,1792]{1,0:T(8,128)(2,1)S(1)} %collective-permute-done.refs_1_, bf16[256,1792]{1,0:T(8,128)(2,1)S(1)} %copy-done.6, bf16[256,1792]{1,0:T(8,128)(2,1)S(1)} %copy-done.9, ...), custom_call_target="tpu_custom_call", output_to_operand_aliasing={{}: (14, {})} | custom-call | flops 201326592 | bytes 98304 | tf_op jit(solution)/shard_map/pallas_call | solution.py:173
  254.0 6.0 %shard_map.63 = (bf16[4,2,64,1024]{3,2,1,0:T(8,128)(2,1)S(1)}, bf16[4,2,64,1024]{3,2,1,0:T(8,128)(2,1)S(1)}) custom-call(bf16[128,1792]{1,0:T(8,128)(2,1)S(1)} %copy-done.21, bf16[128,1792]{1,0:T(8,128)(2,1)} %collective-permute-done.3.refs_1_, bf16[128,1792]{1,0:T(8,128)(2,1)} %collective-permute-done.6.refs_2_, ...), custom_call_target="tpu_custom_call" | custom-call | flops 117440512 | bytes 57344 | tf_op jit(solution)/shard_map/pallas_call | solution.py:80
  260.1 6.1 %shard_map.64 = (bf16[4,2,64,1024]{3,2,1,0:T(8,128)(2,1)S(1)}, bf16[4,2,64,1024]{3,2,1,0:T(8,128)(2,1)S(1)}) custom-call(bf16[128,1792]{1,0:T(8,128)(2,1)S(1)} %copy-done.23, bf16[128,1792]{1,0:T(8,128)(2,1)S(1)} %copy-done.18, bf16[128,1792]{1,0:T(8,128)(2,1)} %collective-permute-done.8.refs_0_.refs_2_.refs_6_, ...), custom_call_target="tpu_custom_call", output_to_operand_aliasing={{0}: (6, {}), {1}: (7, {})} | custom-call | flops 117440512 | bytes 57344 | tf_op jit(solution)/shard_map/pallas_call | solution.py:80
  266.3 1.5 collective-permute-start.20
  267.9 3.0 collective-permute-start.21
  270.9 1.2 collective-permute-start.22
  272.1 9.8 %collective-permute-done.20.refs_1_ = bf16[2,128,1024]{2,1,0:T(8,128)(2,1)S(1)} collective-permute-done((bf16[2,128,1024]{2,1,0:T(8,128)(2,1)S(1)}, bf16[2,128,1024]{2,1,0:T(8,128)(2,1)S(1)}, u32[]{:S(2)}, u32[]{:S(2)}) %collective-permute-start.20) | collective-permute-done | bytes 524320 | tf_op jit(solution)/shard_map/ppermute | solution.py:234
  281.9 12.4 %collective-permute-done.21.refs_2_ = bf16[2,128,1024]{2,1,0:T(8,128)(2,1)S(1)} collective-permute-done((bf16[2,128,1024]{2,1,0:T(8,128)(2,1)S(1)}, bf16[2,128,1024]{2,1,0:T(8,128)(2,1)S(1)}, u32[]{:S(2)}, u32[]{:S(2)}) %collective-permute-start.21) | collective-permute-done | bytes 524320 | tf_op jit(solution)/shard_map/ppermute | solution.py:234
  294.6 2.4 collective-permute-start.26
  297.3 1.2 collective-permute-start.23
  298.5 2.4 collective-permute-start.24
  300.9 1.6 collective-permute-start.25
  302.5 9.5 %shard_map.67.refs_0_ = bf16[1792,1024]{1,0:T(8,128)(2,1)} custom-call(bf16[128,1792]{1,0:T(8,128)(2,1)S(1)} %copy-done.21, bf16[128,1792]{1,0:T(8,128)(2,1)} %collective-permute-done.3.refs_1_, bf16[128,1792]{1,0:T(8,128)(2,1)} %collective-permute-done.6.refs_2_, bf16[128,1792]{1,0:T(8,128)(2,1)} %collective-permute-done.4.refs_3_, ...), custom_call_target="tpu_custom_call" | custom-call | flops 234881024 | bytes 114688 | tf_op jit(solution)/shard_map/pallas_call | solution.py:173
  312.7 1.8 shard_map.68.refs_4_.refs_0_
  316.3 1.2 collective-permute-start.27
  317.5 5.3 %collective-permute-done.27.got = bf16[64,1024]{1,0:T(8,128)(2,1)S(1)} collective-permute-done((bf16[64,1024]{1,0:T(8,128)(2,1)S(1)}, bf16[64,1024]{1,0:T(8,128)(2,1)S(1)}, u32[]{:S(2)}, u32[]{:S(2)}) %collective-permute-start.27) | collective-permute-done | bytes 131104 | tf_op jit(solution)/shard_map/ppermute | solution.py:242
  323.4 1.7 shard_map.70
  (112 shorter events, 23.7 us)
Async XLA Ops:
  7.2 175.6 %all-gather.2.cloned.1.call-start = ((), (), s32[]{:S(2)}) async-start(), calls=%async_computation | async-start | bytes 3932160 | tf_op jit(solution)/shard_map/all_gather | solution.py:359
  36.1 52.1 %copy-start.1 = (bf16[256,1792]{1,0:T(8,128)(2,1)S(1)}, bf16[256,1792]{1,0:T(8,128)(2,1)}, u32[]{:S(2)}) copy-start(bf16[256,1792]{1,0:T(8,128)(2,1)} %shard_map.50.refs_1_.refs_2_.refs_0_) | copy-start | bytes 2752516
  49.2 13.4 %collective-permute-start.14 = (bf16[192,1024]{1,0:T(8,128)(2,1)}, bf16[192,1024]{1,0:T(8,128)(2,1)S(1)}, u32[]{:S(2)}, u32[]{:S(2)}) collective-permute-start(bf16[192,1024]{1,0:T(8,128)(2,1)} %shard_map.54), channel_id=1, source_target_pairs={{0,64},{32,96},{64,0},{96,32},{1,65},{33,97},{65,1},{97,33},{2,66}... | collective-permute-start | bytes 1179656 | tf_op jit(solution)/shard_map/ppermute | solution.py:242
  88.3 21.9 %collective-permute-start.2 = (bf16[256,1792]{1,0:T(8,128)(2,1)S(1)}, bf16[256,1792]{1,0:T(8,128)(2,1)S(1)}, u32[]{:S(2)}, u32[]{:S(2)}) collective-permute-start(bf16[256,1792]{1,0:T(8,128)(2,1)S(1)} %copy-done.1), channel_id=1, source_target_pairs={{0,24},{4,28},{8,0},{12,4},{16,8},{20,12},{24,16},{28,20},{1,25},{... | collective-permute-start | bytes 2752520 | tf_op jit(solution)/shard_map/ppermute | solution.py:226
  91.1 21.3 %collective-permute-start.1 = (bf16[256,1792]{1,0:T(8,128)(2,1)S(1)}, bf16[256,1792]{1,0:T(8,128)(2,1)S(1)}, u32[]{:S(2)}, u32[]{:S(2)}) collective-permute-start(bf16[256,1792]{1,0:T(8,128)(2,1)S(1)} %copy-done.1), channel_id=1, source_target_pairs={{0,4},{4,0},{8,12},{12,8},{16,20},{20,16},{24,28},{28,24},{1,5},{5... | collective-permute-start | bytes 2752520 | tf_op jit(solution)/shard_map/ppermute | solution.py:230
  92.4 21.9 %collective-permute-start = (bf16[256,1792]{1,0:T(8,128)(2,1)S(1)}, bf16[256,1792]{1,0:T(8,128)(2,1)S(1)}, u32[]{:S(2)}, u32[]{:S(2)}) collective-permute-start(bf16[256,1792]{1,0:T(8,128)(2,1)S(1)} %copy-done.1), channel_id=1, source_target_pairs={{0,8},{4,12},{8,16},{12,20},{16,24},{20,28},{24,0},{28,4},{1,9},{5... | collective-permute-start | bytes 2752520 | tf_op jit(solution)/shard_map/ppermute | solution.py:226
  110.2 2.2 copy-start.4
  116.0 21.4 %collective-permute-start.11 = (bf16[256,1792]{1,0:T(8,128)(2,1)}, bf16[256,1792]{1,0:T(8,128)(2,1)}, u32[]{:S(2)}, u32[]{:S(2)}) collective-permute-start(bf16[256,1792]{1,0:T(8,128)(2,1)} %get-tuple-element.42.refs_4_), channel_id=1, source_target_pairs={{0,4},{4,0},{8,12},{12,8},{16,20},{20,16},{24,28},{28,24},{1,5},{5... | collective-permute-start | bytes 2752520 | tf_op jit(solution)/shard_map/ppermute | solution.py:230
  117.0 23.1 %collective-permute-start.10 = (bf16[256,1792]{1,0:T(8,128)(2,1)}, bf16[256,1792]{1,0:T(8,128)(2,1)}, u32[]{:S(2)}, u32[]{:S(2)}) collective-permute-start(bf16[256,1792]{1,0:T(8,128)(2,1)} %get-tuple-element.43.refs_3_), channel_id=1, source_target_pairs={{0,24},{4,28},{8,0},{12,4},{16,8},{20,12},{24,16},{28,20},{1,25},{... | collective-permute-start | bytes 2752520 | tf_op jit(solution)/shard_map/ppermute | solution.py:226
  118.4 38.5 %collective-permute-start.9 = (bf16[256,1792]{1,0:T(8,128)(2,1)}, bf16[256,1792]{1,0:T(8,128)(2,1)S(1)}, u32[]{:S(2)}, u32[]{:S(2)}) collective-permute-start(bf16[256,1792]{1,0:T(8,128)(2,1)} %get-tuple-element.44.refs_2_), channel_id=1, source_target_pairs={{0,8},{4,12},{8,16},{12,20},{16,24},{20,28},{24,0},{28,4},{1,9},{5... | collective-permute-start | bytes 2752520 | tf_op jit(solution)/shard_map/ppermute | solution.py:226
  134.1 39.2 %collective-permute-start.3 = (bf16[128,1792]{1,0:T(8,128)(2,1)}, bf16[128,1792]{1,0:T(8,128)(2,1)}, u32[]{:S(2)}, u32[]{:S(2)}) collective-permute-start(bf16[128,1792]{1,0:T(8,128)(2,1)} %shard_map.51.refs_0_), channel_id=1, source_target_pairs={{0,8},{4,12},{8,16},{12,20},{16,24},{20,28},{24,0},{28,4},{1,9},{5... | collective-permute-start | bytes 1376264 | tf_op jit(solution)/shard_map/ppermute | solution.py:226
  134.2 40.3 %collective-permute-start.6 = (bf16[128,1792]{1,0:T(8,128)(2,1)}, bf16[128,1792]{1,0:T(8,128)(2,1)}, u32[]{:S(2)}, u32[]{:S(2)}) collective-permute-start(bf16[128,1792]{1,0:T(8,128)(2,1)} %shard_map.51.refs_0_), channel_id=1, source_target_pairs={{0,24},{4,28},{8,0},{12,4},{16,8},{20,12},{24,16},{28,20},{1,25},{... | collective-permute-start | bytes 1376264 | tf_op jit(solution)/shard_map/ppermute | solution.py:226
  137.4 38.0 %collective-permute-start.4 = (bf16[128,1792]{1,0:T(8,128)(2,1)}, bf16[128,1792]{1,0:T(8,128)(2,1)}, u32[]{:S(2)}, u32[]{:S(2)}) collective-permute-start(bf16[128,1792]{1,0:T(8,128)(2,1)} %shard_map.51.refs_0_), channel_id=1, source_target_pairs={{0,4},{4,0},{8,12},{12,8},{16,20},{20,16},{24,28},{28,24},{1,5},{5... | collective-permute-start | bytes 1376264 | tf_op jit(solution)/shard_map/ppermute | solution.py:230
  155.2 22.3 %collective-permute-start.13 = (bf16[128,1792]{1,0:T(8,128)(2,1)}, bf16[128,1792]{1,0:T(8,128)(2,1)S(1)}, u32[]{:S(2)}, u32[]{:S(2)}) collective-permute-start(bf16[128,1792]{1,0:T(8,128)(2,1)} %shard_map.53), channel_id=1, source_target_pairs={{0,24},{4,28},{8,0},{12,4},{16,8},{20,12},{24,16},{28,20},{1,25},{... | collective-permute-start | bytes 1376264 | tf_op jit(solution)/shard_map/ppermute | solution.py:226
  172.8 10.0 %collective-permute-start.12 = (bf16[128,1792]{1,0:T(8,128)(2,1)}, bf16[128,1792]{1,0:T(8,128)(2,1)S(1)}, u32[]{:S(2)}, u32[]{:S(2)}) collective-permute-start(bf16[128,1792]{1,0:T(8,128)(2,1)} %shard_map.52), channel_id=1, source_target_pairs={{0,8},{4,12},{8,16},{12,20},{16,24},{20,28},{24,0},{28,4},{1,9},{5... | collective-permute-start | bytes 1376264 | tf_op jit(solution)/shard_map/ppermute | solution.py:226
  177.5 5.3 %copy-start.11 = (bf16[128,1792]{1,0:T(8,128)(2,1)}, bf16[128,1792]{1,0:T(8,128)(2,1)S(1)}, u32[]{:S(2)}) copy-start(bf16[128,1792]{1,0:T(8,128)(2,1)S(1)} %collective-permute-done.13.refs_5_.refs_8_) | copy-start | bytes 1376260
  183.6 23.7 %copy-start.3 = (bf16[256,1792]{1,0:T(8,128)(2,1)S(1)}, bf16[256,1792]{1,0:T(8,128)(2,1)}, u32[]{:S(2)}) copy-start(bf16[256,1792]{1,0:T(8,128)(2,1)} %copy-done.2) | copy-start | bytes 2752516
  183.6 22.0 %collective-permute-start.15 = (bf16[4,2,192,1024]{3,2,1,0:T(8,128)(2,1)}, bf16[4,2,192,1024]{3,2,1,0:T(8,128)(2,1)S(1)}, u32[]{:S(2)}, u32[]{:S(2)}) collective-permute-start(bf16[4,2,192,1024]{3,2,1,0:T(8,128)(2,1)} %shard_map.56.refs_9_), channel_id=1, source_target_pairs={{0,32},{32,0},{64,96},{96,64},{1,33},{33,1},{65,97},{97,65},{2,34}... | collective-permute-start | bytes 9437192 | tf_op jit(solution)/shard_map/ppermute | solution.py:238
  183.6 1.3 copy-start.5
  201.6 35.9 %collective-permute-start.18 = (bf16[4,2,128,1024]{3,2,1,0:T(8,128)(2,1)}, bf16[4,2,128,1024]{3,2,1,0:T(8,128)(2,1)}, u32[]{:S(2)}, u32[]{:S(2)}) collective-permute-start(bf16[4,2,128,1024]{3,2,1,0:T(8,128)(2,1)} %get-tuple-element.21), channel_id=1, source_target_pairs={{0,32},{32,0},{64,96},{96,64},{1,33},{33,1},{65,97},{97,65},{2,34}... | collective-permute-start | bytes 6291464 | tf_op jit(solution)/shard_map/ppermute | solution.py:238
  202.1 14.3 %collective-permute-start.7 = (bf16[128,1792]{1,0:T(8,128)(2,1)S(1)}, bf16[128,1792]{1,0:T(8,128)(2,1)S(1)}, u32[]{:S(2)}, u32[]{:S(2)}) collective-permute-start(bf16[128,1792]{1,0:T(8,128)(2,1)S(1)} %copy-done.20), channel_id=1, source_target_pairs={{0,24},{4,28},{8,0},{12,4},{16,8},{20,12},{24,16},{28,20},{1,25},{... | collective-permute-start | bytes 1376264 | tf_op jit(solution)/shard_map/ppermute | solution.py:226
  202.1 14.3 %collective-permute-start.5 = (bf16[128,1792]{1,0:T(8,128)(2,1)S(1)}, bf16[128,1792]{1,0:T(8,128)(2,1)S(1)}, u32[]{:S(2)}, u32[]{:S(2)}) collective-permute-start(bf16[128,1792]{1,0:T(8,128)(2,1)S(1)} %copy-done.19), channel_id=1, source_target_pairs={{0,8},{4,12},{8,16},{12,20},{16,24},{20,28},{24,0},{28,4},{1,9},{5... | collective-permute-start | bytes 1376264 | tf_op jit(solution)/shard_map/ppermute | solution.py:226
  204.1 22.0 %collective-permute-start.8 = (bf16[128,1792]{1,0:T(8,128)(2,1)}, bf16[128,1792]{1,0:T(8,128)(2,1)}, u32[]{:S(2)}, u32[]{:S(2)}) collective-permute-start(bf16[128,1792]{1,0:T(8,128)(2,1)} %get-tuple-element.45.refs_3_.refs_12_), channel_id=1, source_target_pairs={{0,4},{4,0},{8,12},{12,8},{16,20},{20,16},{24,28},{28,24},{1,5},{5... | collective-permute-start | bytes 1376264 | tf_op jit(solution)/shard_map/ppermute | solution.py:230
  205.6 1.7 copy-start.32
  226.0 34.0 %collective-permute-start.16 = (bf16[64,1792]{1,0:T(8,128)(2,1)}, bf16[64,1792]{1,0:T(8,128)(2,1)}, u32[]{:S(2)}, u32[]{:S(2)}) collective-permute-start(bf16[64,1792]{1,0:T(8,128)(2,1)} %shard_map.59.refs_12_), channel_id=1, source_target_pairs={{0,8},{4,12},{8,16},{12,20},{16,24},{20,28},{24,0},{28,4},{1,9},{5... | collective-permute-start | bytes 688136 | tf_op jit(solution)/shard_map/ppermute | solution.py:226
  226.1 19.0 %copy-start.6 = (bf16[256,1792]{1,0:T(8,128)(2,1)S(1)}, bf16[256,1792]{1,0:T(8,128)(2,1)}, u32[]{:S(2)}) copy-start(bf16[256,1792]{1,0:T(8,128)(2,1)} %copy-done.4) | copy-start | bytes 2752516
  226.1 19.0 %copy-start.13 = (bf16[128,1792]{1,0:T(8,128)(2,1)S(1)}, bf16[128,1792]{1,0:T(8,128)(2,1)}, u32[]{:S(2)}) copy-start(bf16[128,1792]{1,0:T(8,128)(2,1)} %copy-done.11) | copy-start | bytes 1376260
  226.1 19.0 %copy-start.29 = (bf16[64,1792]{1,0:T(8,128)(2,1)S(1)}, bf16[64,1792]{1,0:T(8,128)(2,1)}, u32[]{:S(2)}) copy-start(bf16[64,1792]{1,0:T(8,128)(2,1)} %shard_map.59.refs_12_) | copy-start | bytes 688132
  234.2 25.9 %collective-permute-start.17 = (bf16[64,1792]{1,0:T(8,128)(2,1)}, bf16[64,1792]{1,0:T(8,128)(2,1)}, u32[]{:S(2)}, u32[]{:S(2)}) collective-permute-start(bf16[64,1792]{1,0:T(8,128)(2,1)} %shard_map.60.refs_13_), channel_id=1, source_target_pairs={{0,24},{4,28},{8,0},{12,4},{16,8},{20,12},{24,16},{28,20},{1,25},{... | collective-permute-start | bytes 688136 | tf_op jit(solution)/shard_map/ppermute | solution.py:226
  237.5 3.1 copy-start
  240.6 1.6 copy-start.10
  242.2 3.0 copy-start.9
  242.2 3.0 copy-start.16
  242.2 3.0 copy-start.30
  246.2 7.8 %copy-start.21 = (bf16[128,1792]{1,0:T(8,128)(2,1)S(1)}, bf16[128,1792]{1,0:T(8,128)(2,1)}, u32[]{:S(2)}) copy-start(bf16[128,1792]{1,0:T(8,128)(2,1)} %shard_map.51.refs_0_) | copy-start | bytes 1376260
  254.0 6.1 %copy-start.18 = (bf16[128,1792]{1,0:T(8,128)(2,1)S(1)}, bf16[128,1792]{1,0:T(8,128)(2,1)}, u32[]{:S(2)}) copy-start(bf16[128,1792]{1,0:T(8,128)(2,1)} %copy-done.17) | copy-start | bytes 1376260
  254.0 6.1 %copy-start.23 = (bf16[128,1792]{1,0:T(8,128)(2,1)S(1)}, bf16[128,1792]{1,0:T(8,128)(2,1)}, u32[]{:S(2)}) copy-start(bf16[128,1792]{1,0:T(8,128)(2,1)} %copy-done.22) | copy-start | bytes 1376260
  260.1 34.3 %copy-start.27 = (bf16[2,128,1024]{2,1,0:T(8,128)(2,1)S(1)}, bf16[2,128,1024]{2,1,0:T(8,128)(2,1)}, u32[]{:S(2)}) copy-start(bf16[2,128,1024]{2,1,0:T(8,128)(2,1)} %copy-done.25) | copy-start | bytes 1572868
  266.2 30.8 %collective-permute-start.19 = (bf16[4,2,64,1024]{3,2,1,0:T(8,128)(2,1)S(1)}, bf16[4,2,64,1024]{3,2,1,0:T(8,128)(2,1)S(1)}, u32[]{:S(2)}, u32[]{:S(2)}) collective-permute-start(bf16[4,2,64,1024]{3,2,1,0:T(8,128)(2,1)S(1)} %get-tuple-element.26), channel_id=1, source_target_pairs={{0,32},{32,0},{64,96},{96,64},{1,33},{33,1},{65,97},{97,65},{2,34}... | collective-permute-start | bytes 3145736 | tf_op jit(solution)/shard_map/ppermute | solution.py:238
  266.3 15.6 %collective-permute-start.20 = (bf16[2,128,1024]{2,1,0:T(8,128)(2,1)S(1)}, bf16[2,128,1024]{2,1,0:T(8,128)(2,1)S(1)}, u32[]{:S(2)}, u32[]{:S(2)}) collective-permute-start(bf16[2,128,1024]{2,1,0:T(8,128)(2,1)S(1)} %get-tuple-element.27), channel_id=1, source_target_pairs={{0,1},{1,2},{2,3},{3,0},{4,5},{5,6},{6,7},{7,4},{8,9},{9,10},{10,1... | collective-permute-start | bytes 1572872 | tf_op jit(solution)/shard_map/ppermute | solution.py:234
  267.9 26.5 %collective-permute-start.21 = (bf16[2,128,1024]{2,1,0:T(8,128)(2,1)S(1)}, bf16[2,128,1024]{2,1,0:T(8,128)(2,1)S(1)}, u32[]{:S(2)}, u32[]{:S(2)}) collective-permute-start(bf16[2,128,1024]{2,1,0:T(8,128)(2,1)S(1)} %get-tuple-element.28), channel_id=1, source_target_pairs={{0,2},{1,3},{2,0},{3,1},{4,6},{5,7},{6,4},{7,5},{8,10},{9,11},{10,... | collective-permute-start | bytes 1572872 | tf_op jit(solution)/shard_map/ppermute | solution.py:234
  270.9 23.5 %collective-permute-start.22 = (bf16[2,128,1024]{2,1,0:T(8,128)(2,1)S(1)}, bf16[2,128,1024]{2,1,0:T(8,128)(2,1)S(1)}, u32[]{:S(2)}, u32[]{:S(2)}) collective-permute-start(bf16[2,128,1024]{2,1,0:T(8,128)(2,1)S(1)} %get-tuple-element.29), channel_id=1, source_target_pairs={{0,3},{1,0},{2,1},{3,2},{4,7},{5,4},{6,5},{7,6},{8,11},{9,8},{10,9... | collective-permute-start | bytes 1572872 | tf_op jit(solution)/shard_map/ppermute | solution.py:234
  294.6 17.3 %copy-start.28 = (bf16[128,1024]{1,0:T(8,128)(2,1)}, bf16[128,1024]{1,0:T(8,128)(2,1)S(1)}, u32[]{:S(2)}) copy-start(bf16[128,1024]{1,0:T(8,128)(2,1)S(1)} %get-tuple-element.30.refs_2_.near) | copy-start | bytes 786436
  294.6 17.3 %collective-permute-start.26 = (bf16[128,1024]{1,0:T(8,128)(2,1)S(1)}, bf16[128,1024]{1,0:T(8,128)(2,1)S(1)}, u32[]{:S(2)}, u32[]{:S(2)}) collective-permute-start(bf16[128,1024]{1,0:T(8,128)(2,1)S(1)} %get-tuple-element.35), channel_id=1, source_target_pairs={{0,64},{32,96},{64,0},{96,32},{1,65},{33,97},{65,1},{97,33},{2,66}... | collective-permute-start | bytes 786440 | tf_op jit(solution)/shard_map/ppermute | solution.py:242
  297.3 17.2 %collective-permute-start.23 = (bf16[2,64,1024]{2,1,0:T(8,128)(2,1)S(1)}, bf16[2,64,1024]{2,1,0:T(8,128)(2,1)S(1)}, u32[]{:S(2)}, u32[]{:S(2)}) collective-permute-start(bf16[2,64,1024]{2,1,0:T(8,128)(2,1)S(1)} %get-tuple-element.32), channel_id=1, source_target_pairs={{0,1},{1,2},{2,3},{3,0},{4,5},{5,6},{6,7},{7,4},{8,9},{9,10},{10,1... | collective-permute-start | bytes 786440 | tf_op jit(solution)/shard_map/ppermute | solution.py:234
  298.5 16.0 %collective-permute-start.24 = (bf16[2,64,1024]{2,1,0:T(8,128)(2,1)S(1)}, bf16[2,64,1024]{2,1,0:T(8,128)(2,1)S(1)}, u32[]{:S(2)}, u32[]{:S(2)}) collective-permute-start(bf16[2,64,1024]{2,1,0:T(8,128)(2,1)S(1)} %get-tuple-element.33), channel_id=1, source_target_pairs={{0,2},{1,3},{2,0},{3,1},{4,6},{5,7},{6,4},{7,5},{8,10},{9,11},{10,... | collective-permute-start | bytes 786440 | tf_op jit(solution)/shard_map/ppermute | solution.py:234
  300.9 13.6 %collective-permute-start.25 = (bf16[2,64,1024]{2,1,0:T(8,128)(2,1)S(1)}, bf16[2,64,1024]{2,1,0:T(8,128)(2,1)S(1)}, u32[]{:S(2)}, u32[]{:S(2)}) collective-permute-start(bf16[2,64,1024]{2,1,0:T(8,128)(2,1)S(1)} %get-tuple-element.34), channel_id=1, source_target_pairs={{0,3},{1,0},{2,1},{3,2},{4,7},{5,4},{6,5},{7,6},{8,11},{9,8},{10,9... | collective-permute-start | bytes 786440 | tf_op jit(solution)/shard_map/ppermute | solution.py:234
  316.3 6.5 %collective-permute-start.27 = (bf16[64,1024]{1,0:T(8,128)(2,1)S(1)}, bf16[64,1024]{1,0:T(8,128)(2,1)S(1)}, u32[]{:S(2)}, u32[]{:S(2)}) collective-permute-start(bf16[64,1024]{1,0:T(8,128)(2,1)S(1)} %get-tuple-element.37), channel_id=1, source_target_pairs={{0,64},{32,96},{64,0},{96,32},{1,65},{33,97},{65,1},{97,33},{2,66}... | collective-permute-start | bytes 393224 | tf_op jit(solution)/shard_map/ppermute | solution.py:242
  (17 other events, 15.1 us)
Sparse Core Ops, SparseCore 0:
  88.4 41.3 all-gather.1

commit v3 on v2

v3 whole, which is shorter than its diff:
```python
import functools

import jax
import jax.numpy as jnp
from jax import lax
from jax.experimental import pallas as pl
from jax.experimental.pallas import tpu as pltpu
from jax.sharding import PartitionSpec as P

BLOCK = 192
PARTS = ((0,96),(96,96))
MIB = 1024 * 1024
ANY = pl.BlockSpec(memory_space=pl.ANY)

PIECES = (
    ((0, 0, 0), (0, 0, 1)),
    ((3, 0, 0), (3, 0, 1)),
    ((1, 0, 0), (1, 0, 1)),
    ((0, 1, 0), (0, 1, 1)),
    ((2, 0, 0), (3, 1, 0)),
    ((2, 0, 1), (1, 1, 0)),
    ((1, 1, 1), (3, 1, 1)),
    ((2, 1, 0),),
    ((2, 1, 1),),
)


def source_of(shift, flip):
    col = lax.axis_index("col")
    x = lax.rem(col // 2 + shift, 4)
    z = lax.rem(col + flip, 2)
    return x, z


def grad_input_kernel(n, wanted, split, *refs):
    count = len(wanted)
    chunks, w_hbm = refs[:count], refs[count]
    keep, sends = refs[-7 - split], refs[-6 - split:-6]
    w, g, o, w_sem, g_sem, o_sem = refs[-6:]
    row, y = lax.axis_index("row"), lax.axis_index("depth")
    w_copy = pltpu.make_async_copy(w_hbm, w, w_sem)
    w_copy.start()
    copies, at, places = [], 0, []
    for ref, index in zip(chunks, wanted):
        rows = n * len(PIECES[index])
        copy = pltpu.make_async_copy(ref, g.at[pl.ds(at, rows)], g_sem.at[len(copies)])
        copy.start()
        copies.append((copy, at + rows))
        places += [(at + n * i, p) for i, p in enumerate(PIECES[index])]
        at += rows
    w_copy.wait()
    waited, done, outs = 0, 0, []
    group = 4
    for first in range(0, len(places), group):
        inside = places[first:first + group]
        low, high = inside[0][0], inside[-1][0] + n
        while waited < len(copies) and (waited == 0 or copies[waited - 1][1] < high):
            copies[waited][0].wait()
            waited += 1
        o[low:high, :] = jnp.dot(g[low:high, :], w[...], preferred_element_type=jnp.float32).astype(jnp.bfloat16)
        for start, (shift, flip, q) in inside:
            x, z = source_of(shift, flip)
            apart = lax.rem(x + row, 2)
            far = lax.rem(x // 2 + row // 2, 2)
            ahead = lax.rem(2 * z + q + 4 - y, 4)
            each = 4 // split
            targets = [(apart == 0, keep.at[ahead, far])]
            for k, ref in enumerate(sends):
                targets.append(((apart == 1) & (ahead // each == k), ref.at[lax.rem(ahead, each), far]))
            for here, ref in targets:
                copy = pltpu.make_async_copy(o.at[pl.ds(start, n)], ref, o_sem.at[done])
                outs.append((here, copy))
                pl.when(here)(copy.start)
            done += 1
    for here, copy in outs:
        pl.when(here)(copy.wait)


def grad_input_part(n, wanted, split, chunks, weight, into=(), after=()):
    ff, d = weight.shape
    rows = n * sum(len(PIECES[index]) for index in wanted)
    shapes = [jax.ShapeDtypeStruct((count, 2, n, d), jnp.bfloat16) for count in [4] + [4 // split] * split]
    args = [chunks[index] for index in wanted] + [weight, *after, *into]
    return pl.pallas_call(
        functools.partial(grad_input_kernel, n, wanted, split),
        out_shape=shapes,
        in_specs=[ANY] * len(args),
        out_specs=[ANY] * len(shapes),
        scratch_shapes=[
            pltpu.VMEM((ff, d), jnp.bfloat16),
            pltpu.VMEM((rows, ff), jnp.bfloat16),
            pltpu.VMEM((rows, d), jnp.bfloat16),
            pltpu.SemaphoreType.DMA,
            pltpu.SemaphoreType.DMA((len(wanted),)),
            pltpu.SemaphoreType.DMA((rows // n,)),
        ],
        input_output_aliases={len(args) - len(into) + i: i for i in range(len(into))},
        compiler_params=pltpu.CompilerParams(vmem_limit_bytes=20 * MIB),
        cost_estimate=pl.CostEstimate(
            flops=2 * rows * ff * d , bytes_accessed=rows * ff , transcendentals=0
        ),
    )(*args)


TILE = 256


def grad_weight_kernel(first, last, *refs):
    count = len(PIECES) * len(PARTS)
    chunks, acts_hbm, out = refs[:count], refs[count], refs[-7]
    acts, g, o, a_sem, g_sem, o_sem = refs[-6:]
    row = lax.axis_index("row")
    acts_copy = pltpu.make_async_copy(acts_hbm, acts, a_sem)
    acts_copy.start()
    copies = []
    for tile in range(first, last):
        at, of_tile = tile - first, []
        for part, (low, n) in enumerate(PARTS):
            for ref, pieces in zip(chunks[part * len(PIECES):], PIECES):
                for i, (shift, flip, q) in enumerate(pieces):
                    x, z = source_of(shift, flip)
                    block = lax.rem(x, 2) * 8 + (2 * z + q) * 2 + lax.rem(x // 2 + row // 2, 2)
                    of_tile.append(
                        pltpu.make_async_copy(
                            ref.at[pl.ds(n * i, n), pl.ds(TILE * tile, TILE)],
                            g.at[at, pl.ds(pl.multiple_of(block * BLOCK + low, 16), n), :],
                            g_sem.at[at * 16 * len(PARTS) + len(of_tile)],
                        )
                    )
                    of_tile[-1].start()
        copies.append(of_tile)
    acts_copy.wait()
    outs = []
    for tile in range(first, last):
        at = tile - first
        for copy in copies[at]:
            copy.wait()
        o[at] = lax.dot_general(
            g[at], acts[...], (((0,), (0,)), ((), ())), preferred_element_type=jnp.float32
        ).astype(jnp.bfloat16)
        outs.append(pltpu.make_async_copy(o.at[at], out.at[pl.ds(TILE * tile, TILE), :], o_sem.at[at]))
        outs[-1].start()
    for copy in outs:
        copy.wait()


def grad_weight_tiles(first, last, chunks, acts, into=None, after=()):
    ff, (tokens, d) = chunks[0].shape[-1], acts.shape
    tiles = last - first
    args = [*chunks, acts, *after] + ([] if into is None else [into])
    return pl.pallas_call(
        functools.partial(grad_weight_kernel, first, last),
        out_shape=jax.ShapeDtypeStruct((ff, d), jnp.bfloat16),
        in_specs=[ANY] * len(args),
        out_specs=ANY,
        scratch_shapes=[
            pltpu.VMEM((tokens, d), jnp.bfloat16),
            pltpu.VMEM((tiles, tokens, TILE), jnp.bfloat16),
            pltpu.VMEM((tiles, TILE, d), jnp.bfloat16),
            pltpu.SemaphoreType.DMA,
            pltpu.SemaphoreType.DMA((tiles * 16 * len(PARTS),)),
            pltpu.SemaphoreType.DMA((tiles,)),
        ],
        input_output_aliases={} if into is None else {len(args) - 1: 0},
        compiler_params=pltpu.CompilerParams(vmem_limit_bytes=24 * MIB),
        cost_estimate=pl.CostEstimate(
            flops=2 * tokens * TILE * tiles * d,
            bytes_accessed=2 * (tokens * TILE * tiles + tokens * d + TILE * tiles * d),
            transcendentals=0,
        ),
    )(*args)


def pack_kernel(places, count, *refs):
    out, sems = refs[-2:]
    copies = []
    for k, (index, start, rows, to) in enumerate(places):
        copies.append(pltpu.make_async_copy(refs[index].at[pl.ds(start, rows)], out.at[pl.ds(to, rows)], sems.at[k]))
        copies[-1].start()
    for copy in copies:
        copy.wait()


def pack(sources, after=()):
    args, places, to = [], [], 0
    for array, start, rows in sources:
        places.append((len(args), start, rows, to))
        args.append(array)
        to += rows
    shape = jax.ShapeDtypeStruct((to, args[0].shape[1]), args[0].dtype)
    return pl.pallas_call(
        functools.partial(pack_kernel, tuple(places), len(args)),
        out_shape=shape,
        in_specs=[ANY] * (len(args) + len(after)),
        out_specs=pl.BlockSpec(memory_space=pltpu.VMEM),
        scratch_shapes=[pltpu.SemaphoreType.DMA((len(places),))],
        cost_estimate=pl.CostEstimate(flops=0, bytes_accessed=4 * shape.size, transcendentals=0),
    )(*args, *after)


def along_x(value, shift):
    return lax.ppermute(value, "col", [(i, (i + 2 * shift) % 8) for i in range(8)])


def along_z(value):
    return lax.ppermute(value, "col", [(i, i ^ 1) for i in range(8)])


def along_y(value, shift):
    return lax.ppermute(value, "depth", [(i, (i + shift) % 4) for i in range(4)])


def other_core(value):
    return lax.ppermute(value, "row", [(i, i ^ 1) for i in range(4)])


def other_z_hi(value):
    return lax.ppermute(value, "row", [(i, i ^ 2) for i in range(4)])


def tie_kernel(*refs):
    pass


def tie(value, after):
    return pl.pallas_call(
        tie_kernel,
        out_shape=jax.ShapeDtypeStruct(value.shape, value.dtype),
        in_specs=[ANY] * (1 + len(after)),
        out_specs=ANY,
        input_output_aliases={0: 0},
        compiler_params=pltpu.CompilerParams(has_side_effects=True),
    )(value, *after)


def first_step(own):
    return along_x(own, 1), along_x(own, -1), along_z(own)


def second_sends(left, right, z, after=()):
    n = left.shape[0] // 2
    return (
        pack([(left, 0, n), (z, 0, n)], after),
        pack([(right, n, n), (z, 0, n)], after),
        pack([(right, n, n), (left, n, n)], after),
    )


def second_step(left, right, z):
    return along_x(left, 1), along_x(right, -1), along_z(z)


def third_sends(second, after=()):
    left2, right2, z2 = second
    n = left2.shape[0] // 2
    return pack([(left2, n, n)], after=(right2, *after)), pack([(z2, 0, n)], after=(right2, *after))


def third_step(left, right):
    return along_x(left, 1), along_x(right, -1)


def sum_kernel(groups, *refs):
    outs = refs[len(refs) - len(groups):]
    for out, terms in zip(outs, groups):
        total = None
        for index, at in terms:
            value = (refs[index][...] if at is None else refs[index][at]).astype(jnp.float32)
            total = value if total is None else total + value
        out[...] = total.astype(out.dtype)


def sums(inputs, groups, after=()):
    def shape_of(term):
        return inputs[term[0]].shape if term[1] is None else inputs[term[0]].shape[1:]

    shapes = [jax.ShapeDtypeStruct(shape_of(g[0]), jnp.bfloat16) for g in groups]
    vmem = pl.BlockSpec(memory_space=pltpu.VMEM)
    return pl.pallas_call(
        functools.partial(sum_kernel, groups),
        out_shape=shapes,
        in_specs=[vmem] * len(inputs) + [ANY] * len(after),
        out_specs=[vmem] * len(groups),
        compiler_params=pltpu.CompilerParams(vmem_limit_bytes=16 * MIB),
    )(*inputs, *after)


def add_cores(keep, got, after=()):
    each = 4 // len(got)
    return sums((keep, *got), [((0, i), (1 + i // each, i % each)) for i in range(4)], after)


def send_y(q):
    return [along_y(q[i], i) for i in (1, 2, 3)]


def add_y(q, got, after=()):
    return sums((q[0], *got), [tuple((i, k) for i in range(4)) for k in range(2)], after)


def final_kernel(low, n, has_into, near, got, *refs):
    out, value, sem = refs[-3:]
    value[...] = (near[...].astype(jnp.float32) + got[...].astype(jnp.float32)).astype(value.dtype)
    copy = pltpu.make_async_copy(value, out.at[pl.ds(low, n), :], sem)
    copy.start()
    copy.wait()


def final(low, near, got, into=None, after=()):
    n, d = near.shape
    vmem = pl.BlockSpec(memory_space=pltpu.VMEM)
    args = [near, got, *after] + ([] if into is None else [into])
    return pl.pallas_call(
        functools.partial(final_kernel, low, n, into is not None),
        out_shape=jax.ShapeDtypeStruct((BLOCK, d), jnp.bfloat16),
        in_specs=[vmem] * 2 + [ANY] * (len(args) - 2),
        out_specs=ANY,
        scratch_shapes=[pltpu.VMEM((n, d), jnp.bfloat16), pltpu.SemaphoreType.DMA],
        input_output_aliases={} if into is None else {len(args) - 1: 0},
    )(*args)


ALL = tuple(range(len(PIECES)))
EARLY, LATE = ALL[:7], ALL[7:]
SAME_CHIP = [[0, 1], [2, 3]]


def shards(activations, grad_output, weight):
    ff = grad_output.shape[1]
    tiles, d = ff // TILE, weight.shape[1]
    (low0, n0), (low1, n1) = PARTS

    own0 = pack([(grad_output, low0, n0), (grad_output, BLOCK + low0, n0)])
    first0 = first_step(own0)
    far = other_z_hi(activations)
    pair = pack([(activations, 0, BLOCK), (far, 0, BLOCK)], after=first0)
    acts = lax.all_gather(pair, "depth", axis=0, tiled=True)
    sends = second_sends(*first0)
    second0 = second_step(*sends)
    own1 = pack([(grad_output, low1, n1), (grad_output, BLOCK + low1, n1)], after=sends)
    first1 = first_step(own1)
    sends = third_sends(second0)
    third0 = third_step(*sends)
    chunks0 = [own0, *first0, *second0, *third0]

    part0 = grad_input_part(n0, EARLY, 2, chunks0, weight, after=(own1, *sends))
    keep0, *send0 = grad_input_part(n0, LATE, 2, chunks0, weight, into=part0)
    cores0 = [other_core(v) for v in send0]
    second1 = second_step(*second_sends(*first1, after=(keep0,)))
    q0 = add_cores(keep0, cores0)
    y0 = send_y(q0)
    sends = third_sends(second1, after=(q0[0],))
    third1 = third_step(*sends)
    chunks1 = [own1, *first1, *second1, *third1]
    acts = tie(acts, sends)
    part1 = grad_input_part(n1, EARLY, 2, chunks1, weight, after=(q0[0], acts))
    acts = lax.all_gather(acts, "row", axis=0, tiled=True, axis_index_groups=SAME_CHIP)
    near0 = add_y(q0, y0, after=(part1[0],))
    far0 = other_z_hi(near0[1])
    keep1, *send1 = grad_input_part(n1, LATE, 2, chunks1, weight, into=part1, after=(near0[0],))
    cores1 = [other_core(v) for v in send1]
    chunks = chunks0 + chunks1
    weight_grad = grad_weight_tiles(0, 1, chunks, acts, after=(keep1,))
    q1 = add_cores(keep1, cores1, after=(weight_grad,))
    y1 = send_y(q1)
    weight_grad = grad_weight_tiles(1, 6, chunks, acts, into=weight_grad, after=(q1[0],))
    result = final(low0, near0[0], far0, after=(weight_grad,))
    near1 = add_y(q1, y1, after=(result,))
    far1 = other_z_hi(near1[1])
    weight_grad = grad_weight_tiles(6, tiles, chunks, acts, into=weight_grad, after=(near1[0],))
    result = final(low1, near1[0], far1, into=result, after=(weight_grad,))
    return result, weight_grad


def solution(mesh):
    in_specs = (P(("row", "depth"), "col"), P("col", ("row", "depth")), P(("row", "depth"), "col"))
    out_specs = (P(("row", "depth"), "col"), P(("row", "depth"), "col"))
    return jax.shard_map(shards, mesh=mesh, in_specs=in_specs, out_specs=out_specs, check_vma=False)
```

time: 333 us -> 228 us (0.68)
  Pallas kernels: 184 us -> 82.3 us
  waiting for transfers between devices: 65 us -> 46.8 us
  local copies, waits for them, and re-layouts: 25.8 us -> 43.9 us
    pallas_call x8 -> x13, Pallas kernels: 128 us -> 24.9 us  [pack(): pl.pallas_call(functools.partial(pack_kernel, tuple(places), len(args)),...]
    unnamed x72 -> x116, local copies, waits for them, and re-layouts: 22.7 us -> 43.9 us
    ppermute x6, waiting for transfers between devices: 22.3 us -> 3.21 us  [along_y(): lax.ppermute(value, 'depth', [(i, (i + shift) % 4) for i in range(4)])]
    ppermute x12, waiting for transfers between devices: 25.9 us -> 18.7 us  [along_x(): lax.ppermute(value, 'col', [(i, (i + 2 * shift) % 8) for i in range(8)])]
    ppermute x3, waiting for transfers between devices: 14.6 us -> 21.8 us  [other_z_hi(): return lax.ppermute(value, 'row', [(i, i ^ 2) for i in range(4)])]
    pallas_call x4, Pallas kernels: 2.81 us -> 7.28 us  [sums(): pl.pallas_call(functools.partial(sum_kernel, groups), out_shape=shapes, i...]
    pallas_call x6 -> x7, Pallas kernels: 50 us -> 46.5 us  [the longest x4 23.7 us: grad_input_part(): pl.pallas_call(functools.partial(grad_input_kernel, n, wanted, split), ou...]
  transfers between devices with their start and end apart: 29 -> 31, of which waited for: 9 -> 9; matrix products, arithmetic and copies ran while one was open for 2% -> 0% of each run, Pallas kernels for 33% -> 33%
where the time goes in v3:
time: 228 us; the launch traced here: 226 us
  Pallas kernels  82.3 us (36%)
  waiting for transfers between devices  46.8 us (21%)
  local copies, waits for them, and re-layouts  43.9 us (19%)
  starting transfers between devices  38.6 us (17%)
  between operations  14.7 us (6%)
    unnamed x116, local copies, waits for them, and re-layouts  43.9 us
    pallas_call x13, Pallas kernels, pack(): pl.pallas_call(functools.partial(pack_kernel, tuple(places), len(args)),...  24.9 us
    pallas_call x4, Pallas kernels, grad_input_part(): pl.pallas_call(functools.partial(grad_input_kernel, n, wanted, split), ou...  23.7 us
    pallas_call x3, Pallas kernels, grad_weight_tiles(): pl.pallas_call(functools.partial(grad_weight_kernel, first, last), out_sh...  22.8 us
    ppermute x3, waiting for transfers between devices, other_z_hi(): return lax.ppermute(value, 'row', [(i, i ^ 2) for i in range(4)])  21.8 us
    ppermute x12, waiting for transfers between devices, along_x(): lax.ppermute(value, 'col', [(i, (i + 2 * shift) % 8) for i in range(8)])  18.7 us
    ppermute x12, starting transfers between devices, along_x(): lax.ppermute(value, 'col', [(i, (i + 2 * shift) % 8) for i in range(8)])  17.5 us
    ppermute x6, starting transfers between devices, along_y(): lax.ppermute(value, 'depth', [(i, (i + shift) % 4) for i in range(4)])  9.1 us
  transfers between devices with their start and end apart: 31, of which 9 were waited for; matrix products, arithmetic and copies ran while one was open for 0% of the time, Pallas kernels for 33%

profile of v3, /device:TPU:0, one launch (start us, length us, event | category | flops | bytes accessed | tf_op | source)
XLA Modules:
  0.0 226.2 jit_solution(5031730683498810584)
XLA Ops:
  7.2 2.0 shard_map.50.refs_0_
  9.2 1.6 collective-permute-start
  10.9 1.9 collective-permute-start.1
  12.8 1.7 collective-permute-start.2
  14.5 3.6 %collective-permute-start.21 = (bf16[192,1024]{1,0:T(8,128)(2,1)S(1)}, bf16[192,1024]{1,0:T(8,128)(2,1)S(1)}, u32[]{:S(2)}, u32[]{:S(2)}) collective-permute-start(bf16[192,1024]{1,0:T(8,128)(2,1)S(1)} %copy-done.56), channel_id=1, source_target_pairs={{0,64},{32,96},{64,0},{96,32},{1,65},{33,97},{65,1},{97,33},{2,66}... | collective-permute-start | bytes 1179656 | tf_op jit(solution)/shard_map/ppermute | solution.py:218
  18.1 21.8 %collective-permute-done.21.refs_1_ = bf16[192,1024]{1,0:T(8,128)(2,1)S(1)} collective-permute-done((bf16[192,1024]{1,0:T(8,128)(2,1)S(1)}, bf16[192,1024]{1,0:T(8,128)(2,1)S(1)}, u32[]{:S(2)}, u32[]{:S(2)}) %collective-permute-start.21) | collective-permute-done | bytes 393248 | tf_op jit(solution)/shard_map/ppermute | solution.py:218
  42.0 2.0 shard_map.65
  44.1 2.0 shard_map.51.refs_2_
  47.6 2.0 shard_map.52.refs_3_
  49.6 1.8 collective-permute-start.6
  51.4 2.0 shard_map.53.refs_4_
  53.5 2.2 shard_map.54.refs_8_.refs_0_.refs_9_
  56.0 1.8 collective-permute-start.4
  57.8 8.1 %collective-permute-done.5.refs_0_.refs_4_ = bf16[192,1792]{1,0:T(8,128)(2,1)S(1)} collective-permute-done((bf16[192,1792]{1,0:T(8,128)(2,1)}, bf16[192,1792]{1,0:T(8,128)(2,1)S(1)}, u32[]{:S(2)}, u32[]{:S(2)}) %collective-permute-start.5) | collective-permute-done | bytes 688160 | tf_op jit(solution)/shard_map/ppermute | solution.py:202
  68.3 1.7 shard_map.55.refs_9_
  70.1 1.6 collective-permute-start.7
  72.2 1.7 shard_map.56.refs_10_
  76.6 2.0 copy-done.15
  83.9 10.0 %shard_map.57 = (bf16[4,2,96,1024]{3,2,1,0:T(8,128)(2,1)S(1)}, bf16[2,2,96,1024]{3,2,1,0:T(8,128)(2,1)}, bf16[2,2,96,1024]{3,2,1,0:T(8,128)(2,1)}) custom-call(bf16[192,1792]{1,0:T(8,128)(2,1)S(1)} %copy-done.23, bf16[192,1792]{1,0:T(8,128)(2,1)S(1)} %copy-done.7, bf16[192,1792]{1,0:T(8,128)(2,1)S(1)} %copy-done.11, bf16[192,1792]{1,0:T(8,128)(2,1)S(1)} %copy-done.9, ...), custom_call_target="tpu_custom_call" | custom-call | flops 4932501504 | bytes 2408448 | tf_op jit(solution)/shard_map/pallas_call | solution.py:84
  94.0 2.0 shard_map.58
  97.6 2.0 shard_map.59
  100.3 2.0 shard_map.60
  102.3 2.7 %collective-permute-start.12 = (bf16[192,1792]{1,0:T(8,128)(2,1)}, bf16[192,1792]{1,0:T(8,128)(2,1)}, u32[]{:S(2)}, u32[]{:S(2)}) collective-permute-start(bf16[192,1792]{1,0:T(8,128)(2,1)} %shard_map.60), channel_id=1, source_target_pairs={{0,24},{4,28},{8,0},{12,4},{16,8},{20,12},{24,16},{28,20},{1,25},{... | collective-permute-start | bytes 2064392 | tf_op jit(solution)/shard_map/ppermute | solution.py:202
  104.9 1.9 shard_map.63
  107.0 2.5 %shard_map.61 = (bf16[2,96,1024]{2,1,0:T(8,128)(2,1)S(1)}, bf16[2,96,1024]{2,1,0:T(8,128)(2,1)}, bf16[2,96,1024]{2,1,0:T(8,128)(2,1)}, bf16[2,96,1024]{2,1,0:T(8,128)(2,1)}) custom-call(bf16[4,2,96,1024]{3,2,1,0:T(8,128)(2,1)S(1)} %copy-done.2, bf16[2,2,96,1024]{3,2,1,0:T(8,128)(2,1)} %collective-permute-done.13.refs_1_, ...), custom_call_target="tpu_custom_call" | custom-call | tf_op jit(solution)/shard_map/pallas_call | solution.py:279
  110.3 8.3 %collective-permute-done.10.refs_0_.refs_4_.refs_13_ = bf16[192,1792]{1,0:T(8,128)(2,1)} collective-permute-done((bf16[192,1792]{1,0:T(8,128)(2,1)}, bf16[192,1792]{1,0:T(8,128)(2,1)}, u32[]{:S(2)}, u32[]{:S(2)}) %collective-permute-start.10) | collective-permute-done | bytes 688160 | tf_op jit(solution)/shard_map/ppermute | solution.py:202
  119.8 1.7 shard_map.62.refs_1_
  121.6 2.5 %collective-permute-done.16.refs_0_.refs_6_.refs_15_ = bf16[192,1792]{1,0:T(8,128)(2,1)} collective-permute-done((bf16[192,1792]{1,0:T(8,128)(2,1)}, bf16[192,1792]{1,0:T(8,128)(2,1)}, u32[]{:S(2)}, u32[]{:S(2)}) %collective-permute-start.16) | collective-permute-done | bytes 688160 | tf_op jit(solution)/shard_map/ppermute | solution.py:206
  124.1 1.7 shard_map.64.refs_2_
  125.9 3.2 %collective-permute-start.17 = (bf16[96,1792]{1,0:T(8,128)(2,1)}, bf16[96,1792]{1,0:T(8,128)(2,1)S(1)}, u32[]{:S(2)}, u32[]{:S(2)}) collective-permute-start(bf16[96,1792]{1,0:T(8,128)(2,1)} %shard_map.64.refs_2_), channel_id=1, source_target_pairs={{0,24},{4,28},{8,0},{12,4},{16,8},{20,12},{24,16},{28,20},{1,25},{... | collective-permute-start | bytes 1032200 | tf_op jit(solution)/shard_map/ppermute | solution.py:202
  129.2 1.6 collective-permute-start.18
  130.8 2.9 %collective-permute-start.19 = (bf16[2,96,1024]{2,1,0:T(8,128)(2,1)}, bf16[2,96,1024]{2,1,0:T(8,128)(2,1)S(1)}, u32[]{:S(2)}, u32[]{:S(2)}) collective-permute-start(bf16[2,96,1024]{2,1,0:T(8,128)(2,1)} %get-tuple-element.34), channel_id=1, source_target_pairs={{0,2},{1,3},{2,0},{3,1},{4,6},{5,7},{6,4},{7,5},{8,10},{9,11},{10,... | collective-permute-start | bytes 1179656 | tf_op jit(solution)/shard_map/ppermute | solution.py:210
  135.0 2.7 %copy-done.17 = bf16[1792,1024]{1,0:T(8,128)(2,1)S(1)} copy-done((bf16[1792,1024]{1,0:T(8,128)(2,1)S(1)}, bf16[1792,1024]{1,0:T(8,128)(2,1)}, u32[]{:S(2)}) %copy-start.17) | copy-done | bytes 3670040
  137.7 2.7 %copy-done.18 = bf16[1536,1024]{1,0:T(8,128)(2,1)S(1)} copy-done((bf16[1536,1024]{1,0:T(8,128)(2,1)S(1)}, bf16[1536,1024]{1,0:T(8,128)(2,1)}, u32[]{:S(2)}) %copy-start.18) | copy-done | bytes 3145752
  141.6 9.8 %shard_map.67 = (bf16[4,2,96,1024]{3,2,1,0:T(8,128)(2,1)S(1)}, bf16[2,2,96,1024]{3,2,1,0:T(8,128)(2,1)}, bf16[2,2,96,1024]{3,2,1,0:T(8,128)(2,1)}) custom-call(bf16[192,1792]{1,0:T(8,128)(2,1)S(1)} %copy-done.32, bf16[192,1792]{1,0:T(8,128)(2,1)} %collective-permute-done.3.refs_0_.refs_1_.refs_10_, ...), custom_call_target="tpu_custom_call" | custom-call | flops 4932501504 | bytes 2408448 | tf_op jit(solution)/shard_map/pallas_call | solution.py:84
  152.3 2.0 shard_map.69
  154.9 2.8 %copy-done.3 = bf16[3072,1024]{1,0:T(8,128)(2,1)S(1)} copy-done((bf16[3072,1024]{1,0:T(8,128)(2,1)S(1)}, bf16[3072,1024]{1,0:T(8,128)(2,1)}, u32[]{:S(2)}) %copy-start.3) | copy-done | bytes 6291480
  166.1 4.9 %shard_map.70.refs_3_.refs_20_ = bf16[1792,1024]{1,0:T(8,128)(2,1)} custom-call(bf16[192,1792]{1,0:T(8,128)(2,1)S(1)} %copy-done.24, bf16[192,1792]{1,0:T(8,128)(2,1)S(1)} %copy-done.7, bf16[192,1792]{1,0:T(8,128)(2,1)S(1)} %copy-done.12, bf16[192,1792]{1,0:T(8,128)(2,1)S(1)} %copy-done.9, bf16[192,1792]{1,0:T(8,128)(2,1)S(1)} %copy-done.28, ...), custom_call_target="tpu_custom_call" | custom-call | flops 1610612736 | bytes 8388608 | tf_op jit(solution)/shard_map/pallas_call | solution.py:151
  171.0 2.0 copy-done
  173.0 2.6 %shard_map.71 = (bf16[2,96,1024]{2,1,0:T(8,128)(2,1)S(1)}, bf16[2,96,1024]{2,1,0:T(8,128)(2,1)}, bf16[2,96,1024]{2,1,0:T(8,128)(2,1)}, bf16[2,96,1024]{2,1,0:T(8,128)(2,1)}) custom-call(bf16[4,2,96,1024]{3,2,1,0:T(8,128)(2,1)S(1)} %get-tuple-element.40.refs_19_.refs_0_, bf16[2,2,96,1024]{3,2,1,0:T(8,128)(2,1)} %collective-permute-done.22.refs_1_, ...), custom_call_target="tpu_custom_call" | custom-call | tf_op jit(solution)/shard_map/pallas_call | solution.py:279
  177.0 1.9 collective-permute-start.26
  178.9 13.3 %shard_map.72.refs_0_.refs_20_ = bf16[1792,1024]{1,0:T(8,128)(2,1)} custom-call(bf16[192,1792]{1,0:T(8,128)(2,1)S(1)} %copy-done.24, bf16[192,1792]{1,0:T(8,128)(2,1)S(1)} %copy-done.7, bf16[192,1792]{1,0:T(8,128)(2,1)S(1)} %copy-done.13, bf16[192,1792]{1,0:T(8,128)(2,1)S(1)} %copy-done.9, ...), custom_call_target="tpu_custom_call", output_to_operand_aliasing={{}: (20, {})} | custom-call | flops 8053063680 | bytes 16777216 | tf_op jit(solution)/shard_map/pallas_call | solution.py:151
  192.2 1.9 shard_map.73.refs_4_.refs_1_
  194.1 2.6 %collective-permute-done.24.refs_1_ = bf16[2,96,1024]{2,1,0:T(8,128)(2,1)} collective-permute-done((bf16[2,96,1024]{2,1,0:T(8,128)(2,1)}, bf16[2,96,1024]{2,1,0:T(8,128)(2,1)}, u32[]{:S(2)}, u32[]{:S(2)}) %collective-permute-start.24) | collective-permute-done | bytes 393248 | tf_op jit(solution)/shard_map/ppermute | solution.py:210
  200.7 3.3 %collective-permute-start.28 = (bf16[96,1024]{1,0:T(8,128)(2,1)S(1)}, bf16[96,1024]{1,0:T(8,128)(2,1)}, u32[]{:S(2)}, u32[]{:S(2)}) collective-permute-start(bf16[96,1024]{1,0:T(8,128)(2,1)S(1)} %get-tuple-element.49), channel_id=1, source_target_pairs={{0,64},{32,96},{64,0},{96,32},{1,65},{33,97},{65,1},{97,33},{2,66}... | collective-permute-start | bytes 589832 | tf_op jit(solution)/shard_map/ppermute | solution.py:218
  204.1 2.8 %copy-done.5 = bf16[3072,1024]{1,0:T(8,128)(2,1)S(1)} copy-done((bf16[3072,1024]{1,0:T(8,128)(2,1)S(1)}, bf16[3072,1024]{1,0:T(8,128)(2,1)}, u32[]{:S(2)}) %copy-start.5) | copy-done | bytes 6291480
  213.0 4.6 %shard_map.75.refs_0_ = bf16[1792,1024]{1,0:T(8,128)(2,1)} custom-call(bf16[192,1792]{1,0:T(8,128)(2,1)S(1)} %copy-done.25, bf16[192,1792]{1,0:T(8,128)(2,1)S(1)} %copy-done.7, bf16[192,1792]{1,0:T(8,128)(2,1)S(1)} %copy-done.14, bf16[192,1792]{1,0:T(8,128)(2,1)S(1)} %copy-done.9, bf16[192,1792]{1,0:T(8,128)(2,1)S(1)} %copy-done.30, ...), custom_call_target="tpu_custom_call", output_to_operand_aliasing={{}: (20, {})} | custom-call | flops 1610612736 | bytes 8388608 | tf_op jit(solution)/shard_map/pallas_call | solution.py:151
  217.6 1.8 shard_map.76
  (159 shorter events, 43.6 us)
Async XLA Ops:
  7.2 7.4 %copy-start.56 = (bf16[192,1024]{1,0:T(8,128)(2,1)S(1)}, bf16[192,1024]{1,0:T(8,128)(2,1)}, u32[]{:S(2)}) copy-start(bf16[192,1024]{1,0:T(8,128)(2,1)} %refs_0_.5) | copy-start | bytes 1179652
  7.2 118.6 %all-gather.3.cloned.1.call-start = ((), (), s32[]{:S(2)}) async-start(), calls=%async_computation | async-start | bytes 3932160 | tf_op jit(solution)/shard_map/all_gather | solution.py:337
  9.2 30.7 %collective-permute-start = (bf16[192,1792]{1,0:T(8,128)(2,1)}, bf16[192,1792]{1,0:T(8,128)(2,1)S(1)}, u32[]{:S(2)}, u32[]{:S(2)}) collective-permute-start(bf16[192,1792]{1,0:T(8,128)(2,1)} %shard_map.50.refs_0_), channel_id=1, source_target_pairs={{0,8},{4,12},{8,16},{12,20},{16,24},{20,28},{24,0},{28,4},{1,9},{5... | collective-permute-start | bytes 2064392 | tf_op jit(solution)/shard_map/ppermute | solution.py:202
  10.9 29.0 %collective-permute-start.1 = (bf16[192,1792]{1,0:T(8,128)(2,1)}, bf16[192,1792]{1,0:T(8,128)(2,1)S(1)}, u32[]{:S(2)}, u32[]{:S(2)}) collective-permute-start(bf16[192,1792]{1,0:T(8,128)(2,1)} %shard_map.50.refs_0_), channel_id=1, source_target_pairs={{0,4},{4,0},{8,12},{12,8},{16,20},{20,16},{24,28},{28,24},{1,5},{5... | collective-permute-start | bytes 2064392 | tf_op jit(solution)/shard_map/ppermute | solution.py:206
  12.8 27.1 %collective-permute-start.2 = (bf16[192,1792]{1,0:T(8,128)(2,1)}, bf16[192,1792]{1,0:T(8,128)(2,1)S(1)}, u32[]{:S(2)}, u32[]{:S(2)}) collective-permute-start(bf16[192,1792]{1,0:T(8,128)(2,1)} %shard_map.50.refs_0_), channel_id=1, source_target_pairs={{0,24},{4,28},{8,0},{12,4},{16,8},{20,12},{24,16},{28,20},{1,25},{... | collective-permute-start | bytes 2064392 | tf_op jit(solution)/shard_map/ppermute | solution.py:202
  14.5 25.3 %collective-permute-start.21 = (bf16[192,1024]{1,0:T(8,128)(2,1)S(1)}, bf16[192,1024]{1,0:T(8,128)(2,1)S(1)}, u32[]{:S(2)}, u32[]{:S(2)}) collective-permute-start(bf16[192,1024]{1,0:T(8,128)(2,1)S(1)} %copy-done.56), channel_id=1, source_target_pairs={{0,64},{32,96},{64,0},{96,32},{1,65},{33,97},{65,1},{97,33},{2,66}... | collective-permute-start | bytes 1179656 | tf_op jit(solution)/shard_map/ppermute | solution.py:218
  44.0 110.8 %all-gather.5.cloned.1.call-start = ((), (), s32[]{:S(2)}) async-start(), calls=%async_computation.1 | async-start | bytes 9437184 | tf_op jit(solution)/shard_map/all_gather | solution.py:357
  46.0 19.9 %collective-permute-start.5 = (bf16[192,1792]{1,0:T(8,128)(2,1)}, bf16[192,1792]{1,0:T(8,128)(2,1)S(1)}, u32[]{:S(2)}, u32[]{:S(2)}) collective-permute-start(bf16[192,1792]{1,0:T(8,128)(2,1)} %shard_map.51.refs_2_), channel_id=1, source_target_pairs={{0,8},{4,12},{8,16},{12,20},{16,24},{20,28},{24,0},{28,4},{1,9},{5... | collective-permute-start | bytes 2064392 | tf_op jit(solution)/shard_map/ppermute | solution.py:202
  49.6 17.9 %collective-permute-start.6 = (bf16[192,1792]{1,0:T(8,128)(2,1)}, bf16[192,1792]{1,0:T(8,128)(2,1)S(1)}, u32[]{:S(2)}, u32[]{:S(2)}) collective-permute-start(bf16[192,1792]{1,0:T(8,128)(2,1)} %shard_map.52.refs_3_), channel_id=1, source_target_pairs={{0,24},{4,28},{8,0},{12,4},{16,8},{20,12},{24,16},{28,20},{1,25},{... | collective-permute-start | bytes 2064392 | tf_op jit(solution)/shard_map/ppermute | solution.py:202
  53.4 22.1 %copy-start.7 = (bf16[192,1792]{1,0:T(8,128)(2,1)S(1)}, bf16[192,1792]{1,0:T(8,128)(2,1)}, u32[]{:S(2)}) copy-start(bf16[192,1792]{1,0:T(8,128)(2,1)} %copy-done.6) | copy-start | bytes 2064388
  53.4 22.1 %copy-start.9 = (bf16[192,1792]{1,0:T(8,128)(2,1)S(1)}, bf16[192,1792]{1,0:T(8,128)(2,1)}, u32[]{:S(2)}) copy-start(bf16[192,1792]{1,0:T(8,128)(2,1)} %copy-done.8) | copy-start | bytes 2064388
  53.4 22.1 %copy-start.23 = (bf16[192,1792]{1,0:T(8,128)(2,1)S(1)}, bf16[192,1792]{1,0:T(8,128)(2,1)}, u32[]{:S(2)}) copy-start(bf16[192,1792]{1,0:T(8,128)(2,1)} %shard_map.50.refs_0_) | copy-start | bytes 2064388
  53.4 18.8 %collective-permute-start.8 = (bf16[192,1792]{1,0:T(8,128)(2,1)}, bf16[192,1792]{1,0:T(8,128)(2,1)}, u32[]{:S(2)}, u32[]{:S(2)}) collective-permute-start(bf16[192,1792]{1,0:T(8,128)(2,1)} %shard_map.53.refs_4_), channel_id=1, source_target_pairs={{0,4},{4,0},{8,12},{12,8},{16,20},{20,16},{24,28},{28,24},{1,5},{5... | collective-permute-start | bytes 2064392 | tf_op jit(solution)/shard_map/ppermute | solution.py:206
  55.7 41.9 %collective-permute-start.3 = (bf16[192,1792]{1,0:T(8,128)(2,1)}, bf16[192,1792]{1,0:T(8,128)(2,1)}, u32[]{:S(2)}, u32[]{:S(2)}) collective-permute-start(bf16[192,1792]{1,0:T(8,128)(2,1)} %shard_map.54.refs_8_.refs_0_.refs_9_), channel_id=1, source_target_pairs={{0,8},{4,12},{8,16},{12,20},{16,24},{20,28},{24,0},{28,4},{1,9},{5... | collective-permute-start | bytes 2064392 | tf_op jit(solution)/shard_map/ppermute | solution.py:202
  56.0 41.6 %collective-permute-start.4 = (bf16[192,1792]{1,0:T(8,128)(2,1)}, bf16[192,1792]{1,0:T(8,128)(2,1)}, u32[]{:S(2)}, u32[]{:S(2)}) collective-permute-start(bf16[192,1792]{1,0:T(8,128)(2,1)} %shard_map.54.refs_8_.refs_0_.refs_9_), channel_id=1, source_target_pairs={{0,4},{4,0},{8,12},{12,8},{16,20},{20,16},{24,28},{28,24},{1,5},{5... | collective-permute-start | bytes 2064392 | tf_op jit(solution)/shard_map/ppermute | solution.py:206
  65.9 34.4 %collective-permute-start.11 = (bf16[192,1792]{1,0:T(8,128)(2,1)}, bf16[192,1792]{1,0:T(8,128)(2,1)}, u32[]{:S(2)}, u32[]{:S(2)}) collective-permute-start(bf16[192,1792]{1,0:T(8,128)(2,1)} %shard_map.54.refs_8_.refs_0_.refs_9_), channel_id=1, source_target_pairs={{0,24},{4,28},{8,0},{12,4},{16,8},{20,12},{24,16},{28,20},{1,25},{... | collective-permute-start | bytes 2064392 | tf_op jit(solution)/shard_map/ppermute | solution.py:202
  70.1 23.8 %collective-permute-start.7 = (bf16[96,1792]{1,0:T(8,128)(2,1)}, bf16[96,1792]{1,0:T(8,128)(2,1)S(1)}, u32[]{:S(2)}, u32[]{:S(2)}) collective-permute-start(bf16[96,1792]{1,0:T(8,128)(2,1)} %shard_map.55.refs_9_), channel_id=1, source_target_pairs={{0,8},{4,12},{8,16},{12,20},{16,24},{20,28},{24,0},{28,4},{1,9},{5... | collective-permute-start | bytes 1032200 | tf_op jit(solution)/shard_map/ppermute | solution.py:202
  73.9 20.0 %collective-permute-start.9 = (bf16[96,1792]{1,0:T(8,128)(2,1)}, bf16[96,1792]{1,0:T(8,128)(2,1)S(1)}, u32[]{:S(2)}, u32[]{:S(2)}) collective-permute-start(bf16[96,1792]{1,0:T(8,128)(2,1)} %shard_map.56.refs_10_), channel_id=1, source_target_pairs={{0,24},{4,28},{8,0},{12,4},{16,8},{20,12},{24,16},{28,20},{1,25},{... | collective-permute-start | bytes 1032200 | tf_op jit(solution)/shard_map/ppermute | solution.py:202
  83.9 10.0 %copy-start.16 = (bf16[1792,1024]{1,0:T(8,128)(2,1)S(1)}, bf16[1792,1024]{1,0:T(8,128)(2,1)}, u32[]{:S(2)}) copy-start(bf16[1792,1024]{1,0:T(8,128)(2,1)} %refs_2_.3) | copy-start | bytes 11010052
  97.1 9.9 %collective-permute-start.13 = (bf16[2,2,96,1024]{3,2,1,0:T(8,128)(2,1)}, bf16[2,2,96,1024]{3,2,1,0:T(8,128)(2,1)}, u32[]{:S(2)}, u32[]{:S(2)}) collective-permute-start(bf16[2,2,96,1024]{3,2,1,0:T(8,128)(2,1)} %get-tuple-element.30), channel_id=1, source_target_pairs={{0,32},{32,0},{64,96},{96,64},{1,33},{33,1},{65,97},{97,65},{2,34}... | collective-permute-start | bytes 2359304 | tf_op jit(solution)/shard_map/ppermute | solution.py:214
  97.1 9.9 %collective-permute-start.14 = (bf16[2,2,96,1024]{3,2,1,0:T(8,128)(2,1)}, bf16[2,2,96,1024]{3,2,1,0:T(8,128)(2,1)}, u32[]{:S(2)}, u32[]{:S(2)}) collective-permute-start(bf16[2,2,96,1024]{3,2,1,0:T(8,128)(2,1)} %get-tuple-element.31), channel_id=1, source_target_pairs={{0,32},{32,0},{64,96},{96,64},{1,33},{33,1},{65,97},{97,65},{2,34}... | collective-permute-start | bytes 2359304 | tf_op jit(solution)/shard_map/ppermute | solution.py:214
  99.6 7.4 %copy-start.2 = (bf16[4,2,96,1024]{3,2,1,0:T(8,128)(2,1)S(1)}, bf16[4,2,96,1024]{3,2,1,0:T(8,128)(2,1)}, u32[]{:S(2)}) copy-start(bf16[4,2,96,1024]{3,2,1,0:T(8,128)(2,1)} %copy-done.1) | copy-start | bytes 4718596
  99.6 18.9 %collective-permute-start.10 = (bf16[192,1792]{1,0:T(8,128)(2,1)}, bf16[192,1792]{1,0:T(8,128)(2,1)}, u32[]{:S(2)}, u32[]{:S(2)}) collective-permute-start(bf16[192,1792]{1,0:T(8,128)(2,1)} %shard_map.59), channel_id=1, source_target_pairs={{0,8},{4,12},{8,16},{12,20},{16,24},{20,28},{24,0},{28,4},{1,9},{5... | collective-permute-start | bytes 2064392 | tf_op jit(solution)/shard_map/ppermute | solution.py:202
  102.3 17.6 %collective-permute-start.12 = (bf16[192,1792]{1,0:T(8,128)(2,1)}, bf16[192,1792]{1,0:T(8,128)(2,1)}, u32[]{:S(2)}, u32[]{:S(2)}) collective-permute-start(bf16[192,1792]{1,0:T(8,128)(2,1)} %shard_map.60), channel_id=1, source_target_pairs={{0,24},{4,28},{8,0},{12,4},{16,8},{20,12},{24,16},{28,20},{1,25},{... | collective-permute-start | bytes 2064392 | tf_op jit(solution)/shard_map/ppermute | solution.py:202
  106.9 17.2 %collective-permute-start.16 = (bf16[192,1792]{1,0:T(8,128)(2,1)}, bf16[192,1792]{1,0:T(8,128)(2,1)}, u32[]{:S(2)}, u32[]{:S(2)}) collective-permute-start(bf16[192,1792]{1,0:T(8,128)(2,1)} %shard_map.63), channel_id=1, source_target_pairs={{0,4},{4,0},{8,12},{12,8},{16,20},{20,16},{24,28},{28,24},{1,5},{5... | collective-permute-start | bytes 2064392 | tf_op jit(solution)/shard_map/ppermute | solution.py:206
  125.8 9.2 %copy-start.36 = (bf16[2,96,1024]{2,1,0:T(8,128)(2,1)S(1)}, bf16[2,96,1024]{2,1,0:T(8,128)(2,1)}, u32[]{:S(2)}) copy-start(bf16[2,96,1024]{2,1,0:T(8,128)(2,1)} %copy-done.35) | copy-start | bytes 1179652
  125.9 26.4 %collective-permute-start.15 = (bf16[96,1792]{1,0:T(8,128)(2,1)}, bf16[96,1792]{1,0:T(8,128)(2,1)S(1)}, u32[]{:S(2)}, u32[]{:S(2)}) collective-permute-start(bf16[96,1792]{1,0:T(8,128)(2,1)} %shard_map.62.refs_1_), channel_id=1, source_target_pairs={{0,8},{4,12},{8,16},{12,20},{16,24},{20,28},{24,0},{28,4},{1,9},{5... | collective-permute-start | bytes 1032200 | tf_op jit(solution)/shard_map/ppermute | solution.py:202
  125.9 26.3 %collective-permute-start.17 = (bf16[96,1792]{1,0:T(8,128)(2,1)}, bf16[96,1792]{1,0:T(8,128)(2,1)S(1)}, u32[]{:S(2)}, u32[]{:S(2)}) collective-permute-start(bf16[96,1792]{1,0:T(8,128)(2,1)} %shard_map.64.refs_2_), channel_id=1, source_target_pairs={{0,24},{4,28},{8,0},{12,4},{16,8},{20,12},{24,16},{28,20},{1,25},{... | collective-permute-start | bytes 1032200 | tf_op jit(solution)/shard_map/ppermute | solution.py:202
  129.2 22.2 %collective-permute-start.18 = (bf16[2,96,1024]{2,1,0:T(8,128)(2,1)}, bf16[2,96,1024]{2,1,0:T(8,128)(2,1)S(1)}, u32[]{:S(2)}, u32[]{:S(2)}) collective-permute-start(bf16[2,96,1024]{2,1,0:T(8,128)(2,1)} %get-tuple-element.33), channel_id=1, source_target_pairs={{0,1},{1,2},{2,3},{3,0},{4,5},{5,6},{6,7},{7,4},{8,9},{9,10},{10,1... | collective-permute-start | bytes 1179656 | tf_op jit(solution)/shard_map/ppermute | solution.py:210
  130.8 20.6 %collective-permute-start.19 = (bf16[2,96,1024]{2,1,0:T(8,128)(2,1)}, bf16[2,96,1024]{2,1,0:T(8,128)(2,1)S(1)}, u32[]{:S(2)}, u32[]{:S(2)}) collective-permute-start(bf16[2,96,1024]{2,1,0:T(8,128)(2,1)} %get-tuple-element.34), channel_id=1, source_target_pairs={{0,2},{1,3},{2,0},{3,1},{4,6},{5,7},{6,4},{7,5},{8,10},{9,11},{10,... | collective-permute-start | bytes 1179656 | tf_op jit(solution)/shard_map/ppermute | solution.py:210
  133.6 17.8 %collective-permute-start.20 = (bf16[2,96,1024]{2,1,0:T(8,128)(2,1)}, bf16[2,96,1024]{2,1,0:T(8,128)(2,1)S(1)}, u32[]{:S(2)}, u32[]{:S(2)}) collective-permute-start(bf16[2,96,1024]{2,1,0:T(8,128)(2,1)} %get-tuple-element.35), channel_id=1, source_target_pairs={{0,3},{1,0},{2,1},{3,2},{4,7},{5,4},{6,5},{7,6},{8,11},{9,8},{10,9... | collective-permute-start | bytes 1179656 | tf_op jit(solution)/shard_map/ppermute | solution.py:210
  154.3 16.7 %collective-permute-start.22 = (bf16[2,2,96,1024]{3,2,1,0:T(8,128)(2,1)}, bf16[2,2,96,1024]{3,2,1,0:T(8,128)(2,1)}, u32[]{:S(2)}, u32[]{:S(2)}) collective-permute-start(bf16[2,2,96,1024]{3,2,1,0:T(8,128)(2,1)} %get-tuple-element.41), channel_id=1, source_target_pairs={{0,32},{32,0},{64,96},{96,64},{1,33},{33,1},{65,97},{97,65},{2,34}... | collective-permute-start | bytes 2359304 | tf_op jit(solution)/shard_map/ppermute | solution.py:214
  154.4 16.6 %collective-permute-start.23 = (bf16[2,2,96,1024]{3,2,1,0:T(8,128)(2,1)}, bf16[2,2,96,1024]{3,2,1,0:T(8,128)(2,1)}, u32[]{:S(2)}, u32[]{:S(2)}) collective-permute-start(bf16[2,2,96,1024]{3,2,1,0:T(8,128)(2,1)} %get-tuple-element.42), channel_id=1, source_target_pairs={{0,32},{32,0},{64,96},{96,64},{1,33},{33,1},{65,97},{97,65},{2,34}... | collective-permute-start | bytes 2359304 | tf_op jit(solution)/shard_map/ppermute | solution.py:214
  154.9 37.3 %collective-permute-start.27 = (bf16[96,1024]{1,0:T(8,128)(2,1)}, bf16[96,1024]{1,0:T(8,128)(2,1)}, u32[]{:S(2)}, u32[]{:S(2)}) collective-permute-start(bf16[96,1024]{1,0:T(8,128)(2,1)} %get-tuple-element.47), channel_id=1, source_target_pairs={{0,64},{32,96},{64,0},{96,32},{1,65},{33,97},{65,1},{97,33},{2,66}... | collective-permute-start | bytes 589832 | tf_op jit(solution)/shard_map/ppermute | solution.py:218
  154.9 2.8 %copy-start.3 = (bf16[3072,1024]{1,0:T(8,128)(2,1)S(1)}, bf16[3072,1024]{1,0:T(8,128)(2,1)}, u32[]{:S(2)}) copy-start(bf16[3072,1024]{1,0:T(8,128)(2,1)} %all-gather.5.cloned.1.call-done.refs_18_) | copy-start | bytes 18874372
  166.1 12.8 %copy-start.4 = (bf16[3072,1024]{1,0:T(8,128)(2,1)S(1)}, bf16[3072,1024]{1,0:T(8,128)(2,1)}, u32[]{:S(2)}) copy-start(bf16[3072,1024]{1,0:T(8,128)(2,1)} %all-gather.5.cloned.1.call-done.refs_18_) | copy-start | bytes 18874372
  166.1 12.8 %copy-start.13 = (bf16[192,1792]{1,0:T(8,128)(2,1)S(1)}, bf16[192,1792]{1,0:T(8,128)(2,1)}, u32[]{:S(2)}) copy-start(bf16[192,1792]{1,0:T(8,128)(2,1)} %copy-done.10) | copy-start | bytes 2064388
  166.1 12.8 %copy-start.29 = (bf16[192,1792]{1,0:T(8,128)(2,1)S(1)}, bf16[192,1792]{1,0:T(8,128)(2,1)}, u32[]{:S(2)}) copy-start(bf16[192,1792]{1,0:T(8,128)(2,1)} %copy-done.26) | copy-start | bytes 2064388
  175.6 16.5 %copy-start.52 = (bf16[2,96,1024]{2,1,0:T(8,128)(2,1)}, bf16[2,96,1024]{2,1,0:T(8,128)(2,1)S(1)}, u32[]{:S(2)}) copy-start(bf16[2,96,1024]{2,1,0:T(8,128)(2,1)S(1)} %get-tuple-element.43.refs_19_.refs_0_) | copy-start | bytes 1179652
  175.6 21.1 %collective-permute-start.24 = (bf16[2,96,1024]{2,1,0:T(8,128)(2,1)}, bf16[2,96,1024]{2,1,0:T(8,128)(2,1)}, u32[]{:S(2)}, u32[]{:S(2)}) collective-permute-start(bf16[2,96,1024]{2,1,0:T(8,128)(2,1)} %get-tuple-element.44), channel_id=1, source_target_pairs={{0,1},{1,2},{2,3},{3,0},{4,5},{5,6},{6,7},{7,4},{8,9},{9,10},{10,1... | collective-permute-start | bytes 1179656 | tf_op jit(solution)/shard_map/ppermute | solution.py:210
  176.2 20.5 %collective-permute-start.25 = (bf16[2,96,1024]{2,1,0:T(8,128)(2,1)}, bf16[2,96,1024]{2,1,0:T(8,128)(2,1)}, u32[]{:S(2)}, u32[]{:S(2)}) collective-permute-start(bf16[2,96,1024]{2,1,0:T(8,128)(2,1)} %get-tuple-element.45), channel_id=1, source_target_pairs={{0,2},{1,3},{2,0},{3,1},{4,6},{5,7},{6,4},{7,5},{8,10},{9,11},{10,... | collective-permute-start | bytes 1179656 | tf_op jit(solution)/shard_map/ppermute | solution.py:210
  177.0 20.3 %collective-permute-start.26 = (bf16[2,96,1024]{2,1,0:T(8,128)(2,1)}, bf16[2,96,1024]{2,1,0:T(8,128)(2,1)}, u32[]{:S(2)}, u32[]{:S(2)}) collective-permute-start(bf16[2,96,1024]{2,1,0:T(8,128)(2,1)} %get-tuple-element.46), channel_id=1, source_target_pairs={{0,3},{1,0},{2,1},{3,2},{4,7},{5,4},{6,5},{7,6},{8,11},{9,8},{10,9... | collective-permute-start | bytes 1179656 | tf_op jit(solution)/shard_map/ppermute | solution.py:210
  192.2 11.9 %copy-start.14 = (bf16[192,1792]{1,0:T(8,128)(2,1)S(1)}, bf16[192,1792]{1,0:T(8,128)(2,1)}, u32[]{:S(2)}) copy-start(bf16[192,1792]{1,0:T(8,128)(2,1)} %copy-done.10) | copy-start | bytes 2064388
  192.2 11.9 %copy-start.22 = (bf16[192,1792]{1,0:T(8,128)(2,1)S(1)}, bf16[192,1792]{1,0:T(8,128)(2,1)}, u32[]{:S(2)}) copy-start(bf16[192,1792]{1,0:T(8,128)(2,1)} %copy-done.19) | copy-start | bytes 2064388
  192.2 11.9 %copy-start.25 = (bf16[192,1792]{1,0:T(8,128)(2,1)S(1)}, bf16[192,1792]{1,0:T(8,128)(2,1)}, u32[]{:S(2)}) copy-start(bf16[192,1792]{1,0:T(8,128)(2,1)} %shard_map.50.refs_0_) | copy-start | bytes 2064388
  200.7 16.9 %copy-start.50 = (bf16[96,1024]{1,0:T(8,128)(2,1)}, bf16[96,1024]{1,0:T(8,128)(2,1)S(1)}, u32[]{:S(2)}) copy-start(bf16[96,1024]{1,0:T(8,128)(2,1)S(1)} %get-tuple-element.48.refs_19_.near) | copy-start | bytes 589828
  200.7 16.9 %collective-permute-start.28 = (bf16[96,1024]{1,0:T(8,128)(2,1)S(1)}, bf16[96,1024]{1,0:T(8,128)(2,1)}, u32[]{:S(2)}, u32[]{:S(2)}) collective-permute-start(bf16[96,1024]{1,0:T(8,128)(2,1)S(1)} %get-tuple-element.49), channel_id=1, source_target_pairs={{0,64},{32,96},{64,0},{96,32},{1,65},{33,97},{65,1},{97,33},{2,66}... | collective-permute-start | bytes 589832 | tf_op jit(solution)/shard_map/ppermute | solution.py:218
  204.1 2.8 %copy-start.5 = (bf16[3072,1024]{1,0:T(8,128)(2,1)S(1)}, bf16[3072,1024]{1,0:T(8,128)(2,1)}, u32[]{:S(2)}) copy-start(bf16[3072,1024]{1,0:T(8,128)(2,1)} %all-gather.5.cloned.1.call-done.refs_18_) | copy-start | bytes 18874372
  (41 other events, 54.3 us)
Sparse Core Ops, SparseCore 0:
  44.1 38.1 all-gather.2
  126.0 16.5 all-gather.4

commit v4 on v3

v4 whole, which is shorter than its diff:
```python
import functools

import jax
import jax.numpy as jnp
from jax import lax
from jax.experimental import pallas as pl
from jax.experimental.pallas import tpu as pltpu
from jax.sharding import PartitionSpec as P

BLOCK = 192
PARTS = ((0, BLOCK),)
MIB = 1024 * 1024
ANY = pl.BlockSpec(memory_space=pltpu.HBM)

PIECES = (
    ((0, 0, 0), (0, 0, 1)),
    ((3, 0, 0), (3, 0, 1)),
    ((1, 0, 0), (1, 0, 1)),
    ((0, 1, 0), (0, 1, 1)),
    ((2, 0, 0), (3, 1, 0)),
    ((2, 0, 1), (1, 1, 0)),
    ((1, 1, 1), (3, 1, 1)),
    ((2, 1, 0),),
    ((2, 1, 1),),
)


def source_of(shift, flip):
    col = lax.axis_index("col")
    x = lax.rem(col // 2 + shift, 4)
    z = lax.rem(col + flip, 2)
    return x, z


def grad_input_kernel(n, wanted, split, *refs):
    count = len(wanted)
    chunks, w_hbm = refs[:count], refs[count]
    keep, sends = refs[-7 - split], refs[-6 - split:-6]
    w, g, o, w_sem, g_sem, o_sem = refs[-6:]
    row, y = lax.axis_index("row"), lax.axis_index("depth")
    w_copy = pltpu.make_async_copy(w_hbm, w, w_sem)
    w_copy.start()
    copies, at, places = [], 0, []
    for ref, index in zip(chunks, wanted):
        rows = n * len(PIECES[index])
        copy = pltpu.make_async_copy(ref, g.at[pl.ds(at, rows)], g_sem.at[len(copies)])
        copy.start()
        copies.append((copy, at + rows))
        places += [(at + n * i, p) for i, p in enumerate(PIECES[index])]
        at += rows
    w_copy.wait()
    waited, done, outs = 0, 0, []
    group = 4
    for first in range(0, len(places), group):
        inside = places[first:first + group]
        low, high = inside[0][0], inside[-1][0] + n
        while waited < len(copies) and (waited == 0 or copies[waited - 1][1] < high):
            copies[waited][0].wait()
            waited += 1
        o[low:high, :] = jnp.dot(g[low:high, :], w[...], preferred_element_type=jnp.float32).astype(jnp.bfloat16)
        for start, (shift, flip, q) in inside:
            x, z = source_of(shift, flip)
            apart = lax.rem(x + row, 2)
            far = lax.rem(x // 2 + row // 2, 2)
            ahead = lax.rem(2 * z + q + 4 - y, 4)
            each = 4 // split
            targets = [(apart == 0, keep.at[ahead, far])]
            for k, ref in enumerate(sends):
                targets.append(((apart == 1) & (ahead // each == k), ref.at[lax.rem(ahead, each), far]))
            for here, ref in targets:
                copy = pltpu.make_async_copy(o.at[pl.ds(start, n)], ref, o_sem.at[done])
                outs.append((here, copy))
                pl.when(here)(copy.start)
            done += 1
    for here, copy in outs:
        pl.when(here)(copy.wait)


def grad_input_part(n, wanted, split, chunks, weight, into=(), after=()):
    ff, d = weight.shape
    rows = n * sum(len(PIECES[index]) for index in wanted)
    shapes = [jax.ShapeDtypeStruct((count, 2, n, d), jnp.bfloat16) for count in [4] + [4 // split] * split]
    args = [chunks[index] for index in wanted] + [weight, *after, *into]
    return pl.pallas_call(
        functools.partial(grad_input_kernel, n, wanted, split),
        out_shape=shapes,
        in_specs=[ANY] * len(args),
        out_specs=[ANY] * len(shapes),
        scratch_shapes=[
            pltpu.VMEM((ff, d), jnp.bfloat16),
            pltpu.VMEM((rows, ff), jnp.bfloat16),
            pltpu.VMEM((rows, d), jnp.bfloat16),
            pltpu.SemaphoreType.DMA,
            pltpu.SemaphoreType.DMA((len(wanted),)),
            pltpu.SemaphoreType.DMA((rows // n,)),
        ],
        input_output_aliases={len(args) - len(into) + i: i for i in range(len(into))},
        compiler_params=pltpu.CompilerParams(vmem_limit_bytes=60 * MIB),
        cost_estimate=pl.CostEstimate(
            flops=2 * rows * ff * d , bytes_accessed=rows * ff , transcendentals=0
        ),
    )(*args)


TILE = 256


def grad_weight_kernel(first, last, *refs):
    count = len(PIECES) * len(PARTS)
    chunks, acts_hbm, out = refs[:count], refs[count], refs[-7]
    acts, g, o, a_sem, g_sem, o_sem = refs[-6:]
    acts_copy = pltpu.make_async_copy(acts_hbm, acts, a_sem)
    acts_copy.start()
    copies = []
    for tile in range(first, last):
        at, of_tile = tile - first, []
        for part, (low, n) in enumerate(PARTS):
            for ref, pieces in zip(chunks[part * len(PIECES):], PIECES):
                for i, (shift, flip, q) in enumerate(pieces):
                    x, z = source_of(shift, flip)
                    block = 4 * x + 2 * z + q
                    of_tile.append(
                        pltpu.make_async_copy(
                            ref.at[pl.ds(n * i, n), pl.ds(TILE * tile, TILE)],
                            g.at[at, pl.ds(pl.multiple_of(block * BLOCK + low, 16), n), :],
                            g_sem.at[at * 16 * len(PARTS) + len(of_tile)],
                        )
                    )
                    of_tile[-1].start()
        copies.append(of_tile)
    acts_copy.wait()
    outs = []
    for tile in range(first, last):
        at = tile - first
        for copy in copies[at]:
            copy.wait()
        o[at] = lax.dot_general(
            g[at], acts[...], (((0,), (0,)), ((), ())), preferred_element_type=jnp.float32
        ).astype(jnp.bfloat16)
        outs.append(pltpu.make_async_copy(o.at[at], out.at[pl.ds(TILE * tile, TILE), :], o_sem.at[at]))
        outs[-1].start()
    for copy in outs:
        copy.wait()


def grad_weight_tiles(first, last, chunks, acts, into=None, after=()):
    ff, (tokens, d) = chunks[0].shape[-1], acts.shape
    tiles = last - first
    args = [*chunks, acts, *after] + ([] if into is None else [into])
    return pl.pallas_call(
        functools.partial(grad_weight_kernel, first, last),
        out_shape=jax.ShapeDtypeStruct((ff, d), jnp.bfloat16),
        in_specs=[ANY] * len(args),
        out_specs=ANY,
        scratch_shapes=[
            pltpu.VMEM((tokens, d), jnp.bfloat16),
            pltpu.VMEM((tiles, tokens, TILE), jnp.bfloat16),
            pltpu.VMEM((tiles, TILE, d), jnp.bfloat16),
            pltpu.SemaphoreType.DMA,
            pltpu.SemaphoreType.DMA((tiles * 16 * len(PARTS),)),
            pltpu.SemaphoreType.DMA((tiles,)),
        ],
        input_output_aliases={} if into is None else {len(args) - 1: 0},
        compiler_params=pltpu.CompilerParams(vmem_limit_bytes=60 * MIB),
        cost_estimate=pl.CostEstimate(
            flops=2 * tokens * TILE * tiles * d,
            bytes_accessed=2 * (tokens * TILE * tiles + tokens * d + TILE * tiles * d),
            transcendentals=0,
        ),
    )(*args)


def along_x(value, shift):
    return lax.ppermute(value, "col", [(i, (i + 2 * shift) % 8) for i in range(8)])


def along_z(value):
    return lax.ppermute(value, "col", [(i, i ^ 1) for i in range(8)])


def along_y(value, shift):
    return lax.ppermute(value, "depth", [(i, (i + shift) % 4) for i in range(4)])


def other_core(value):
    return lax.ppermute(value, "row", [(i, i ^ 1) for i in range(4)])


def other_z_hi(value):
    return lax.ppermute(value, "row", [(i, i ^ 2) for i in range(4)])


def first_step(own):
    return along_x(own, 1), along_x(own, -1), along_z(own)


def second_sends(left, right, z):
    n = left.shape[0] // 2
    return (
        jnp.concatenate([left[:n], z[:n]]),
        jnp.concatenate([right[n:], z[:n]]),
        jnp.concatenate([right[n:], left[n:]]),
    )


def second_step(left, right, z):
    return along_x(left, 1), along_x(right, -1), along_z(z)


def rows_kernel(start, *refs):
    out, sem = refs[-2:]
    copy = pltpu.make_async_copy(refs[0].at[pl.ds(start, out.shape[0])], out, sem)
    copy.start()
    copy.wait()


def rows_of(value, start, count, after):
    return pl.pallas_call(
        functools.partial(rows_kernel, start),
        out_shape=jax.ShapeDtypeStruct((count, value.shape[1]), value.dtype),
        in_specs=[ANY] * (1 + len(after)),
        out_specs=pl.BlockSpec(memory_space=pltpu.VMEM),
        scratch_shapes=[pltpu.SemaphoreType.DMA],
        compiler_params=pltpu.CompilerParams(vmem_limit_bytes=60 * MIB),
    )(value, *after)


def third_sends(left2, z2, after):
    n = left2.shape[0] // 2
    return rows_of(left2, n, n, after), rows_of(z2, 0, n, after)


def third_step(left, right):
    return along_x(left, 1), along_x(right, -1)


HALF = BLOCK // 2


def wide(value):
    return value.astype(jnp.float32)


def cores_kernel(keep, got, *refs):
    own_y, *to_y, own_z, to_z = refs[-6:]
    for i in range(4):
        for far in range(2):
            total = (wide(keep[i, far]) + wide(got[i, far])).astype(jnp.bfloat16)
            (to_y[i - 1] if i else own_y)[far] = total[:HALF]
            (to_z if far else own_z)[i] = total[HALF:]


def first_sums_kernel(own_y, got1, got2, got3, own_z, got_z, *refs):
    near, to_far, at0, at1, at2, at3 = refs[-6:]
    for far, out in enumerate((near, to_far)):
        out[...] = (
            wide(own_y[far]) + wide(got1[far]) + wide(got2[far]) + wide(got3[far])
        ).astype(jnp.bfloat16)
    for i, out in enumerate((at0, at1, at2, at3)):
        out[...] = (wide(own_z[i]) + wide(got_z[i])).astype(jnp.bfloat16)


def last_sums_kernel(near, got_far, at0, got1, got2, got3, *refs):
    out = refs[-1]
    out[:HALF, :] = (wide(near[...]) + wide(got_far[...])).astype(jnp.bfloat16)
    out[HALF:, :] = (wide(at0[...]) + wide(got1[...]) + wide(got2[...]) + wide(got3[...])).astype(jnp.bfloat16)


def in_vmem(kernel, inputs, shapes, after=()):
    vmem = pl.BlockSpec(memory_space=pltpu.VMEM)
    return pl.pallas_call(
        kernel,
        out_shape=[jax.ShapeDtypeStruct(shape, jnp.bfloat16) for shape in shapes],
        in_specs=[vmem] * len(inputs) + [ANY] * len(after),
        out_specs=[vmem] * len(shapes),
        compiler_params=pltpu.CompilerParams(vmem_limit_bytes=60 * MIB),
    )(*inputs, *after)


def shards(activations, grad_output, weight):
    tiles, d = grad_output.shape[1] // TILE, weight.shape[1]
    acts = lax.all_gather(activations, ("row", "depth"), axis=0, tiled=True)

    first = first_step(grad_output)
    sends = second_sends(*first)
    second = second_step(*sends)
    chunks = [grad_output, *first]
    part = grad_input_part(BLOCK, (0, 1, 2, 3), 1, chunks, weight, after=sends)
    sends = third_sends(second[0], second[2], (part[0],))
    third = third_step(*sends)
    chunks += [*second, *third]
    part = grad_input_part(BLOCK, (4, 5, 6), 1, chunks, weight, into=part, after=sends)
    keep, send = grad_input_part(BLOCK, (7, 8), 1, chunks, weight, into=part)

    got = other_core(send)
    weight_grad = grad_weight_tiles(0, 2, chunks, acts, after=(keep,))
    halves = [(2, HALF, d)] * 4 + [(4, HALF, d)] * 2
    own_y, *to_y, own_z, to_z = in_vmem(cores_kernel, (keep, got), halves, after=(weight_grad,))
    got_y = [along_y(to_y[i - 1], i) for i in (1, 2, 3)]
    got_z = other_z_hi(to_z)
    weight_grad = grad_weight_tiles(2, 5, chunks, acts, into=weight_grad, after=(own_y,))
    near, to_far, *at = in_vmem(
        first_sums_kernel, (own_y, *got_y, own_z, got_z), [(HALF, d)] * 6, after=(weight_grad,)
    )
    got_far = other_z_hi(to_far)
    got_y = [along_y(at[i], i) for i in (1, 2, 3)]
    weight_grad = grad_weight_tiles(5, tiles, chunks, acts, into=weight_grad, after=(near,))
    (result,) = in_vmem(
        last_sums_kernel, (near, got_far, at[0], *got_y), [(BLOCK, d)], after=(weight_grad,)
    )
    return result, weight_grad


def solution(mesh):
    in_specs = (P(("row", "depth"), "col"), P("col", ("row", "depth")), P(("row", "depth"), "col"))
    out_specs = (P(("row", "depth"), "col"), P(("row", "depth"), "col"))
    return jax.shard_map(shards, mesh=mesh, in_specs=in_specs, out_specs=out_specs, check_vma=False)
```

time: 228 us -> 193 us (0.85)
  local copies, waits for them, and re-layouts: 43.9 us -> 8.94 us
  waiting for transfers between devices: 46.8 us -> 73.1 us
  Pallas kernels: 82.3 us -> 66.6 us
  starting transfers between devices: 38.6 us -> 27.3 us
    unnamed x116 -> x32, local copies, waits for them, and re-layouts: 43.9 us -> 8.76 us
    ppermute x12 -> x6, waiting for transfers between devices: 18.7 us -> 50.6 us  [along_x(): lax.ppermute(value, 'col', [(i, (i + 2 * shift) % 8) for i in range(8)])]
    pallas_call x20 -> x5, Pallas kernels: 35.8 us -> 13.9 us  [the longest x3 9.99 us: in_vmem(): pl.pallas_call(kernel, out_shape=[jax.ShapeDtypeStruct(shape, jnp.bfloat1...]
    ppermute x3 -> x2, waiting for transfers between devices: 21.8 us -> 0.01 us  [other_z_hi(): return lax.ppermute(value, 'row', [(i, i ^ 2) for i in range(4)])]
    ppermute x4 -> x2, waiting for transfers between devices: 3.03 us -> 16.6 us  [along_z(): return lax.ppermute(value, 'col', [(i, i ^ 1) for i in range(8)])]
    ppermute x12 -> x6, starting transfers between devices: 17.5 us -> 8.98 us  [along_x(): lax.ppermute(value, 'col', [(i, (i + 2 * shift) % 8) for i in range(8)])]
    pallas_call x3, Pallas kernels: 22.8 us -> 28.6 us  [grad_weight_tiles(): pl.pallas_call(functools.partial(grad_weight_kernel, first, last), out_sh...]
    ppermute x3 -> x2, starting transfers between devices: 6.91 us -> 3.51 us  [other_z_hi(): return lax.ppermute(value, 'row', [(i, i ^ 2) for i in range(4)])]
  transfers between devices with their start and end apart: 31 -> 18, of which waited for: 9 -> 6; matrix products, arithmetic and copies ran while one was open for 0% -> 1% of each run, Pallas kernels for 33% -> 29%
where the time goes in v4:
time: 193 us; the launch traced here: 192 us
  waiting for transfers between devices  73.1 us (38%)
  Pallas kernels  66.6 us (35%)
  starting transfers between devices  27.3 us (14%)
  between operations  14.3 us (7%)
  local copies, waits for them, and re-layouts  8.94 us (5%)
  other arithmetic  2.16 us (1%)
    ppermute x6, waiting for transfers between devices, along_x(): lax.ppermute(value, 'col', [(i, (i + 2 * shift) % 8) for i in range(8)])  50.6 us
    pallas_call x3, Pallas kernels, grad_weight_tiles(): pl.pallas_call(functools.partial(grad_weight_kernel, first, last), out_sh...  28.6 us
    pallas_call x3, Pallas kernels, grad_input_part(): pl.pallas_call(functools.partial(grad_input_kernel, n, wanted, split), ou...  24 us
    ppermute x2, waiting for transfers between devices, along_z(): return lax.ppermute(value, 'col', [(i, i ^ 1) for i in range(8)])  16.6 us
    ppermute x6, starting transfers between devices, along_y(): lax.ppermute(value, 'depth', [(i, (i + shift) % 4) for i in range(4)])  10.9 us
    pallas_call x3, Pallas kernels, in_vmem(): pl.pallas_call(kernel, out_shape=[jax.ShapeDtypeStruct(shape, jnp.bfloat1...  9.99 us
    ppermute x6, starting transfers between devices, along_x(): lax.ppermute(value, 'col', [(i, (i + 2 * shift) % 8) for i in range(8)])  8.98 us
    unnamed x32, local copies, waits for them, and re-layouts  8.76 us
  transfers between devices with their start and end apart: 18, of which 6 were waited for; matrix products, arithmetic and copies ran while one was open for 1% of the time, Pallas kernels for 29%

profile of v4, /device:TPU:0, one launch (start us, length us, event | category | flops | bytes accessed | tf_op | source)
XLA Modules:
  0.0 192.4 jit_solution(2822359037901445426)
XLA Ops:
  7.2 0.7 all-gather.2.cloned.1.call-update
  7.9 2.9 %collective-permute-start.3 = (bf16[384,1792]{1,0:T(8,128)(2,1)}, bf16[384,1792]{1,0:T(8,128)(2,1)S(1)}, u32[]{:S(2)}, u32[]{:S(2)}) collective-permute-start(bf16[384,1792]{1,0:T(8,128)(2,1)} %refs_0_.7), channel_id=1, source_target_pairs={{0,24},{4,28},{8,0},{12,4},{16,8},{20,12},{24,16},{28,20},{1,25},{... | collective-permute-start | bytes 4128776 | tf_op jit(solution)/shard_map/ppermute | solution.py:174
  10.8 1.9 collective-permute-start.1
  12.7 27.8 %collective-permute-done.3.refs_2_ = bf16[384,1792]{1,0:T(8,128)(2,1)S(1)} collective-permute-done((bf16[384,1792]{1,0:T(8,128)(2,1)}, bf16[384,1792]{1,0:T(8,128)(2,1)S(1)}, u32[]{:S(2)}, u32[]{:S(2)}) %collective-permute-start.3) | collective-permute-done | bytes 1376288 | tf_op jit(solution)/shard_map/ppermute | solution.py:174
  40.6 6.5 %collective-permute-done.1.refs_3_ = bf16[384,1792]{1,0:T(8,128)(2,1)S(1)} collective-permute-done((bf16[384,1792]{1,0:T(8,128)(2,1)}, bf16[384,1792]{1,0:T(8,128)(2,1)S(1)}, u32[]{:S(2)}, u32[]{:S(2)}) %collective-permute-start.1) | collective-permute-done | bytes 1376288 | tf_op jit(solution)/shard_map/ppermute | solution.py:178
  47.1 1.0 copy-done.4
  48.2 1.1 copy-done.2
  49.2 0.1 fusion
  49.3 2.2 %pad_maximum_fusion.2 = (bf16[384,1792]{1,0:T(8,128)(2,1)}, bf16[384,1792]{1,0:T(8,128)(2,1)}, bf16[384,1792]{1,0:T(8,128)(2,1)}) fusion(bf16[192,1792]{1,0:T(8,128)(2,1)S(1)} %slice.20, bf16[192,1792]{1,0:T(8,128)(2,1)S(1)} %get-tuple-element.38, bf16[192,1792]{1,0:T(8,128)(2,1)S(1)} %slice.19, bf16[192,1792]{1,0:T(8,128)(2,1)S(1)} %get-tuple-element.39), kind=kLoop, calls=%fused_computation.2 | loop fusion | flops 6881280 | bytes 6881280 | tf_op jit(solution)/shard_map/concatenate | solution.py:202
  51.5 1.7 collective-permute-start.5
  53.2 3.2 %collective-permute-start.7 = (bf16[384,1792]{1,0:T(8,128)(2,1)}, bf16[384,1792]{1,0:T(8,128)(2,1)}, u32[]{:S(2)}, u32[]{:S(2)}) collective-permute-start(bf16[384,1792]{1,0:T(8,128)(2,1)} %get-tuple-element.41.refs_6_), channel_id=1, source_target_pairs={{0,24},{4,28},{8,0},{12,4},{16,8},{20,12},{24,16},{28,20},{1,25},{... | collective-permute-start | bytes 4128776 | tf_op jit(solution)/shard_map/ppermute | solution.py:174
  56.4 10.6 %shard_map.50 = (bf16[4,2,192,1024]{3,2,1,0:T(8,128)(2,1)}, bf16[4,2,192,1024]{3,2,1,0:T(8,128)(2,1)}) custom-call(bf16[384,1792]{1,0:T(8,128)(2,1)} %refs_0_.7, bf16[384,1792]{1,0:T(8,128)(2,1)} %copy-done.2, bf16[384,1792]{1,0:T(8,128)(2,1)} %copy-done.3, bf16[384,1792]{1,0:T(8,128)(2,1)} %copy-done.4, bf16[1792,1024]{1,0:T(8,128)(2,1)} %refs_2_.1, ...), custom_call_target="tpu_custom_call" | custom-call | flops 5637144576 | bytes 2752512 | tf_op jit(solution)/shard_map/pallas_call | solution.py:84
  67.1 16.8 %collective-permute-done.2.refs_0_.refs_4_ = bf16[384,1792]{1,0:T(8,128)(2,1)S(1)} collective-permute-done((bf16[384,1792]{1,0:T(8,128)(2,1)}, bf16[384,1792]{1,0:T(8,128)(2,1)S(1)}, u32[]{:S(2)}, u32[]{:S(2)}) %collective-permute-start.2) | collective-permute-done | bytes 1376288 | tf_op jit(solution)/shard_map/ppermute | solution.py:174
  83.9 1.1 copy-done
  85.0 2.0 %shard_map.51.refs_4_ = bf16[192,1792]{1,0:T(8,128)(2,1)} custom-call(bf16[384,1792]{1,0:T(8,128)(2,1)} %copy-done, bf16[4,2,192,1024]{3,2,1,0:T(8,128)(2,1)} %get-tuple-element.20.refs_1_.refs_6_), custom_call_target="tpu_custom_call" | custom-call | tf_op jit(solution)/shard_map/pallas_call | solution.py:218
  86.9 0.1 collective-permute-start.4
  87.0 10.2 %collective-permute-done.5.refs_0_.refs_2_.refs_6_ = bf16[384,1792]{1,0:T(8,128)(2,1)S(1)} collective-permute-done((bf16[384,1792]{1,0:T(8,128)(2,1)}, bf16[384,1792]{1,0:T(8,128)(2,1)S(1)}, u32[]{:S(2)}, u32[]{:S(2)}) %collective-permute-start.5) | collective-permute-done | bytes 1376288 | tf_op jit(solution)/shard_map/ppermute | solution.py:178
  97.2 1.1 copy-done.1
  98.3 2.0 %shard_map.52.refs_5_ = bf16[192,1792]{1,0:T(8,128)(2,1)} custom-call(bf16[384,1792]{1,0:T(8,128)(2,1)} %copy-done.1, bf16[4,2,192,1024]{3,2,1,0:T(8,128)(2,1)} %get-tuple-element.20.refs_1_.refs_6_), custom_call_target="tpu_custom_call" | custom-call | tf_op jit(solution)/shard_map/pallas_call | solution.py:218
  100.2 2.8 %collective-permute-start.6 = (bf16[192,1792]{1,0:T(8,128)(2,1)}, bf16[192,1792]{1,0:T(8,128)(2,1)S(1)}, u32[]{:S(2)}, u32[]{:S(2)}) collective-permute-start(bf16[192,1792]{1,0:T(8,128)(2,1)} %shard_map.52.refs_5_), channel_id=1, source_target_pairs={{0,24},{4,28},{8,0},{12,4},{16,8},{20,12},{24,16},{28,20},{1,25},{... | collective-permute-start | bytes 2064392 | tf_op jit(solution)/shard_map/ppermute | solution.py:174
  103.0 8.5 %shard_map.53 = (bf16[4,2,192,1024]{3,2,1,0:T(8,128)(2,1)}, bf16[4,2,192,1024]{3,2,1,0:T(8,128)(2,1)}) custom-call(bf16[384,1792]{1,0:T(8,128)(2,1)} %copy-done, bf16[384,1792]{1,0:T(8,128)(2,1)} %collective-permute-done.7.refs_1_.refs_5_, bf16[384,1792]{1,0:T(8,128)(2,1)} %copy-done.1, ...), custom_call_target="tpu_custom_call", output_to_operand_aliasing={{0}: (6, {}), {1}: (7, {})} | custom-call | flops 4227858432 | bytes 2064384 | tf_op jit(solution)/shard_map/pallas_call | solution.py:84
  111.5 6.0 %collective-permute-done.6.refs_1_.refs_8_ = bf16[192,1792]{1,0:T(8,128)(2,1)S(1)} collective-permute-done((bf16[192,1792]{1,0:T(8,128)(2,1)}, bf16[192,1792]{1,0:T(8,128)(2,1)S(1)}, u32[]{:S(2)}, u32[]{:S(2)}) %collective-permute-start.6) | collective-permute-done | bytes 688160 | tf_op jit(solution)/shard_map/ppermute | solution.py:174
  117.5 0.8 copy-done.6
  118.3 4.9 %shard_map.54 = (bf16[4,2,192,1024]{3,2,1,0:T(8,128)(2,1)}, bf16[4,2,192,1024]{3,2,1,0:T(8,128)(2,1)}) custom-call(bf16[192,1792]{1,0:T(8,128)(2,1)} %copy-done.5, bf16[192,1792]{1,0:T(8,128)(2,1)} %copy-done.6, bf16[1792,1024]{1,0:T(8,128)(2,1)} %refs_2_.1, ...), custom_call_target="tpu_custom_call", output_to_operand_aliasing={{0}: (3, {}), {1}: (4, {})} | custom-call | flops 1409286144 | bytes 688128 | tf_op jit(solution)/shard_map/pallas_call | solution.py:84
  123.3 0.3 collective-permute-start.8
  123.6 8.8 %shard_map.55.refs_0_.refs_11_ = bf16[1792,1024]{1,0:T(8,128)(2,1)} custom-call(bf16[384,1792]{1,0:T(8,128)(2,1)} %refs_0_.7, bf16[384,1792]{1,0:T(8,128)(2,1)} %copy-done.2, bf16[384,1792]{1,0:T(8,128)(2,1)} %copy-done.3, bf16[384,1792]{1,0:T(8,128)(2,1)} %copy-done.4, bf16[384,1792]{1,0:T(8,128)(2,1)} %copy-done, ...), custom_call_target="tpu_custom_call" | custom-call | flops 3221225472 | bytes 10485760 | tf_op jit(solution)/shard_map/pallas_call | solution.py:150
  132.4 1.7 copy-done.7
  134.1 4.7 %shard_map.56 = (bf16[2,96,1024]{2,1,0:T(8,128)(2,1)}, bf16[2,96,1024]{2,1,0:T(8,128)(2,1)}, bf16[2,96,1024]{2,1,0:T(8,128)(2,1)}, bf16[2,96,1024]{2,1,0:T(8,128...) custom-call(bf16[4,2,192,1024]{3,2,1,0:T(8,128)(2,1)} %get-tuple-element.24.refs_10_.keep, ...), custom_call_target="tpu_custom_call" | custom-call | tf_op jit(solution)/shard_map/pallas_call | solution.py:271
  138.8 2.8 %collective-permute-start.12 = (bf16[4,96,1024]{2,1,0:T(8,128)(2,1)}, bf16[4,96,1024]{2,1,0:T(8,128)(2,1)S(1)}, u32[]{:S(2)}, u32[]{:S(2)}) collective-permute-start(bf16[4,96,1024]{2,1,0:T(8,128)(2,1)} %get-tuple-element.31), channel_id=1, source_target_pairs={{0,64},{32,96},{64,0},{96,32},{1,65},{33,97},{65,1},{97,33},{2,66}... | collective-permute-start | bytes 2359304 | tf_op jit(solution)/shard_map/ppermute | solution.py:190
  141.6 1.5 collective-permute-start.9
  143.1 2.7 %collective-permute-start.10 = (bf16[2,96,1024]{2,1,0:T(8,128)(2,1)}, bf16[2,96,1024]{2,1,0:T(8,128)(2,1)S(1)}, u32[]{:S(2)}, u32[]{:S(2)}) collective-permute-start(bf16[2,96,1024]{2,1,0:T(8,128)(2,1)} %get-tuple-element.28), channel_id=1, source_target_pairs={{0,2},{1,3},{2,0},{3,1},{4,6},{5,7},{6,4},{7,5},{8,10},{9,11},{10,... | collective-permute-start | bytes 1179656 | tf_op jit(solution)/shard_map/ppermute | solution.py:182
  145.8 1.4 collective-permute-start.11
  147.2 11.2 %shard_map.57.refs_0_.refs_11_ = bf16[1792,1024]{1,0:T(8,128)(2,1)} custom-call(bf16[384,1792]{1,0:T(8,128)(2,1)} %refs_0_.7, bf16[384,1792]{1,0:T(8,128)(2,1)} %copy-done.2, bf16[384,1792]{1,0:T(8,128)(2,1)} %copy-done.3, bf16[384,1792]{1,0:T(8,128)(2,1)} %copy-done.4, bf16[384,1792]{1,0:T(8,128)(2,1)} %copy-done, ...), custom_call_target="tpu_custom_call", output_to_operand_aliasing={{}: (11, {})} | custom-call | flops 4831838208 | bytes 12582912 | tf_op jit(solution)/shard_map/pallas_call | solution.py:150
  158.5 5.1 %collective-permute-done.10.got2 = bf16[2,96,1024]{2,1,0:T(8,128)(2,1)S(1)} collective-permute-done((bf16[2,96,1024]{2,1,0:T(8,128)(2,1)}, bf16[2,96,1024]{2,1,0:T(8,128)(2,1)S(1)}, u32[]{:S(2)}, u32[]{:S(2)}) %collective-permute-start.10) | collective-permute-done | bytes 393248 | tf_op jit(solution)/shard_map/ppermute | solution.py:182
  163.6 0.8 copy-done.10
  164.4 0.2 copy-done.11
  164.6 0.2 copy-done.8
  164.8 3.0 %shard_map.58 = (bf16[96,1024]{1,0:T(8,128)(2,1)}, bf16[96,1024]{1,0:T(8,128)(2,1)}, bf16[96,1024]{1,0:T(8,128)(2,1)}, bf16[96,1024]{1,0:T(8,128)(2,1)}, bf16[96...) custom-call(bf16[2,96,1024]{2,1,0:T(8,128)(2,1)} %get-tuple-element.26.refs_10_.own_y, bf16[2,96,1024]{2,1,0:T(8,128)(2,1)} %copy-done.9, ...), custom_call_target="tpu_custom_call" | custom-call | tf_op jit(solution)/shard_map/pallas_call | solution.py:271
  167.8 0.7 collective-permute-start.13
  168.5 1.2 collective-permute-start.14
  169.7 2.4 %collective-permute-start.15 = (bf16[96,1024]{1,0:T(8,128)(2,1)}, bf16[96,1024]{1,0:T(8,128)(2,1)S(1)}, u32[]{:S(2)}, u32[]{:S(2)}) collective-permute-start(bf16[96,1024]{1,0:T(8,128)(2,1)} %get-tuple-element.36), channel_id=1, source_target_pairs={{0,2},{1,3},{2,0},{3,1},{4,6},{5,7},{6,4},{7,5},{8,10},{9,11},{10,... | collective-permute-start | bytes 589832 | tf_op jit(solution)/shard_map/ppermute | solution.py:182
  172.1 1.6 collective-permute-start.16
  173.7 8.7 %shard_map.59.refs_0_ = bf16[1792,1024]{1,0:T(8,128)(2,1)} custom-call(bf16[384,1792]{1,0:T(8,128)(2,1)} %refs_0_.7, bf16[384,1792]{1,0:T(8,128)(2,1)} %copy-done.2, bf16[384,1792]{1,0:T(8,128)(2,1)} %copy-done.3, bf16[384,1792]{1,0:T(8,128)(2,1)} %copy-done.4, bf16[384,1792]{1,0:T(8,128)(2,1)} %copy-done, ...), custom_call_target="tpu_custom_call", output_to_operand_aliasing={{}: (11, {})} | custom-call | flops 3221225472 | bytes 10485760 | tf_op jit(solution)/shard_map/pallas_call | solution.py:150
  182.5 0.6 copy-done.12
  183.1 0.1 copy-done.13
  183.1 0.1 copy-done.14
  183.2 0.1 copy-done.15
  183.3 2.2 %shard_map.60 = bf16[192,1024]{1,0:T(8,128)(2,1)} custom-call(bf16[96,1024]{1,0:T(8,128)(2,1)} %get-tuple-element.32.refs_10_.near, bf16[96,1024]{1,0:T(8,128)(2,1)} %copy-done.12, bf16[96,1024]{1,0:T(8,128)(2,1)} %get-tuple-element.34.at0, bf16[96,1024]{1,0:T(8,128)(2,1)} %copy-done.13, bf16[96,1024]{1,0:T(8,128)(2,1)} %copy-done.14, ...), custom_call_target="tpu_custom_call" | custom-call | tf_op jit(solution)/shard_map/pallas_call | solution.py:271
  (36 shorter events, 0.2 us)
Async XLA Ops:
  7.2 116.4 %all-gather.2.cloned.1.call-start = ((), (), s32[]{:S(2)}) async-start(), calls=%async_computation | async-start | bytes 6684672 | tf_op jit(solution)/shard_map/all_gather | solution.py:282
  7.9 32.7 %collective-permute-start.3 = (bf16[384,1792]{1,0:T(8,128)(2,1)}, bf16[384,1792]{1,0:T(8,128)(2,1)S(1)}, u32[]{:S(2)}, u32[]{:S(2)}) collective-permute-start(bf16[384,1792]{1,0:T(8,128)(2,1)} %refs_0_.7), channel_id=1, source_target_pairs={{0,24},{4,28},{8,0},{12,4},{16,8},{20,12},{24,16},{28,20},{1,25},{... | collective-permute-start | bytes 4128776 | tf_op jit(solution)/shard_map/ppermute | solution.py:174
  10.8 36.3 %collective-permute-start.1 = (bf16[384,1792]{1,0:T(8,128)(2,1)}, bf16[384,1792]{1,0:T(8,128)(2,1)S(1)}, u32[]{:S(2)}, u32[]{:S(2)}) collective-permute-start(bf16[384,1792]{1,0:T(8,128)(2,1)} %refs_0_.7), channel_id=1, source_target_pairs={{0,4},{4,0},{8,12},{12,8},{16,20},{20,16},{24,28},{28,24},{1,5},{5... | collective-permute-start | bytes 4128776 | tf_op jit(solution)/shard_map/ppermute | solution.py:178
  12.7 35.4 %collective-permute-start = (bf16[384,1792]{1,0:T(8,128)(2,1)}, bf16[384,1792]{1,0:T(8,128)(2,1)S(1)}, u32[]{:S(2)}, u32[]{:S(2)}) collective-permute-start(bf16[384,1792]{1,0:T(8,128)(2,1)} %refs_0_.7), channel_id=1, source_target_pairs={{0,8},{4,12},{8,16},{12,20},{16,24},{20,28},{24,0},{28,4},{1,9},{5... | collective-permute-start | bytes 4128776 | tf_op jit(solution)/shard_map/ppermute | solution.py:174
  40.6 6.5 %copy-start.3 = (bf16[384,1792]{1,0:T(8,128)(2,1)}, bf16[384,1792]{1,0:T(8,128)(2,1)S(1)}, u32[]{:S(2)}) copy-start(bf16[384,1792]{1,0:T(8,128)(2,1)S(1)} %collective-permute-done.3.refs_2_) | copy-start | bytes 4128772
  47.1 1.1 copy-start.4
  48.2 1.1 copy-start.2
  51.5 32.4 %collective-permute-start.2 = (bf16[384,1792]{1,0:T(8,128)(2,1)}, bf16[384,1792]{1,0:T(8,128)(2,1)S(1)}, u32[]{:S(2)}, u32[]{:S(2)}) collective-permute-start(bf16[384,1792]{1,0:T(8,128)(2,1)} %get-tuple-element.42.refs_5_), channel_id=1, source_target_pairs={{0,8},{4,12},{8,16},{12,20},{16,24},{20,28},{24,0},{28,4},{1,9},{5... | collective-permute-start | bytes 4128776 | tf_op jit(solution)/shard_map/ppermute | solution.py:174
  51.5 45.7 %collective-permute-start.5 = (bf16[384,1792]{1,0:T(8,128)(2,1)}, bf16[384,1792]{1,0:T(8,128)(2,1)S(1)}, u32[]{:S(2)}, u32[]{:S(2)}) collective-permute-start(bf16[384,1792]{1,0:T(8,128)(2,1)} %get-tuple-element.40.refs_7_), channel_id=1, source_target_pairs={{0,4},{4,0},{8,12},{12,8},{16,20},{20,16},{24,28},{28,24},{1,5},{5... | collective-permute-start | bytes 4128776 | tf_op jit(solution)/shard_map/ppermute | solution.py:178
  53.2 49.8 %collective-permute-start.7 = (bf16[384,1792]{1,0:T(8,128)(2,1)}, bf16[384,1792]{1,0:T(8,128)(2,1)}, u32[]{:S(2)}, u32[]{:S(2)}) collective-permute-start(bf16[384,1792]{1,0:T(8,128)(2,1)} %get-tuple-element.41.refs_6_), channel_id=1, source_target_pairs={{0,24},{4,28},{8,0},{12,4},{16,8},{20,12},{24,16},{28,20},{1,25},{... | collective-permute-start | bytes 4128776 | tf_op jit(solution)/shard_map/ppermute | solution.py:174
  83.9 1.1 copy-start
  86.9 24.5 %collective-permute-start.4 = (bf16[192,1792]{1,0:T(8,128)(2,1)}, bf16[192,1792]{1,0:T(8,128)(2,1)S(1)}, u32[]{:S(2)}, u32[]{:S(2)}) collective-permute-start(bf16[192,1792]{1,0:T(8,128)(2,1)} %shard_map.51.refs_4_), channel_id=1, source_target_pairs={{0,8},{4,12},{8,16},{12,20},{16,24},{20,28},{24,0},{28,4},{1,9},{5... | collective-permute-start | bytes 2064392 | tf_op jit(solution)/shard_map/ppermute | solution.py:174
  97.2 1.1 copy-start.1
  100.2 17.3 %collective-permute-start.6 = (bf16[192,1792]{1,0:T(8,128)(2,1)}, bf16[192,1792]{1,0:T(8,128)(2,1)S(1)}, u32[]{:S(2)}, u32[]{:S(2)}) collective-permute-start(bf16[192,1792]{1,0:T(8,128)(2,1)} %shard_map.52.refs_5_), channel_id=1, source_target_pairs={{0,24},{4,28},{8,0},{12,4},{16,8},{20,12},{24,16},{28,20},{1,25},{... | collective-permute-start | bytes 2064392 | tf_op jit(solution)/shard_map/ppermute | solution.py:174
  111.5 6.0 %copy-start.5 = (bf16[192,1792]{1,0:T(8,128)(2,1)}, bf16[192,1792]{1,0:T(8,128)(2,1)S(1)}, u32[]{:S(2)}) copy-start(bf16[192,1792]{1,0:T(8,128)(2,1)S(1)} %collective-permute-done.4.refs_0_.refs_7_) | copy-start | bytes 2064388
  117.5 0.8 copy-start.6
  123.3 9.1 %collective-permute-start.8 = (bf16[4,2,192,1024]{3,2,1,0:T(8,128)(2,1)}, bf16[4,2,192,1024]{3,2,1,0:T(8,128)(2,1)S(1)}, u32[]{:S(2)}, u32[]{:S(2)}) collective-permute-start(bf16[4,2,192,1024]{3,2,1,0:T(8,128)(2,1)} %get-tuple-element.25), channel_id=1, source_target_pairs={{0,32},{32,0},{64,96},{96,64},{1,33},{33,1},{65,97},{97,65},{2,34}... | collective-permute-start | bytes 9437192 | tf_op jit(solution)/shard_map/ppermute | solution.py:186
  132.3 1.7 copy-start.7
  138.8 24.8 %collective-permute-start.12 = (bf16[4,96,1024]{2,1,0:T(8,128)(2,1)}, bf16[4,96,1024]{2,1,0:T(8,128)(2,1)S(1)}, u32[]{:S(2)}, u32[]{:S(2)}) collective-permute-start(bf16[4,96,1024]{2,1,0:T(8,128)(2,1)} %get-tuple-element.31), channel_id=1, source_target_pairs={{0,64},{32,96},{64,0},{96,32},{1,65},{33,97},{65,1},{97,33},{2,66}... | collective-permute-start | bytes 2359304 | tf_op jit(solution)/shard_map/ppermute | solution.py:190
  141.6 16.9 %collective-permute-start.9 = (bf16[2,96,1024]{2,1,0:T(8,128)(2,1)}, bf16[2,96,1024]{2,1,0:T(8,128)(2,1)S(1)}, u32[]{:S(2)}, u32[]{:S(2)}) collective-permute-start(bf16[2,96,1024]{2,1,0:T(8,128)(2,1)} %get-tuple-element.27), channel_id=1, source_target_pairs={{0,1},{1,2},{2,3},{3,0},{4,5},{5,6},{6,7},{7,4},{8,9},{9,10},{10,1... | collective-permute-start | bytes 1179656 | tf_op jit(solution)/shard_map/ppermute | solution.py:182
  143.1 20.5 %collective-permute-start.10 = (bf16[2,96,1024]{2,1,0:T(8,128)(2,1)}, bf16[2,96,1024]{2,1,0:T(8,128)(2,1)S(1)}, u32[]{:S(2)}, u32[]{:S(2)}) collective-permute-start(bf16[2,96,1024]{2,1,0:T(8,128)(2,1)} %get-tuple-element.28), channel_id=1, source_target_pairs={{0,2},{1,3},{2,0},{3,1},{4,6},{5,7},{6,4},{7,5},{8,10},{9,11},{10,... | collective-permute-start | bytes 1179656 | tf_op jit(solution)/shard_map/ppermute | solution.py:182
  145.8 17.8 %collective-permute-start.11 = (bf16[2,96,1024]{2,1,0:T(8,128)(2,1)}, bf16[2,96,1024]{2,1,0:T(8,128)(2,1)S(1)}, u32[]{:S(2)}, u32[]{:S(2)}) collective-permute-start(bf16[2,96,1024]{2,1,0:T(8,128)(2,1)} %get-tuple-element.29), channel_id=1, source_target_pairs={{0,3},{1,0},{2,1},{3,2},{4,7},{5,4},{6,5},{7,6},{8,11},{9,8},{10,9... | collective-permute-start | bytes 1179656 | tf_op jit(solution)/shard_map/ppermute | solution.py:182
  158.5 5.2 %copy-start.9 = (bf16[2,96,1024]{2,1,0:T(8,128)(2,1)}, bf16[2,96,1024]{2,1,0:T(8,128)(2,1)S(1)}, u32[]{:S(2)}) copy-start(bf16[2,96,1024]{2,1,0:T(8,128)(2,1)S(1)} %collective-permute-done.9.got1) | copy-start | bytes 1179652
  163.6 0.8 copy-start.10
  163.6 1.0 copy-start.11
  163.6 1.1 copy-start.8
  167.8 14.6 %collective-permute-start.13 = (bf16[96,1024]{1,0:T(8,128)(2,1)}, bf16[96,1024]{1,0:T(8,128)(2,1)S(1)}, u32[]{:S(2)}, u32[]{:S(2)}) collective-permute-start(bf16[96,1024]{1,0:T(8,128)(2,1)} %get-tuple-element.33), channel_id=1, source_target_pairs={{0,64},{32,96},{64,0},{96,32},{1,65},{33,97},{65,1},{97,33},{2,66}... | collective-permute-start | bytes 589832 | tf_op jit(solution)/shard_map/ppermute | solution.py:190
  168.5 13.9 %collective-permute-start.14 = (bf16[96,1024]{1,0:T(8,128)(2,1)}, bf16[96,1024]{1,0:T(8,128)(2,1)S(1)}, u32[]{:S(2)}, u32[]{:S(2)}) collective-permute-start(bf16[96,1024]{1,0:T(8,128)(2,1)} %get-tuple-element.35), channel_id=1, source_target_pairs={{0,1},{1,2},{2,3},{3,0},{4,5},{5,6},{6,7},{7,4},{8,9},{9,10},{10,1... | collective-permute-start | bytes 589832 | tf_op jit(solution)/shard_map/ppermute | solution.py:182
  169.7 12.7 %collective-permute-start.15 = (bf16[96,1024]{1,0:T(8,128)(2,1)}, bf16[96,1024]{1,0:T(8,128)(2,1)S(1)}, u32[]{:S(2)}, u32[]{:S(2)}) collective-permute-start(bf16[96,1024]{1,0:T(8,128)(2,1)} %get-tuple-element.36), channel_id=1, source_target_pairs={{0,2},{1,3},{2,0},{3,1},{4,6},{5,7},{6,4},{7,5},{8,10},{9,11},{10,... | collective-permute-start | bytes 589832 | tf_op jit(solution)/shard_map/ppermute | solution.py:182
  172.1 10.4 %collective-permute-start.16 = (bf16[96,1024]{1,0:T(8,128)(2,1)}, bf16[96,1024]{1,0:T(8,128)(2,1)S(1)}, u32[]{:S(2)}, u32[]{:S(2)}) collective-permute-start(bf16[96,1024]{1,0:T(8,128)(2,1)} %get-tuple-element.37), channel_id=1, source_target_pairs={{0,3},{1,0},{2,1},{3,2},{4,7},{5,4},{6,5},{7,6},{8,11},{9,8},{10,9... | collective-permute-start | bytes 589832 | tf_op jit(solution)/shard_map/ppermute | solution.py:182
  182.4 0.7 copy-start.12
  182.4 0.7 copy-start.13
  182.4 0.8 copy-start.14
  182.5 0.8 copy-start.15
Sparse Core Ops, SparseCore 0:
  10.4 81.6 all-gather.1
